TPU v7x, 256 devices: a whole 4x4x8 slice. The times are simulated.
256 devices in a mesh: ctx: 32 (over x, z_hi, core), exp: 8 (over y, z_lo).
Axes of the slice: x: 4, y: 4, z: 8 (z_hi: 4, z_lo: 2; z = z_hi * 2 + z_lo), core: 2. Of those that a mesh axis runs over, the one named last changes fastest.
Arguments:
- tokens: bfloat16 [4096, 2880], P('ctx'), may hold values from -6 to 6
- positions: int32 [4096], P('ctx'), may hold values from 0 to 4095, as said below
- norm_attn: float32 [2880], replicated, may hold values from 0.5 to 1.5
- norm_moe: float32 [2880], replicated, may hold values from 0.5 to 1.5
- w_query: bfloat16 [2880, 4096], P(None, 'exp')
- key_matrix: bfloat16 [2880, 512], P(None, 'exp'), may hold values from -0.109375 to 0.109375
- value_matrix: bfloat16 [2880, 512], P(None, 'exp'), may hold values from -0.109375 to 0.109375
- w_out: bfloat16 [4096, 2880], P('exp'), may hold values from -0.09375 to 0.09375
- sinks: float32 [64], P('exp'), may hold values from 6 to 13
- expert_ids: int32 [4096, 4], P('ctx'), may hold values from 0 to 31, all different within a row; in each aligned block of 128 rows (0 to 127, 128 to 255, ...) at most 24 rows name the same one
- expert_weights: float32 [4096, 4], P('ctx'), may hold values from 0.1 to 0.6
- w_gate: bfloat16 [32, 2880, 1440], P('ctx', None, 'exp'), may hold values from -0.109375 to 0.109375
- w_up: bfloat16 [32, 2880, 1440], P('ctx', None, 'exp'), may hold values from -0.109375 to 0.109375
- w_down: bfloat16 [32, 1440, 2880], P('ctx', 'exp'), may hold values from -0.15625 to 0.15625
Outputs:
- attended: bfloat16 [4096, 2880], P(('ctx', 'exp'))
- layer_out: bfloat16 [4096, 2880], P(('ctx', 'exp'))
Inputs may be any that keep to these rules, and one draw needn't show every extreme that they name: `positions`: a permutation of 0 to 4095; each aligned run of 128 rows holds 128 consecutive positions in increasing order. `expert_ids`: the 4 experts of a row differ; in each aligned block of 128 rows no expert is named by more than 24 rows, a bound that some block reaches.
All inputs are finite; a program needn't handle non-finite values.
Results may differ from a plain program's by a relative error of at most 0.02.
The roundings to bfloat16 on the way count: a program that leaves them out, or rounds other values in their place, can miss the bound.
Values may be sent and summed in bfloat16 or wider, within the bound.
No kernel may reach another device: no remote copies, remote signals or barrier semaphores. Data moves between devices by JAX's collectives and lax.ppermute only.
A program may use at most 128 MiB of HBM per device.

v0:
```python
import jax
import jax.numpy as jnp
from jax import lax
from jax.sharding import PartitionSpec as P

HEAD_WIDTH = 64


EPSILON = 1e-05


def shifted(block, axis, distance):
    devices = range(lax.axis_size(axis))
    route = [((i - distance) % len(devices), i) for i in devices]
    return lax.ppermute(block, axis, route)


def rms_norm(values, gain_vector):
    mean_square = jnp.mean(values * values, axis=-1, keepdims=True)
    return values * lax.rsqrt(mean_square + EPSILON) * gain_vector


def local(
    tokens,
    positions,
    norm_attn,
    norm_moe,
    w_query,
    key_matrix,
    value_matrix,
    w_out,
    sinks,
    expert_ids,
    expert_weights,
    w_gate,
    w_up,
    w_down,
):
    ctx_count = lax.axis_size("ctx")
    exp_count = lax.axis_size("exp")
    rows_all = tokens.shape[0]
    width = tokens.shape[1]
    local_heads = sinks.shape[0]
    kv_heads = key_matrix.shape[1] // HEAD_WIDTH
    group_width = local_heads // kv_heads
    key_width = kv_heads * HEAD_WIDTH
    score_scale = HEAD_WIDTH ** (-0.5)
    hidden_in = tokens.astype(jnp.float32)
    normed = rms_norm(hidden_in, norm_attn).astype(jnp.bfloat16)
    query_rows = jnp.dot(normed, w_query, preferred_element_type=jnp.float32).astype(jnp.bfloat16)
    query_rows = query_rows.reshape(rows_all, kv_heads, group_width, HEAD_WIDTH)
    key_projected = jnp.dot(normed, key_matrix, preferred_element_type=jnp.float32).astype(
        jnp.bfloat16
    )
    value_projected = jnp.dot(normed, value_matrix, preferred_element_type=jnp.float32).astype(
        jnp.bfloat16
    )
    kv_block = jnp.concatenate([key_projected, value_projected], axis=1)
    all_positions = lax.all_gather(positions, "ctx", axis=0, tiled=True)
    start_top = jnp.broadcast_to(
        sinks.reshape(kv_heads, group_width, 1), (kv_heads, group_width, rows_all)
    )
    start_den = jnp.ones((kv_heads, group_width, rows_all), jnp.float32)
    start_acc = jnp.zeros((kv_heads, group_width, rows_all, HEAD_WIDTH), jnp.float32)

    def absorb(carry_state, block_rows, block_pos):
        top_old, denominator, accumulated = carry_state
        key_rows = block_rows.shape[0]
        key_part = block_rows[:, :key_width].reshape(key_rows, kv_heads, HEAD_WIDTH)
        value_part = block_rows[:, key_width:].reshape(key_rows, kv_heads, HEAD_WIDTH)
        scores = (
            jnp.einsum("qhgd,khd->hgqk", query_rows, key_part, preferred_element_type=jnp.float32)
            * score_scale
        )
        visible = block_pos[None, :] <= positions[:, None]
        scores = jnp.where(visible[None, None], scores, -1e30)
        top_new = jnp.maximum(top_old, jnp.max(scores, axis=-1))
        rescale = jnp.exp(top_old - top_new)
        weights = jnp.exp(scores - top_new[..., None])
        denominator = denominator * rescale + jnp.sum(weights, axis=-1)
        mixed = jnp.einsum(
            "hgqk,khd->hgqd",
            weights.astype(jnp.bfloat16),
            value_part,
            preferred_element_type=jnp.float32,
        )
        accumulated = accumulated * rescale[..., None] + mixed
        return (top_new, denominator, accumulated)

    first_state = absorb((start_top, start_den, start_acc), kv_block, positions)
    ctx_index = lax.axis_index("ctx")

    def cycle_step(cycle_turn, loop_carry):
        carry_state, block_rows = loop_carry
        block_rows = shifted(block_rows, "ctx", 1)
        source_index = (ctx_index - cycle_turn - 1 + ctx_count) % ctx_count
        block_pos = lax.dynamic_slice_in_dim(all_positions, source_index * rows_all, rows_all, 0)
        return (absorb(carry_state, block_rows, block_pos), block_rows)

    final_state, _ = lax.fori_loop(0, ctx_count - 1, cycle_step, (first_state, kv_block))
    top_last, den_last, acc_last = final_state
    head_out = (acc_last / den_last[..., None]).astype(jnp.bfloat16)
    head_out = jnp.transpose(head_out, (2, 0, 1, 3)).reshape(rows_all, local_heads * HEAD_WIDTH)
    partial_value = jnp.dot(head_out, w_out, preferred_element_type=jnp.float32)
    member = lax.axis_index("exp")
    share_rows = rows_all // exp_count
    attended_all = lax.psum(partial_value.astype(jnp.bfloat16), "exp")
    residual_all = hidden_in + attended_all.astype(jnp.float32)
    moe_in = rms_norm(residual_all, norm_moe).astype(jnp.bfloat16)
    attended = lax.dynamic_slice_in_dim(attended_all, member * share_rows, share_rows, 0)
    residual = lax.dynamic_slice_in_dim(residual_all, member * share_rows, share_rows, 0)
    local_experts = w_gate.shape[0]
    experts_all = local_experts * ctx_count
    top_k = expert_ids.shape[1]
    slot_count = rows_all * top_k * 3 // (2 * experts_all)
    flat_ids = expert_ids.reshape(-1)
    chosen = (flat_ids[:, None] == jnp.arange(experts_all, dtype=jnp.int32)[None, :]).astype(
        jnp.int32
    )
    slot_rank = jnp.cumsum(chosen, axis=0) - 1
    slot_of = jnp.sum(chosen * slot_rank, axis=1)
    target = flat_ids * slot_count + slot_of
    all_cells = jnp.arange(experts_all * slot_count, dtype=jnp.int32)
    matches = target[None, :] == all_cells[:, None]
    filled = jnp.any(matches, axis=1)
    route_rows = jnp.arange(rows_all * top_k, dtype=jnp.int32) // top_k
    source = jnp.sum(jnp.where(matches, route_rows[None, :], 0), axis=1)
    outgoing = jnp.where(filled[:, None], moe_in[source], jnp.zeros((), jnp.bfloat16))
    outgoing = outgoing.reshape(ctx_count, local_experts, slot_count, width)
    arrived = lax.all_to_all(outgoing, "ctx", split_axis=0, concat_axis=0, tiled=True)
    gate_act = jnp.einsum("sjcd,jdf->sjcf", arrived, w_gate, preferred_element_type=jnp.float32)
    up_act = jnp.einsum("sjcd,jdf->sjcf", arrived, w_up, preferred_element_type=jnp.float32)
    activated = (gate_act * jax.nn.sigmoid(1.702 * gate_act) * (up_act + 1.0)).astype(jnp.bfloat16)
    expert_part = jnp.einsum(
        "sjcf,jfd->sjcd", activated, w_down, preferred_element_type=jnp.float32
    ).astype(jnp.bfloat16)
    returned = lax.all_to_all(expert_part, "ctx", split_axis=0, concat_axis=0, tiled=True).reshape(
        experts_all * slot_count, width
    )
    picked = returned[target].astype(jnp.float32).reshape(rows_all, top_k, width)
    combined = jnp.sum(picked * expert_weights[:, :, None], axis=1)
    expert_sum = lax.psum_scatter(
        combined.astype(jnp.bfloat16), "exp", scatter_dimension=0, tiled=True
    ).astype(jnp.float32)
    layer_out = (residual + expert_sum).astype(jnp.bfloat16)
    return (attended, layer_out)


def solution(mesh):
    in_specs = (
        P("ctx", None),
        P("ctx"),
        P(),
        P(),
        P(None, "exp"),
        P(None, "exp"),
        P(None, "exp"),
        P("exp", None),
        P("exp"),
        P("ctx", None),
        P("ctx", None),
        P("ctx", None, "exp"),
        P("ctx", None, "exp"),
        P("ctx", "exp", None),
    )
    out_specs = (P(("ctx", "exp"), None), P(("ctx", "exp"), None))
    return jax.shard_map(local, mesh=mesh, in_specs=in_specs, out_specs=out_specs, check_vma=False)
```

profile of v0, /device:TPU:1, one launch (start us, length us, event | category | flops | bytes accessed | tf_op | source)
XLA Modules:
  0.0 732.0 jit_solution(11495671486481691809)
XLA Ops:
  15.8 48.4 %all-gather = s32[32,1,128]{2,1,0:T(1,128)S(1)} all-gather(s32[1,1,128]{2,1,0:T(1,128)S(1)} %bitcast.183), channel_id=1, replica_groups=mesh['ctx'=32,'exp'=8] {'ctx'}, dimensions={0}, use_global_device_ids=true | all-gather | bytes 16896 | tf_op jit(solution)/shard_map/all_gather | solution.py:59
  64.2 251.5 %while.23 = (s32[]{:T(128)}, f32[1,8,128]{2,1,0:T(8,128)S(1)}, f32[1,8,128]{2,1,0:T(8,128)S(1)}, f32[1,8,128,64]{2,3,1,0:T(8,128)S(1)}, bf16[128,128]{0,1:T(8,12...) while((s32[]{:T(128)}, f32[1,8,128]{2,1,0:T(8,128)S(1)}, ...), condition=%wide.region_6.7_spmd, body=%wide.region_3.6_spmd.sunk | while | flops 34622480 | bytes 2558316 | solution.py:100
  83.1 7.3 %collective-permute-done = bf16[128,128]{0,1:T(8,128)(2,1)S(1)} collective-permute-done((bf16[128,128]{0,1:T(8,128)(2,1)S(1)}, bf16[128,128]{0,1:T(8,128)(2,1)S(1)}, u32[]{:S(2)}, u32[]{:S(2)}) %collective-permute-start) | collective-permute-done | bytes 32800 | tf_op jit(solution)/shard_map/while/body/eval_jaxpr/ppermute | solution.py:15
  91.4 7.3 %collective-permute-done = bf16[128,128]{0,1:T(8,128)(2,1)S(1)} collective-permute-done((bf16[128,128]{0,1:T(8,128)(2,1)S(1)}, bf16[128,128]{0,1:T(8,128)(2,1)S(1)}, u32[]{:S(2)}, u32[]{:S(2)}) %collective-permute-start) | collective-permute-done | bytes 32800 | tf_op jit(solution)/shard_map/while/body/eval_jaxpr/ppermute | solution.py:15
  99.7 7.3 %collective-permute-done = bf16[128,128]{0,1:T(8,128)(2,1)S(1)} collective-permute-done((bf16[128,128]{0,1:T(8,128)(2,1)S(1)}, bf16[128,128]{0,1:T(8,128)(2,1)S(1)}, u32[]{:S(2)}, u32[]{:S(2)}) %collective-permute-start) | collective-permute-done | bytes 32800 | tf_op jit(solution)/shard_map/while/body/eval_jaxpr/ppermute | solution.py:15
  108.1 7.3 %collective-permute-done = bf16[128,128]{0,1:T(8,128)(2,1)S(1)} collective-permute-done((bf16[128,128]{0,1:T(8,128)(2,1)S(1)}, bf16[128,128]{0,1:T(8,128)(2,1)S(1)}, u32[]{:S(2)}, u32[]{:S(2)}) %collective-permute-start) | collective-permute-done | bytes 32800 | tf_op jit(solution)/shard_map/while/body/eval_jaxpr/ppermute | solution.py:15
  116.4 7.3 %collective-permute-done = bf16[128,128]{0,1:T(8,128)(2,1)S(1)} collective-permute-done((bf16[128,128]{0,1:T(8,128)(2,1)S(1)}, bf16[128,128]{0,1:T(8,128)(2,1)S(1)}, u32[]{:S(2)}, u32[]{:S(2)}) %collective-permute-start) | collective-permute-done | bytes 32800 | tf_op jit(solution)/shard_map/while/body/eval_jaxpr/ppermute | solution.py:15
  124.7 7.3 %collective-permute-done = bf16[128,128]{0,1:T(8,128)(2,1)S(1)} collective-permute-done((bf16[128,128]{0,1:T(8,128)(2,1)S(1)}, bf16[128,128]{0,1:T(8,128)(2,1)S(1)}, u32[]{:S(2)}, u32[]{:S(2)}) %collective-permute-start) | collective-permute-done | bytes 32800 | tf_op jit(solution)/shard_map/while/body/eval_jaxpr/ppermute | solution.py:15
  133.0 7.3 %collective-permute-done = bf16[128,128]{0,1:T(8,128)(2,1)S(1)} collective-permute-done((bf16[128,128]{0,1:T(8,128)(2,1)S(1)}, bf16[128,128]{0,1:T(8,128)(2,1)S(1)}, u32[]{:S(2)}, u32[]{:S(2)}) %collective-permute-start) | collective-permute-done | bytes 32800 | tf_op jit(solution)/shard_map/while/body/eval_jaxpr/ppermute | solution.py:15
  141.3 7.3 %collective-permute-done = bf16[128,128]{0,1:T(8,128)(2,1)S(1)} collective-permute-done((bf16[128,128]{0,1:T(8,128)(2,1)S(1)}, bf16[128,128]{0,1:T(8,128)(2,1)S(1)}, u32[]{:S(2)}, u32[]{:S(2)}) %collective-permute-start) | collective-permute-done | bytes 32800 | tf_op jit(solution)/shard_map/while/body/eval_jaxpr/ppermute | solution.py:15
  149.7 7.3 %collective-permute-done = bf16[128,128]{0,1:T(8,128)(2,1)S(1)} collective-permute-done((bf16[128,128]{0,1:T(8,128)(2,1)S(1)}, bf16[128,128]{0,1:T(8,128)(2,1)S(1)}, u32[]{:S(2)}, u32[]{:S(2)}) %collective-permute-start) | collective-permute-done | bytes 32800 | tf_op jit(solution)/shard_map/while/body/eval_jaxpr/ppermute | solution.py:15
  158.0 7.3 %collective-permute-done = bf16[128,128]{0,1:T(8,128)(2,1)S(1)} collective-permute-done((bf16[128,128]{0,1:T(8,128)(2,1)S(1)}, bf16[128,128]{0,1:T(8,128)(2,1)S(1)}, u32[]{:S(2)}, u32[]{:S(2)}) %collective-permute-start) | collective-permute-done | bytes 32800 | tf_op jit(solution)/shard_map/while/body/eval_jaxpr/ppermute | solution.py:15
  166.3 7.3 %collective-permute-done = bf16[128,128]{0,1:T(8,128)(2,1)S(1)} collective-permute-done((bf16[128,128]{0,1:T(8,128)(2,1)S(1)}, bf16[128,128]{0,1:T(8,128)(2,1)S(1)}, u32[]{:S(2)}, u32[]{:S(2)}) %collective-permute-start) | collective-permute-done | bytes 32800 | tf_op jit(solution)/shard_map/while/body/eval_jaxpr/ppermute | solution.py:15
  174.6 7.3 %collective-permute-done = bf16[128,128]{0,1:T(8,128)(2,1)S(1)} collective-permute-done((bf16[128,128]{0,1:T(8,128)(2,1)S(1)}, bf16[128,128]{0,1:T(8,128)(2,1)S(1)}, u32[]{:S(2)}, u32[]{:S(2)}) %collective-permute-start) | collective-permute-done | bytes 32800 | tf_op jit(solution)/shard_map/while/body/eval_jaxpr/ppermute | solution.py:15
  182.9 7.3 %collective-permute-done = bf16[128,128]{0,1:T(8,128)(2,1)S(1)} collective-permute-done((bf16[128,128]{0,1:T(8,128)(2,1)S(1)}, bf16[128,128]{0,1:T(8,128)(2,1)S(1)}, u32[]{:S(2)}, u32[]{:S(2)}) %collective-permute-start) | collective-permute-done | bytes 32800 | tf_op jit(solution)/shard_map/while/body/eval_jaxpr/ppermute | solution.py:15
  191.3 7.3 %collective-permute-done = bf16[128,128]{0,1:T(8,128)(2,1)S(1)} collective-permute-done((bf16[128,128]{0,1:T(8,128)(2,1)S(1)}, bf16[128,128]{0,1:T(8,128)(2,1)S(1)}, u32[]{:S(2)}, u32[]{:S(2)}) %collective-permute-start) | collective-permute-done | bytes 32800 | tf_op jit(solution)/shard_map/while/body/eval_jaxpr/ppermute | solution.py:15
  320.2 75.6 %all-reduce.2.cloned.1.call-done = bf16[128,2880]{0,1:T(8,128)(2,1)} async-done(((bf16[128,2880]{0,1:T(8,128)(2,1)}), bf16[128,2880]{0,1:T(8,128)(2,1)}) %all-reduce.2.cloned.1.call-update) | async-done | bytes 737296 | tf_op jit(solution)/shard_map/psum | solution.py:107
  402.4 10.5 %gather_fusion = bf16[768,2880]{1,0:T(8,128)(2,1)} fusion(bf16[128,2880]{1,0:T(8,128)(2,1)} %copy.73, s32[1024]{0:T(1024)S(1)} %pad_clamp_fusion.1), kind=kCustom, calls=%fused_computation | custom fusion | bytes 8850432 | tf_op jit(solution)/shard_map/gather | solution.py:128
  415.7 117.8 %all_to_all.10 = bf16[32,1,24,2880]{3,2,1,0:T(8,128)(2,1)S(1)} all-to-all(bf16[32,1,24,2880]{3,2,1,0:T(8,128)(2,1)S(1)} %broadcast_select_fusion), channel_id=1, replica_groups=mesh['ctx'=32,'exp'=8] {'ctx'}, dimensions={0} | all-to-all | bytes 8847360 | tf_op jit(solution)/shard_map/all_to_all | solution.py:130
  537.9 10.2 %fusion.14 = bf16[32,1,24,2880]{3,2,1,0:T(8,128)(2,1)} fusion(bf16[1,180,2880]{2,1,0:T(8,128)(2,1)} %param.29, bf16[32,1,24,2880]{3,2,1,0:T(8,128)(2,1)} %copy-done.4, bf16[1,2880,180]{1,2,0:T(8,128)(2,1)} %param.28, f32[32,1,24,180]{3,2,0,1:T(8,128)} %fusion.19), kind=kOutput, calls=%fused_computation.27 | convolution fusion | flops 1595842560 | bytes 11473920 | tf_op jit(solution)/shard_map/sjcf,jfd->sjcd/dot_general | solution.py:134
  553.5 103.3 %all-to-all-done.1 = bf16[32,1,24,2880]{3,2,1,0:T(8,128)(2,1)} async-done(((bf16[32,1,24,2880]{3,2,1,0:T(8,128)(2,1)}), bf16[32,1,24,2880]{3,2,1,0:T(8,128)(2,1)}, u32[]{:S(2)}, u32[]{:S(2)}) %all-to-all-start.1) | async-done | bytes 4423712 | tf_op jit(solution)/shard_map/all_to_all | solution.py:137
  656.8 9.6 %gather_fusion.1 = bf16[512,2880]{1,0:T(8,128)(2,1)} fusion(bf16[768,2880]{1,0:T(8,128)(2,1)} %bitcast.49, s32[1024]{0:T(1024)S(1)} %pad_clamp_fusion), kind=kCustom, calls=%fused_computation.1 | custom fusion | bytes 5900288 | tf_op jit(solution)/shard_map/gather | solution.py:140
  672.9 7.9 %multiply_reduce_fusion = bf16[128,2880]{1,0:T(8,128)(2,1)} fusion(f32[128,4,2880]{2,1,0:T(4,128)} %reshape.479, f32[128,4]{1,0:T(8,128)S(1)} %copy.77), kind=kLoop, calls=%fused_computation.20 | loop fusion | flops 2580480 | bytes 6637568 | tf_op jit(solution)/shard_map/reduce_sum | solution.py:141
  689.7 28.4 %reduce-scatter.4.cloned.1.call-done = bf16[16,2880]{1,0:T(8,128)(2,1)} async-done(((bf16[128,2880]{1,0:T(8,128)(2,1)}), bf16[16,2880]{1,0:T(8,128)(2,1)}) %reduce-scatter.4.cloned.1.call-update) | async-done | bytes 92176
  (408 shorter events, 199.8 us)
Async XLA Ops:
  7.2 388.6 %all-reduce.2.cloned.1.call-start = ((), (), s32[]{:S(2)}) async-start(), calls=%async_computation.3 | async-start | bytes 1474560 | tf_op jit(solution)/shard_map/psum | solution.py:107
  66.1 7.7 %collective-permute-start = (bf16[128,128]{0,1:T(8,128)(2,1)S(1)}, bf16[128,128]{0,1:T(8,128)(2,1)S(1)}, u32[]{:S(2)}, u32[]{:S(2)}) collective-permute-start(bf16[128,128]{0,1:T(8,128)(2,1)S(1)} %get-tuple-element.426), channel_id=1, source_target_pairs={{248,0},{0,8},{8,16},{16,24},{24,32},{32,40},{40,48},{48,56},{56,6... | collective-permute-start | bytes 98312 | tf_op jit(solution)/shard_map/while/body/eval_jaxpr/ppermute | solution.py:15
  82.8 7.6 %collective-permute-start = (bf16[128,128]{0,1:T(8,128)(2,1)S(1)}, bf16[128,128]{0,1:T(8,128)(2,1)S(1)}, u32[]{:S(2)}, u32[]{:S(2)}) collective-permute-start(bf16[128,128]{0,1:T(8,128)(2,1)S(1)} %get-tuple-element.426), channel_id=1, source_target_pairs={{248,0},{0,8},{8,16},{16,24},{24,32},{32,40},{40,48},{48,56},{56,6... | collective-permute-start | bytes 98312 | tf_op jit(solution)/shard_map/while/body/eval_jaxpr/ppermute | solution.py:15
  91.1 7.6 %collective-permute-start = (bf16[128,128]{0,1:T(8,128)(2,1)S(1)}, bf16[128,128]{0,1:T(8,128)(2,1)S(1)}, u32[]{:S(2)}, u32[]{:S(2)}) collective-permute-start(bf16[128,128]{0,1:T(8,128)(2,1)S(1)} %get-tuple-element.426), channel_id=1, source_target_pairs={{248,0},{0,8},{8,16},{16,24},{24,32},{32,40},{40,48},{48,56},{56,6... | collective-permute-start | bytes 98312 | tf_op jit(solution)/shard_map/while/body/eval_jaxpr/ppermute | solution.py:15
  99.5 7.6 %collective-permute-start = (bf16[128,128]{0,1:T(8,128)(2,1)S(1)}, bf16[128,128]{0,1:T(8,128)(2,1)S(1)}, u32[]{:S(2)}, u32[]{:S(2)}) collective-permute-start(bf16[128,128]{0,1:T(8,128)(2,1)S(1)} %get-tuple-element.426), channel_id=1, source_target_pairs={{248,0},{0,8},{8,16},{16,24},{24,32},{32,40},{40,48},{48,56},{56,6... | collective-permute-start | bytes 98312 | tf_op jit(solution)/shard_map/while/body/eval_jaxpr/ppermute | solution.py:15
  107.8 7.6 %collective-permute-start = (bf16[128,128]{0,1:T(8,128)(2,1)S(1)}, bf16[128,128]{0,1:T(8,128)(2,1)S(1)}, u32[]{:S(2)}, u32[]{:S(2)}) collective-permute-start(bf16[128,128]{0,1:T(8,128)(2,1)S(1)} %get-tuple-element.426), channel_id=1, source_target_pairs={{248,0},{0,8},{8,16},{16,24},{24,32},{32,40},{40,48},{48,56},{56,6... | collective-permute-start | bytes 98312 | tf_op jit(solution)/shard_map/while/body/eval_jaxpr/ppermute | solution.py:15
  116.1 7.6 %collective-permute-start = (bf16[128,128]{0,1:T(8,128)(2,1)S(1)}, bf16[128,128]{0,1:T(8,128)(2,1)S(1)}, u32[]{:S(2)}, u32[]{:S(2)}) collective-permute-start(bf16[128,128]{0,1:T(8,128)(2,1)S(1)} %get-tuple-element.426), channel_id=1, source_target_pairs={{248,0},{0,8},{8,16},{16,24},{24,32},{32,40},{40,48},{48,56},{56,6... | collective-permute-start | bytes 98312 | tf_op jit(solution)/shard_map/while/body/eval_jaxpr/ppermute | solution.py:15
  124.4 7.6 %collective-permute-start = (bf16[128,128]{0,1:T(8,128)(2,1)S(1)}, bf16[128,128]{0,1:T(8,128)(2,1)S(1)}, u32[]{:S(2)}, u32[]{:S(2)}) collective-permute-start(bf16[128,128]{0,1:T(8,128)(2,1)S(1)} %get-tuple-element.426), channel_id=1, source_target_pairs={{248,0},{0,8},{8,16},{16,24},{24,32},{32,40},{40,48},{48,56},{56,6... | collective-permute-start | bytes 98312 | tf_op jit(solution)/shard_map/while/body/eval_jaxpr/ppermute | solution.py:15
  132.7 7.6 %collective-permute-start = (bf16[128,128]{0,1:T(8,128)(2,1)S(1)}, bf16[128,128]{0,1:T(8,128)(2,1)S(1)}, u32[]{:S(2)}, u32[]{:S(2)}) collective-permute-start(bf16[128,128]{0,1:T(8,128)(2,1)S(1)} %get-tuple-element.426), channel_id=1, source_target_pairs={{248,0},{0,8},{8,16},{16,24},{24,32},{32,40},{40,48},{48,56},{56,6... | collective-permute-start | bytes 98312 | tf_op jit(solution)/shard_map/while/body/eval_jaxpr/ppermute | solution.py:15
  141.1 7.6 %collective-permute-start = (bf16[128,128]{0,1:T(8,128)(2,1)S(1)}, bf16[128,128]{0,1:T(8,128)(2,1)S(1)}, u32[]{:S(2)}, u32[]{:S(2)}) collective-permute-start(bf16[128,128]{0,1:T(8,128)(2,1)S(1)} %get-tuple-element.426), channel_id=1, source_target_pairs={{248,0},{0,8},{8,16},{16,24},{24,32},{32,40},{40,48},{48,56},{56,6... | collective-permute-start | bytes 98312 | tf_op jit(solution)/shard_map/while/body/eval_jaxpr/ppermute | solution.py:15
  149.4 7.6 %collective-permute-start = (bf16[128,128]{0,1:T(8,128)(2,1)S(1)}, bf16[128,128]{0,1:T(8,128)(2,1)S(1)}, u32[]{:S(2)}, u32[]{:S(2)}) collective-permute-start(bf16[128,128]{0,1:T(8,128)(2,1)S(1)} %get-tuple-element.426), channel_id=1, source_target_pairs={{248,0},{0,8},{8,16},{16,24},{24,32},{32,40},{40,48},{48,56},{56,6... | collective-permute-start | bytes 98312 | tf_op jit(solution)/shard_map/while/body/eval_jaxpr/ppermute | solution.py:15
  157.7 7.6 %collective-permute-start = (bf16[128,128]{0,1:T(8,128)(2,1)S(1)}, bf16[128,128]{0,1:T(8,128)(2,1)S(1)}, u32[]{:S(2)}, u32[]{:S(2)}) collective-permute-start(bf16[128,128]{0,1:T(8,128)(2,1)S(1)} %get-tuple-element.426), channel_id=1, source_target_pairs={{248,0},{0,8},{8,16},{16,24},{24,32},{32,40},{40,48},{48,56},{56,6... | collective-permute-start | bytes 98312 | tf_op jit(solution)/shard_map/while/body/eval_jaxpr/ppermute | solution.py:15
  166.0 7.6 %collective-permute-start = (bf16[128,128]{0,1:T(8,128)(2,1)S(1)}, bf16[128,128]{0,1:T(8,128)(2,1)S(1)}, u32[]{:S(2)}, u32[]{:S(2)}) collective-permute-start(bf16[128,128]{0,1:T(8,128)(2,1)S(1)} %get-tuple-element.426), channel_id=1, source_target_pairs={{248,0},{0,8},{8,16},{16,24},{24,32},{32,40},{40,48},{48,56},{56,6... | collective-permute-start | bytes 98312 | tf_op jit(solution)/shard_map/while/body/eval_jaxpr/ppermute | solution.py:15
  174.3 7.6 %collective-permute-start = (bf16[128,128]{0,1:T(8,128)(2,1)S(1)}, bf16[128,128]{0,1:T(8,128)(2,1)S(1)}, u32[]{:S(2)}, u32[]{:S(2)}) collective-permute-start(bf16[128,128]{0,1:T(8,128)(2,1)S(1)} %get-tuple-element.426), channel_id=1, source_target_pairs={{248,0},{0,8},{8,16},{16,24},{24,32},{32,40},{40,48},{48,56},{56,6... | collective-permute-start | bytes 98312 | tf_op jit(solution)/shard_map/while/body/eval_jaxpr/ppermute | solution.py:15
  182.7 7.6 %collective-permute-start = (bf16[128,128]{0,1:T(8,128)(2,1)S(1)}, bf16[128,128]{0,1:T(8,128)(2,1)S(1)}, u32[]{:S(2)}, u32[]{:S(2)}) collective-permute-start(bf16[128,128]{0,1:T(8,128)(2,1)S(1)} %get-tuple-element.426), channel_id=1, source_target_pairs={{248,0},{0,8},{8,16},{16,24},{24,32},{32,40},{40,48},{48,56},{56,6... | collective-permute-start | bytes 98312 | tf_op jit(solution)/shard_map/while/body/eval_jaxpr/ppermute | solution.py:15
  191.0 7.6 %collective-permute-start = (bf16[128,128]{0,1:T(8,128)(2,1)S(1)}, bf16[128,128]{0,1:T(8,128)(2,1)S(1)}, u32[]{:S(2)}, u32[]{:S(2)}) collective-permute-start(bf16[128,128]{0,1:T(8,128)(2,1)S(1)} %get-tuple-element.426), channel_id=1, source_target_pairs={{248,0},{0,8},{8,16},{16,24},{24,32},{32,40},{40,48},{48,56},{56,6... | collective-permute-start | bytes 98312 | tf_op jit(solution)/shard_map/while/body/eval_jaxpr/ppermute | solution.py:15
  199.3 7.6 %collective-permute-start = (bf16[128,128]{0,1:T(8,128)(2,1)S(1)}, bf16[128,128]{0,1:T(8,128)(2,1)S(1)}, u32[]{:S(2)}, u32[]{:S(2)}) collective-permute-start(bf16[128,128]{0,1:T(8,128)(2,1)S(1)} %get-tuple-element.426), channel_id=1, source_target_pairs={{248,0},{0,8},{8,16},{16,24},{24,32},{32,40},{40,48},{48,56},{56,6... | collective-permute-start | bytes 98312 | tf_op jit(solution)/shard_map/while/body/eval_jaxpr/ppermute | solution.py:15
  207.6 7.6 %collective-permute-start = (bf16[128,128]{0,1:T(8,128)(2,1)S(1)}, bf16[128,128]{0,1:T(8,128)(2,1)S(1)}, u32[]{:S(2)}, u32[]{:S(2)}) collective-permute-start(bf16[128,128]{0,1:T(8,128)(2,1)S(1)} %get-tuple-element.426), channel_id=1, source_target_pairs={{248,0},{0,8},{8,16},{16,24},{24,32},{32,40},{40,48},{48,56},{56,6... | collective-permute-start | bytes 98312 | tf_op jit(solution)/shard_map/while/body/eval_jaxpr/ppermute | solution.py:15
  215.9 7.6 %collective-permute-start = (bf16[128,128]{0,1:T(8,128)(2,1)S(1)}, bf16[128,128]{0,1:T(8,128)(2,1)S(1)}, u32[]{:S(2)}, u32[]{:S(2)}) collective-permute-start(bf16[128,128]{0,1:T(8,128)(2,1)S(1)} %get-tuple-element.426), channel_id=1, source_target_pairs={{248,0},{0,8},{8,16},{16,24},{24,32},{32,40},{40,48},{48,56},{56,6... | collective-permute-start | bytes 98312 | tf_op jit(solution)/shard_map/while/body/eval_jaxpr/ppermute | solution.py:15
  224.3 7.6 %collective-permute-start = (bf16[128,128]{0,1:T(8,128)(2,1)S(1)}, bf16[128,128]{0,1:T(8,128)(2,1)S(1)}, u32[]{:S(2)}, u32[]{:S(2)}) collective-permute-start(bf16[128,128]{0,1:T(8,128)(2,1)S(1)} %get-tuple-element.426), channel_id=1, source_target_pairs={{248,0},{0,8},{8,16},{16,24},{24,32},{32,40},{40,48},{48,56},{56,6... | collective-permute-start | bytes 98312 | tf_op jit(solution)/shard_map/while/body/eval_jaxpr/ppermute | solution.py:15
  232.6 7.6 %collective-permute-start = (bf16[128,128]{0,1:T(8,128)(2,1)S(1)}, bf16[128,128]{0,1:T(8,128)(2,1)S(1)}, u32[]{:S(2)}, u32[]{:S(2)}) collective-permute-start(bf16[128,128]{0,1:T(8,128)(2,1)S(1)} %get-tuple-element.426), channel_id=1, source_target_pairs={{248,0},{0,8},{8,16},{16,24},{24,32},{32,40},{40,48},{48,56},{56,6... | collective-permute-start | bytes 98312 | tf_op jit(solution)/shard_map/while/body/eval_jaxpr/ppermute | solution.py:15
  240.9 7.6 %collective-permute-start = (bf16[128,128]{0,1:T(8,128)(2,1)S(1)}, bf16[128,128]{0,1:T(8,128)(2,1)S(1)}, u32[]{:S(2)}, u32[]{:S(2)}) collective-permute-start(bf16[128,128]{0,1:T(8,128)(2,1)S(1)} %get-tuple-element.426), channel_id=1, source_target_pairs={{248,0},{0,8},{8,16},{16,24},{24,32},{32,40},{40,48},{48,56},{56,6... | collective-permute-start | bytes 98312 | tf_op jit(solution)/shard_map/while/body/eval_jaxpr/ppermute | solution.py:15
  548.1 108.7 %all-to-all-start.1 = ((bf16[32,1,24,2880]{3,2,1,0:T(8,128)(2,1)}), bf16[32,1,24,2880]{3,2,1,0:T(8,128)(2,1)}, u32[]{:S(2)}, u32[]{:S(2)}) async-start(bf16[32,1,24,2880]{3,2,1,0:T(8,128)(2,1)} %fusion.14), calls=%async_computation.1 | async-start | bytes 9043968 | tf_op jit(solution)/shard_map/all_to_all | solution.py:137
  553.1 165.1 %reduce-scatter.4.cloned.1.call-start = ((), (), s32[]{:S(2)}) async-start(), calls=%async_computation.4 | async-start | bytes 847872
  (23 other events, 605.5 us)
Sparse Core Ops, SparseCore 0:
  317.8 77.9 all-reduce.1
  685.6 32.5 reduce-scatter.3
where the time goes:
time: 737 us; the launch traced here: 732 us
  waiting for transfers between devices  426 us (58%)
  blocking collectives  166 us (23%)
  local copies, waits for them, and re-layouts  47.7 us (6%)
  matrix products  36.4 us (5%)
  other arithmetic  27.7 us (4%)
  between operations  14.4 us (2%)
  starting transfers between devices  10.6 us (1%)
    ppermute x31, waiting for transfers between devices, shifted(): return lax.ppermute(block, axis, route)  219 us
    all_to_all x1, blocking collectives, local(): lax.all_to_all(outgoing, 'ctx', split_axis=0, concat_axis=0, tiled=True)  118 us
    all_to_all x1, waiting for transfers between devices, local(): lax.all_to_all(expert_part, 'ctx', split_axis=0, concat_axis=0, tiled=True)  103 us
    psum x1, waiting for transfers between devices, local(): attended_all = lax.psum(partial_value.astype(jnp.bfloat16), 'exp')  75.6 us
    all_gather x1, blocking collectives, local(): all_positions = lax.all_gather(positions, 'ctx', axis=0, tiled=True)  48.4 us
    unnamed x3, waiting for transfers between devices  28.5 us
  transfers between devices with their start and end apart: 34, of which 34 were waited for; matrix products, arithmetic and copies ran while one was open for 2% of the time, Pallas kernels for 0%

commit v1 on v0

v1 whole, which is shorter than its diff:
```python
import functools

import jax
import jax.numpy as jnp
from jax import lax
from jax.experimental import pallas as pl
from jax.experimental.pallas import tpu as pltpu
from jax.sharding import PartitionSpec as P

HEAD_WIDTH = 64
EPSILON = 1e-05
CHUNK = 384
EXTRA = 16
BF16 = jnp.bfloat16
F32 = jnp.float32
VMEM = pl.BlockSpec(memory_space=pltpu.VMEM)
SMEM = pl.BlockSpec(memory_space=pltpu.SMEM)


def call(kernel, out_shapes, in_specs, vmem_mib=48):
    single = not isinstance(out_shapes, (list, tuple))
    out_specs = VMEM if single else [VMEM] * len(out_shapes)
    return pl.pallas_call(
        kernel,
        out_shape=out_shapes,
        in_specs=in_specs,
        out_specs=out_specs,
        compiler_params=pltpu.CompilerParams(vmem_limit_bytes=vmem_mib * 1024 * 1024),
    )


def shape(dims, dtype=BF16):
    return jax.ShapeDtypeStruct(dims, dtype)


def dot(a, b, contract=((1,), (0,))):
    return lax.dot_general(a, b, (contract, ((), ())), preferred_element_type=F32)


def spans(width):
    return [(start, min(CHUNK, width - start)) for start in range(0, width, CHUNK)]


def kv_kernel(pos_ref, tokens_ref, gain_ref, key_ref, value_ref, normed_ref, payload_ref):
    rows = tokens_ref.shape[0]
    values = tokens_ref[...].astype(F32)
    mean_square = jnp.mean(values * values, axis=-1, keepdims=True)
    normed = (values * lax.rsqrt(mean_square + EPSILON) * gain_ref[...]).astype(BF16)
    normed_ref[...] = normed
    keys = dot(normed, key_ref[...])
    vals = dot(normed, value_ref[...])
    payload_ref[:rows, :] = jnp.concatenate([keys, vals], axis=1).astype(BF16)
    base = pos_ref[0]
    lane = lax.broadcasted_iota(jnp.int32, (EXTRA, payload_ref.shape[1]), 1)
    marks = jnp.where(lane == 0, base // 128, jnp.where(lane == 1, base % 128, 0))
    payload_ref[rows:, :] = marks.astype(F32).astype(BF16)


def query_kernel(normed_ref, w_ref, out_ref):
    rows = normed_ref.shape[0]
    heads = w_ref.shape[1] // HEAD_WIDTH
    queries = dot(normed_ref[...], w_ref[...]).astype(BF16)
    queries = queries * jnp.asarray(HEAD_WIDTH ** (-0.5), BF16)
    for head in range(heads):
        out_ref[head * rows:(head + 1) * rows, :] = queries[
            :, head * HEAD_WIDTH:(head + 1) * HEAD_WIDTH
        ]


def route_kernel(experts, slots, ids_ref, weights_ref, gather_ref, combine_ref):
    rows, top = ids_ref.shape
    cells = experts * slots
    expert_lane = lax.broadcasted_iota(jnp.int32, (rows, experts), 1)
    chosen = [(ids_ref[:, k:k + 1] == expert_lane).astype(F32) for k in range(top)]
    named = functools.reduce(jnp.add, chosen)
    below = lax.broadcasted_iota(jnp.int32, (rows, rows), 1) < lax.broadcasted_iota(
        jnp.int32, (rows, rows), 0
    )
    place = dot(below.astype(BF16), named.astype(BF16)) + (expert_lane * slots).astype(F32)
    cell = lax.broadcasted_iota(jnp.int32, (rows, cells), 1).astype(F32)
    filled = jnp.zeros((rows, cells), F32)
    scaled = jnp.zeros((rows, cells), F32)
    for k in range(top):
        target = jnp.sum(chosen[k] * place, axis=1, keepdims=True)
        match = cell == target
        filled = jnp.where(match, 1.0, filled)
        scaled = jnp.where(match, weights_ref[:, k:k + 1], scaled)
    gather_ref[...] = filled.T.astype(BF16)
    for part in range(3):
        rounded = scaled.astype(BF16)
        combine_ref[part * rows:(part + 1) * rows, :] = rounded
        scaled = scaled - rounded.astype(F32)


def attention_kernel(blocks, pos_ref, query_ref, kv_ref, sink_ref, w_ref, out_ref):
    count, padded, pair = kv_ref.shape
    rows = padded - EXTRA
    columns = query_ref.shape[0]
    width = w_ref.shape[1]
    key_row = lax.broadcasted_iota(jnp.int32, (rows, columns), 0)
    query_row = lax.broadcasted_iota(jnp.int32, (rows, columns), 1) % rows
    offset = (key_row - query_row).astype(F32)
    mine = pos_ref[0].astype(F32)

    def step(turn, carry):
        top_old, den, mixed = carry
        parts = []
        held = []
        for j in range(blocks):
            block = turn * blocks + j
            marks = kv_ref[block, rows:rows + EXTRA, :].astype(F32)
            base = marks[0:1, 0:1] * 128.0 + marks[0:1, 1:2]
            kv = kv_ref[block, :rows, :]
            held.append(kv[:, HEAD_WIDTH:])
            scores = dot(kv[:, :HEAD_WIDTH], query_ref[...], ((1,), (1,)))
            parts.append(jnp.where(offset <= mine - base, scores, -1e30))
        scores = jnp.concatenate(parts, axis=0)
        vals = jnp.concatenate(held, axis=0)
        top_new = jnp.maximum(top_old, jnp.max(scores, axis=0, keepdims=True))
        rescale = jnp.exp(top_old - top_new)
        probs = jnp.exp(scores - top_new)
        den = den * rescale + jnp.sum(probs, axis=0, keepdims=True)
        mixed = mixed * rescale + dot(vals, probs.astype(BF16), ((0,), (0,)))
        return top_new, den, mixed

    start = (
        sink_ref[...],
        jnp.ones((1, columns), F32),
        jnp.zeros((pair - HEAD_WIDTH, columns), F32),
    )
    _, den, mixed = lax.fori_loop(0, count // blocks, step, start)
    heads = (mixed / den).astype(BF16)
    stacked = jnp.concatenate(
        [heads[:, head * rows:(head + 1) * rows] for head in range(columns // rows)], axis=0
    )
    for index, (first, size) in enumerate(spans(width)):
        part = dot(stacked, w_ref[:, first:first + size], ((0,), (0,))).astype(BF16)
        out_ref[index, :, :size] = part
        if size < CHUNK:
            out_ref[index, :, size:] = jnp.zeros((rows, CHUNK - size), BF16)


def residual_kernel(parts_ref, tokens_ref, attended_ref, residual_ref, squares_ref):
    total = parts_ref[0].astype(F32)
    for index in range(1, parts_ref.shape[0]):
        total = total + parts_ref[index].astype(F32)
    attended = total.astype(BF16)
    attended_ref[...] = attended
    residual = tokens_ref[...].astype(F32) + attended.astype(F32)
    residual_ref[...] = residual
    column = jnp.sum(residual * residual, axis=1, keepdims=True)
    squares_ref[...] = jnp.broadcast_to(column, (column.shape[0], 128)).T[:8, :]


def dispatch_kernel(width, squares_ref, residual_ref, gain_ref, gather_ref, out_ref):
    total = squares_ref[0]
    for index in range(1, squares_ref.shape[0]):
        total = total + squares_ref[index]
    column = jnp.broadcast_to(total[0:1, :], (total.shape[1], total.shape[1])).T[:, 0:1]
    scale = lax.rsqrt(column / width + EPSILON)
    moe_in = (residual_ref[...] * scale * gain_ref[...]).astype(BF16)
    out_ref[...] = dot(gather_ref[...], moe_in).astype(BF16)


def expert_kernel(width, sets, rows_ref, *refs):
    weights, out_ref = refs[:-1], refs[-1]
    hidden = []
    for index in range(sets):
        gate_ref, up_ref = weights[3 * index], weights[3 * index + 1]
        gate, up = 0.0, 0.0
        for place, (first, size) in enumerate(spans(width)):
            rows = rows_ref[place, :, :size]
            gate = gate + dot(rows, gate_ref[first:first + size, :])
            up = up + dot(rows, up_ref[first:first + size, :])
        hidden.append((gate * jax.nn.sigmoid(1.702 * gate) * (up + 1.0)).astype(BF16))
    for place, (first, size) in enumerate(spans(width)):
        part = 0.0
        for index in range(sets):
            part = part + dot(hidden[index], weights[3 * index + 2][:, first:first + size])
        out_ref[place, :, :size] = part.astype(BF16)
        if size < CHUNK:
            out_ref[place, :, size:] = jnp.zeros((part.shape[0], CHUNK - size), BF16)


def sum_kernel(groups, parts_ref, out_ref):
    for half, members in enumerate(groups):
        total = parts_ref[members[0]].astype(F32)
        for index in members[1:]:
            total = total + parts_ref[index].astype(F32)
        out_ref[half] = total.astype(BF16)


def combine_kernel(returned_ref, combine_ref, residual_ref, attended_ref, out_ref):
    rows = residual_ref.shape[0]
    mixed = dot(combine_ref[...], returned_ref[...])
    total = mixed[:rows] + mixed[rows:2 * rows] + mixed[2 * rows:]
    out_ref[:, :CHUNK] = attended_ref[...]
    out_ref[:, CHUNK:] = (residual_ref[...] + total).astype(BF16)


def finish_kernel(parts_ref, attended_ref, layer_ref):
    for index, (first, size) in enumerate(spans(attended_ref.shape[1])):
        attended_ref[:, first:first + size] = parts_ref[index, :, :size]
        layer_ref[:, first:first + size] = parts_ref[index, :, CHUNK:CHUNK + size]


def exchange(block, axis):
    return lax.all_to_all(block, axis, split_axis=0, concat_axis=0, tiled=True)


def local(
    tokens,
    positions,
    norm_attn,
    norm_moe,
    w_query,
    key_matrix,
    value_matrix,
    w_out,
    sinks,
    expert_ids,
    expert_weights,
    w_gate,
    w_up,
    w_down,
):
    ctx_count = lax.axis_size("ctx")
    exp_count = lax.axis_size("exp")
    rows, width = tokens.shape
    heads = sinks.shape[0]
    top = expert_ids.shape[1]
    experts = ctx_count
    slots = rows * top * 3 // (2 * experts)
    padded_width = exp_count * CHUNK
    member = lax.axis_index("exp")

    own = (w_gate[0], w_up[0], w_down[0])
    swap = [(i, i ^ 2) for i in range(exp_count)]
    other = tuple(lax.ppermute(w, "exp", swap) for w in own)

    normed, payload = call(
        kv_kernel,
        [shape((rows, width)), shape((rows + EXTRA, 2 * HEAD_WIDTH))],
        [SMEM, VMEM, VMEM, VMEM, VMEM],
    )(positions, tokens, norm_attn[None], key_matrix, value_matrix)
    gathered = exchange(jnp.broadcast_to(payload[None], (ctx_count,) + payload.shape), "ctx")
    queries = call(query_kernel, shape((heads * rows, HEAD_WIDTH)), [VMEM, VMEM])(normed, w_query)
    gather_table, combine_table = call(
        functools.partial(route_kernel, experts, slots),
        [shape((experts * slots, rows)), shape((3 * rows, experts * slots))],
        [VMEM, VMEM],
    )(expert_ids, expert_weights)
    sink_row = jnp.repeat(sinks, rows)[None]
    own_tokens = lax.dynamic_slice_in_dim(
        jnp.pad(tokens, ((0, 0), (0, padded_width - width))), member * CHUNK, CHUNK, 1
    )
    own_gain = lax.dynamic_slice_in_dim(
        jnp.pad(norm_moe, (0, padded_width - width)), member * CHUNK, CHUNK, 0
    )[None]

    partial_sums = call(
        functools.partial(attention_kernel, 4),
        shape((exp_count, rows, CHUNK)),
        [SMEM, VMEM, VMEM, VMEM, VMEM],
    )(positions, queries, gathered, sink_row, w_out)
    parts = exchange(partial_sums, "exp")
    attended, residual, squares = call(
        residual_kernel,
        [shape((rows, CHUNK)), shape((rows, CHUNK), F32), shape((8, rows), F32)],
        [VMEM, VMEM],
    )(parts, own_tokens)
    all_squares = exchange(jnp.broadcast_to(squares[None], (exp_count, 8, rows)), "exp")
    outgoing = call(
        functools.partial(dispatch_kernel, width),
        shape((experts * slots, CHUNK)),
        [VMEM, VMEM, VMEM, VMEM],
    )(all_squares, residual, own_gain, gather_table)

    arrived = exchange(outgoing.reshape(ctx_count, slots, CHUNK), "ctx")
    halves = arrived.reshape(2, ctx_count * slots // 2, CHUNK)
    expert_rows = exchange(
        jnp.stack([halves[(i >> 1) & 1] for i in range(exp_count)]), "exp"
    )
    products = call(
        functools.partial(expert_kernel, width, 2),
        shape(expert_rows.shape),
        [VMEM] * 7,
        56,
    )(expert_rows, *own, *other)
    product_parts = exchange(products, "exp")
    groups = [[i for i in range(exp_count) if (i >> 1) & 1 == half] for half in range(2)]
    summed = call(functools.partial(sum_kernel, groups), shape(halves.shape), [VMEM])(product_parts)
    returned = exchange(summed.reshape(ctx_count, slots, CHUNK), "ctx")
    final = call(combine_kernel, shape((rows, 2 * CHUNK)), [VMEM] * 4)(
        returned.reshape(experts * slots, CHUNK), combine_table, residual, attended
    )
    final = exchange(final.reshape(exp_count, rows // exp_count, 2 * CHUNK), "exp")
    out = shape((rows // exp_count, width))
    return tuple(call(finish_kernel, [out, out], [VMEM])(final))


def solution(mesh):
    in_specs = (
        P("ctx", None),
        P("ctx"),
        P(),
        P(),
        P(None, "exp"),
        P(None, "exp"),
        P(None, "exp"),
        P("exp", None),
        P("exp"),
        P("ctx", None),
        P("ctx", None),
        P("ctx", None, "exp"),
        P("ctx", None, "exp"),
        P("ctx", "exp", None),
    )
    out_specs = (P(("ctx", "exp"), None), P(("ctx", "exp"), None))
    return jax.shard_map(local, mesh=mesh, in_specs=in_specs, out_specs=out_specs, check_vma=False)
```

time: 737 us -> 307 us (0.42)
  waiting for transfers between devices: 426 us -> 123 us
  blocking collectives: 166 us -> 95.9 us
  matrix products: 36.4 us -> 0 us
  other arithmetic: 27.7 us -> 0 us
  Pallas kernels: 0 us -> 26.9 us
  starting transfers between devices: 10.6 us -> 30.6 us
  local copies, waits for them, and re-layouts: 47.7 us -> 29.2 us
  between operations: 14.4 us -> 0.84 us
    ppermute x31 -> x3, waiting for transfers between devices: 219 us -> 85 us  [local(): other = tuple((lax.ppermute(w, 'exp', swap) for w in own))]
    psum x1 -> x0, waiting for transfers between devices: 75.6 us -> none  [local(): attended_all = lax.psum(partial_value.astype(jnp.bfloat16), 'exp')]
    all_to_all x1 -> x4, waiting for transfers between devices: 103 us -> 37.7 us  [exchange(): return lax.all_to_all(block, axis, split_axis=0, concat_axis=0, tiled=True)]
    all_gather x1 -> x0, blocking collectives: 48.4 us -> none  [local(): all_positions = lax.all_gather(positions, 'ctx', axis=0, tiled=True)]
    dot_general x70 -> x0, matrix products: 36.4 us -> none  [the longest x1 10.2 us: local(): jnp.einsum('sjcf,jfd->sjcd', activated, w_down, preferred_element_type=jn...]
    unnamed x3 -> x0, waiting for transfers between devices: 28.5 us -> none
    pallas_call x0 -> x10, Pallas kernels: none -> 26.9 us  [the longest x1 11.6 us: local(): call(functools.partial(attention_kernel, 4), shape((exp_count, rows, CHUN...]
    all_to_all x1 -> x4, starting transfers between devices: 4.98 us -> 27.8 us  [exchange(): return lax.all_to_all(block, axis, split_axis=0, concat_axis=0, tiled=True)]
  transfers between devices with their start and end apart: 34 -> 7, of which waited for: 34 -> 6; matrix products, arithmetic and copies ran while one was open for 2% -> 4% of each run, Pallas kernels for 0% -> 0%
where the time goes in v1:
time: 307 us; the launch traced here: 306 us
  waiting for transfers between devices  123 us (40%)
  blocking collectives  95.9 us (31%)
  starting transfers between devices  30.6 us (10%)
  local copies, waits for them, and re-layouts  29.2 us (10%)
  Pallas kernels  26.9 us (9%)
    all_to_all x4, blocking collectives, exchange(): return lax.all_to_all(block, axis, split_axis=0, concat_axis=0, tiled=True)  95.9 us
    ppermute x3, waiting for transfers between devices, local(): other = tuple((lax.ppermute(w, 'exp', swap) for w in own))  85 us
    all_to_all x4, waiting for transfers between devices, exchange(): return lax.all_to_all(block, axis, split_axis=0, concat_axis=0, tiled=True)  37.7 us
    all_to_all x4, starting transfers between devices, exchange(): return lax.all_to_all(block, axis, split_axis=0, concat_axis=0, tiled=True)  27.8 us
    unnamed x43, local copies, waits for them, and re-layouts  20.4 us
    pallas_call x1, Pallas kernels, local(): call(functools.partial(attention_kernel, 4), shape((exp_count, rows, CHUN...  11.6 us
    pallas_call x1, Pallas kernels, local(): call(functools.partial(expert_kernel, width, 2), shape(expert_rows.shape)...  10.4 us
  transfers between devices with their start and end apart: 7, of which 6 were waited for; matrix products, arithmetic and copies ran while one was open for 4% of the time, Pallas kernels for 0%

profile of v1, /device:TPU:1, one launch (start us, length us, event | category | flops | bytes accessed | tf_op | source)
XLA Modules:
  0.0 306.1 jit_solution(5769003643825698925)
XLA Ops:
  0.7 1.5 copy.25.tokens_ref
  2.2 1.6 copy.26.key_ref
  7.7 12.6 %all-to-all-start = ((bf16[32,144,128]{2,1,0:T(8,128)(2,1)}), bf16[32,144,128]{2,1,0:T(8,128)(2,1)}, u32[]{:S(2)}, u32[]{:S(2)}) async-start(bf16[32,144,128]{2,1,0:T(8,128)(2,1)} %broadcast_in_dim.22), calls=%async_computation | async-start | bytes 2359296 | tf_op jit(solution)/shard_map/all_to_all | solution.py:208
  20.3 3.3 %copy.28.w_ref = bf16[512,2880]{1,0:T(8,128)(2,1)S(1)} copy(bf16[512,2880]{0,1:T(8,128)(2,1)} %param.21) | data formatting | bytes 5898240 | tf_op args[7]
  23.7 1.8 copy-done.2
  27.3 22.9 %all-to-all-done.kv_ref = bf16[32,144,128]{2,1,0:T(8,128)(2,1)} async-done(((bf16[32,144,128]{2,1,0:T(8,128)(2,1)}), bf16[32,144,128]{2,1,0:T(8,128)(2,1)}, u32[]{:S(2)}, u32[]{:S(2)}) %all-to-all-start) | async-done | bytes 1179680 | tf_op jit(solution)/shard_map/all_to_all | solution.py:208
  50.3 11.6 %shard_map.151 = bf16[8,128,384]{2,1,0:T(8,128)(2,1)S(1)} custom-call(s32[128]{0:T(128)S(1)} %copy-done.5, bf16[1024,64]{1,0:T(8,128)(2,1)S(1)} %shard_map.150.query_ref, bf16[32,144,128]{2,1,0:T(8,128)(2,1)} %all-to-all-done.kv_ref, f32[1,1024]{1,0:T(1,128)S(1)} %bitcast.32, bf16[512,2880]{1,0:T(8,128)(2,1)S(1)} %copy.28.w_ref), custom_call_target="tpu_custom_call" | custom-call | tf_op jit(solution)/shard_map/pallas_call | solution.py:261
  62.8 6.9 %all-to-all-start.1 = ((bf16[8,128,384]{2,1,0:T(8,128)(2,1)}), bf16[8,128,384]{2,1,0:T(8,128)(2,1)S(1)}, u32[]{:S(2)}, u32[]{:S(2)}) async-start(bf16[8,128,384]{2,1,0:T(8,128)(2,1)} %copy-done.1), calls=%async_computation.1 | async-start | bytes 1572864 | tf_op jit(solution)/shard_map/all_to_all | solution.py:208
  70.6 10.6 %all-to-all-done.1.parts_ref = bf16[8,128,384]{2,1,0:T(8,128)(2,1)S(1)} async-done(((bf16[8,128,384]{2,1,0:T(8,128)(2,1)}), bf16[8,128,384]{2,1,0:T(8,128)(2,1)S(1)}, u32[]{:S(2)}, u32[]{:S(2)}) %all-to-all-start.1) | async-done | bytes 786464 | tf_op jit(solution)/shard_map/all_to_all | solution.py:208
  82.1 3.8 %all-to-all-start.2 = ((f32[8,8,128]{2,1,0:T(8,128)}), f32[8,8,128]{2,1,0:T(8,128)S(1)}, u32[]{:S(2)}, u32[]{:S(2)}) async-start(f32[8,8,128]{2,1,0:T(8,128)} %broadcast_in_dim.24), calls=%async_computation.2 | async-start | bytes 65536 | tf_op jit(solution)/shard_map/all_to_all | solution.py:208
  87.0 4.1 %all-to-all-done.2.squares_ref = f32[8,8,128]{2,1,0:T(8,128)S(1)} async-done(((f32[8,8,128]{2,1,0:T(8,128)}), f32[8,8,128]{2,1,0:T(8,128)S(1)}, u32[]{:S(2)}, u32[]{:S(2)}) %all-to-all-start.2) | async-done | bytes 32800 | tf_op jit(solution)/shard_map/all_to_all | solution.py:208
  91.5 26.6 %all_to_all.40 = bf16[32,24,384]{2,1,0:T(8,128)(2,1)S(1)} all-to-all(bf16[32,24,384]{2,1,0:T(8,128)(2,1)S(1)} %bitcast.29), channel_id=1, replica_groups=mesh['ctx'=32,'exp'=8] {'ctx'}, dimensions={0} | all-to-all | bytes 1179648 | tf_op jit(solution)/shard_map/all_to_all | solution.py:208
  124.2 4.5 %all-to-all-start.4 = ((bf16[8,384,384]{2,1,0:T(8,128)(2,1)}), bf16[8,384,384]{2,1,0:T(8,128)(2,1)}, u32[]{:S(2)}, u32[]{:S(2)}) async-start(bf16[8,384,384]{2,1,0:T(8,128)(2,1)} %bitcast_dynamic-update-slice_fusion.3), calls=%async_computation.4 | async-start | bytes 4718592 | tf_op jit(solution)/shard_map/all_to_all | solution.py:208
  131.5 1.7 copy.32
  133.2 1.6 copy.33
  134.8 43.6 %collective-permute-done = bf16[2880,180]{0,1:T(8,128)(2,1)} collective-permute-done((bf16[2880,180]{0,1:T(8,128)(2,1)S(1)}, bf16[2880,180]{0,1:T(8,128)(2,1)}, u32[]{:S(2)}, u32[]{:S(2)}) %collective-permute-start) | collective-permute-done | bytes 1036832 | tf_op jit(solution)/shard_map/ppermute | solution.py:239
  178.4 2.6 copy.36.refs_3_
  181.0 20.7 %collective-permute-done.1 = bf16[2880,180]{0,1:T(8,128)(2,1)} collective-permute-done((bf16[2880,180]{0,1:T(8,128)(2,1)S(1)}, bf16[2880,180]{0,1:T(8,128)(2,1)}, u32[]{:S(2)}, u32[]{:S(2)}) %collective-permute-start.1) | collective-permute-done | bytes 1036832 | tf_op jit(solution)/shard_map/ppermute | solution.py:239
  201.7 2.5 copy.37.refs_4_
  204.2 20.7 %collective-permute-done.2.refs_5_ = bf16[180,2880]{1,0:T(8,128)(2,1)} collective-permute-done((bf16[180,2880]{1,0:T(8,128)(2,1)}, bf16[180,2880]{1,0:T(8,128)(2,1)}, u32[]{:S(2)}, u32[]{:S(2)}) %collective-permute-start.2) | collective-permute-done | bytes 1036832 | tf_op jit(solution)/shard_map/ppermute | solution.py:239
  224.9 10.4 %shard_map.155 = bf16[8,384,384]{2,1,0:T(8,128)(2,1)} custom-call(bf16[8,384,384]{2,1,0:T(8,128)(2,1)} %all-to-all-done.4.rows_ref, bf16[2880,180]{1,0:T(8,128)(2,1)} %bitcast.41, bf16[2880,180]{1,0:T(8,128)(2,1)} %bitcast.42, bf16[180,2880]{1,0:T(8,128)(2,1)} %bitcast.46, bf16[2880,180]{1,0:T(8,128)(2,1)} %copy.36.refs_3_, bf16[2880,180]{1,0:T(8,128)(2,1)} %copy.37.refs_4_, ...), custom_call_target="tpu_custom_call" | custom-call | tf_op jit(solution)/shard_map/pallas_call | solution.py:284
  235.3 35.2 %all_to_all.41.parts_ref = bf16[8,384,384]{2,1,0:T(8,128)(2,1)S(1)} all-to-all(bf16[8,384,384]{2,1,0:T(8,128)(2,1)} %shard_map.155), channel_id=1, replica_groups=mesh['ctx'=32,'exp'=8] {'exp'}, dimensions={0} | all-to-all | bytes 4718592 | tf_op jit(solution)/shard_map/all_to_all | solution.py:208
  270.8 25.6 %all_to_all.42 = bf16[32,24,384]{2,1,0:T(8,128)(2,1)S(1)} all-to-all(bf16[32,24,384]{2,1,0:T(8,128)(2,1)S(1)} %bitcast.30), channel_id=1, replica_groups=mesh['ctx'=32,'exp'=8] {'ctx'}, dimensions={0} | all-to-all | bytes 1179648 | tf_op jit(solution)/shard_map/all_to_all | solution.py:208
  296.9 8.4 %all_to_all.43.parts_ref = bf16[8,16,768]{2,1,0:T(8,128)(2,1)S(1)} all-to-all(bf16[8,16,768]{2,1,0:T(8,128)(2,1)S(1)} %bitcast.31), channel_id=1, replica_groups=mesh['ctx'=32,'exp'=8] {'exp'}, dimensions={0} | all-to-all | bytes 393216 | tf_op jit(solution)/shard_map/all_to_all | solution.py:208
  (58 shorter events, 20.2 us)
Async XLA Ops:
  0.6 3.2 %copy-start.8 = (bf16[2880,64]{0,1:T(8,128)(2,1)S(1)}, bf16[2880,64]{0,1:T(8,128)(2,1)}, u32[]{:S(2)}) copy-start(bf16[2880,64]{0,1:T(8,128)(2,1)} %param.20) | copy-start | bytes 1105924
  0.6 3.5 %copy-start.9 = (f32[2880]{0:T(1024)S(1)}, f32[2880]{0:T(1024)}, u32[]{:S(2)}) copy-start(f32[2880]{0:T(1024)} %param.16) | copy-start | bytes 34564
  0.7 3.5 %copy-start.5 = (s32[128]{0:T(128)S(1)}, s32[128]{0:T(128)}, u32[]{:S(2)}) copy-start(s32[128]{0:T(128)} %pos_ref.3) | copy-start | bytes 1540
  2.2 5.5 %copy-start = (bf16[128,2880]{1,0:T(8,128)(2,1)}, bf16[128,2880]{1,0:T(8,128)(2,1)S(1)}, u32[]{:S(2)}) copy-start(bf16[128,2880]{1,0:T(8,128)(2,1)S(1)} %copy.25.tokens_ref) | copy-start | bytes 2211844
  5.6 0.9 copy-start.3
  7.7 42.6 %all-to-all-start = ((bf16[32,144,128]{2,1,0:T(8,128)(2,1)}), bf16[32,144,128]{2,1,0:T(8,128)(2,1)}, u32[]{:S(2)}, u32[]{:S(2)}) async-start(bf16[32,144,128]{2,1,0:T(8,128)(2,1)} %broadcast_in_dim.22), calls=%async_computation | async-start | bytes 2359296 | tf_op jit(solution)/shard_map/all_to_all | solution.py:208
  23.6 26.6 %copy-start.13 = (f32[8]{0:T(128)S(1)}, f32[8]{0:T(128)}, u32[]{:S(2)}) copy-start(f32[8]{0:T(128)} %param.22) | copy-start | bytes 100
  23.7 1.8 copy-start.2
  25.5 1.1 copy-start.4
  61.9 0.9 copy-start.1
  62.8 23.1 %copy-start.10 = (f32[2880]{0:T(1024)S(1)}, f32[2880]{0:T(1024)}, u32[]{:S(2)}) copy-start(f32[2880]{0:T(1024)} %param.17) | copy-start | bytes 34564
  62.8 23.2 %copy-start.11 = (s32[128,4]{0,1:T(4,128)S(1)}, s32[128,4]{0,1:T(4,128)}, u32[]{:S(2)}) copy-start(s32[128,4]{0,1:T(4,128)} %param.23) | copy-start | bytes 6148
  62.8 23.3 %copy-start.12 = (f32[128,4]{0,1:T(4,128)S(1)}, f32[128,4]{0,1:T(4,128)}, u32[]{:S(2)}) copy-start(f32[128,4]{0,1:T(4,128)} %param.24) | copy-start | bytes 6148
  62.8 18.4 %all-to-all-start.1 = ((bf16[8,128,384]{2,1,0:T(8,128)(2,1)}), bf16[8,128,384]{2,1,0:T(8,128)(2,1)S(1)}, u32[]{:S(2)}, u32[]{:S(2)}) async-start(bf16[8,128,384]{2,1,0:T(8,128)(2,1)} %copy-done.1), calls=%async_computation.1 | async-start | bytes 1572864 | tf_op jit(solution)/shard_map/all_to_all | solution.py:208
  82.1 8.9 %all-to-all-start.2 = ((f32[8,8,128]{2,1,0:T(8,128)}), f32[8,8,128]{2,1,0:T(8,128)S(1)}, u32[]{:S(2)}, u32[]{:S(2)}) async-start(f32[8,8,128]{2,1,0:T(8,128)} %broadcast_in_dim.24), calls=%async_computation.2 | async-start | bytes 65536 | tf_op jit(solution)/shard_map/all_to_all | solution.py:208
  124.2 4.5 %copy-start.6 = (bf16[1,2880,180]{1,2,0:T(8,128)(2,1)S(1)}, bf16[1,2880,180]{1,2,0:T(8,128)(2,1)}, u32[]{:S(2)}) copy-start(bf16[1,2880,180]{1,2,0:T(8,128)(2,1)} %param.25) | copy-start | bytes 3110404
  124.2 5.9 %copy-start.7 = (bf16[1,2880,180]{1,2,0:T(8,128)(2,1)S(1)}, bf16[1,2880,180]{1,2,0:T(8,128)(2,1)}, u32[]{:S(2)}) copy-start(bf16[1,2880,180]{1,2,0:T(8,128)(2,1)} %param.26) | copy-start | bytes 3110404
  124.2 100.7 %all-to-all-start.4 = ((bf16[8,384,384]{2,1,0:T(8,128)(2,1)}), bf16[8,384,384]{2,1,0:T(8,128)(2,1)}, u32[]{:S(2)}, u32[]{:S(2)}) async-start(bf16[8,384,384]{2,1,0:T(8,128)(2,1)} %bitcast_dynamic-update-slice_fusion.3), calls=%async_computation.4 | async-start | bytes 4718592 | tf_op jit(solution)/shard_map/all_to_all | solution.py:208
  128.7 49.8 %collective-permute-start = (bf16[2880,180]{0,1:T(8,128)(2,1)S(1)}, bf16[2880,180]{0,1:T(8,128)(2,1)}, u32[]{:S(2)}, u32[]{:S(2)}) collective-permute-start(bf16[2880,180]{0,1:T(8,128)(2,1)S(1)} %bitcast.43), channel_id=1, source_target_pairs={{0,2},{1,3},{2,0},{3,1},{4,6},{5,7},{6,4},{7,5},{8,10},{9,11},{10,... | collective-permute-start | bytes 3110408 | tf_op jit(solution)/shard_map/ppermute | solution.py:239
  130.0 71.6 %collective-permute-start.1 = (bf16[2880,180]{0,1:T(8,128)(2,1)S(1)}, bf16[2880,180]{0,1:T(8,128)(2,1)}, u32[]{:S(2)}, u32[]{:S(2)}) collective-permute-start(bf16[2880,180]{0,1:T(8,128)(2,1)S(1)} %bitcast.44), channel_id=1, source_target_pairs={{0,2},{1,3},{2,0},{3,1},{4,6},{5,7},{6,4},{7,5},{8,10},{9,11},{10,... | collective-permute-start | bytes 3110408 | tf_op jit(solution)/shard_map/ppermute | solution.py:239
  130.2 94.6 %collective-permute-start.2 = (bf16[180,2880]{1,0:T(8,128)(2,1)}, bf16[180,2880]{1,0:T(8,128)(2,1)}, u32[]{:S(2)}, u32[]{:S(2)}) collective-permute-start(bf16[180,2880]{1,0:T(8,128)(2,1)} %bitcast.45), channel_id=1, source_target_pairs={{0,2},{1,3},{2,0},{3,1},{4,6},{5,7},{6,4},{7,5},{8,10},{9,11},{10,... | collective-permute-start | bytes 3110408 | tf_op jit(solution)/shard_map/ppermute | solution.py:239

commit v2 on v1

v2 whole, which is shorter than its diff:
```python
import functools

import jax
import jax.numpy as jnp
from jax import lax
from jax.experimental import pallas as pl
from jax.experimental.pallas import tpu as pltpu
from jax.sharding import PartitionSpec as P

HEAD_WIDTH = 64
EPSILON = 1e-05
CHUNK = 384
TAIL = 16
MAIN = CHUNK - TAIL
EXTRA = 16
BF16 = jnp.bfloat16
F32 = jnp.float32
VMEM = pl.BlockSpec(memory_space=pltpu.VMEM)
SMEM = pl.BlockSpec(memory_space=pltpu.SMEM)
HBM = pl.BlockSpec(memory_space=pltpu.HBM)


def in_hbm(array):
    return pltpu.with_memory_space_constraint(array, pltpu.HBM)


def call(kernel, out_shapes, in_specs, vmem_mib=24):
    single = not isinstance(out_shapes, (list, tuple))
    out_specs = VMEM if single else [VMEM] * len(out_shapes)
    return pl.pallas_call(
        kernel,
        out_shape=out_shapes,
        in_specs=in_specs,
        out_specs=out_specs,
        compiler_params=pltpu.CompilerParams(vmem_limit_bytes=vmem_mib * 1024 * 1024),
    )


def shape(dims, dtype=BF16):
    return jax.ShapeDtypeStruct(dims, dtype)


def dot(a, b, contract=((1,), (0,))):
    return lax.dot_general(a, b, (contract, ((), ())), preferred_element_type=F32)


def spans(width):
    return [(start, min(CHUNK, width - start)) for start in range(0, width, CHUNK)]


def fetch(sources, held, sems):
    copies = [
        pltpu.make_async_copy(source, target, sems.at[index])
        for index, (source, target) in enumerate(zip(sources, held))
    ]
    for copy in copies:
        copy.start()
    return copies


def tail_spans(width):
    full = width // CHUNK
    return [(full * CHUNK, width - full * CHUNK)] + [
        (place * CHUNK + MAIN, TAIL) for place in range(full)
    ]


def kv_kernel(
    pos_ref, tokens_hbm, gain_hbm, key_hbm, value_hbm, normed_ref, payload_ref,
    tokens_ref, gain_ref, key_ref, value_ref, sems,
):
    sources = (tokens_hbm, gain_hbm, key_hbm, value_hbm)
    copies = fetch(sources, (tokens_ref, gain_ref, key_ref, value_ref), sems)
    rows = tokens_ref.shape[1]
    copies[0].wait()
    values = tokens_ref[...].T.astype(F32)
    mean_square = jnp.mean(values * values, axis=-1, keepdims=True)
    copies[1].wait()
    normed = (values * lax.rsqrt(mean_square + EPSILON) * gain_ref[...][None, :]).astype(BF16)
    normed_ref[...] = normed
    copies[2].wait()
    keys = dot(normed, key_ref[...], ((1,), (1,)))
    copies[3].wait()
    vals = dot(normed, value_ref[...], ((1,), (1,)))
    payload_ref[:rows, :] = jnp.concatenate([keys, vals], axis=1).astype(BF16)
    base = pos_ref[0]
    lane = lax.broadcasted_iota(jnp.int32, (EXTRA, payload_ref.shape[1]), 1)
    marks = jnp.where(lane == 0, base // 128, jnp.where(lane == 1, base % 128, 0))
    payload_ref[rows:, :] = marks.astype(F32).astype(BF16)


def project_kv(positions, tokens, gain, keys, vals):
    width, rows = tokens.shape
    arrays = (tokens, gain, keys, vals)
    return pl.pallas_call(
        kv_kernel,
        out_shape=[shape((rows, width)), shape((rows + EXTRA, 2 * HEAD_WIDTH))],
        in_specs=[SMEM] + [HBM] * 4,
        out_specs=[VMEM, VMEM],
        scratch_shapes=[pltpu.VMEM(a.shape, a.dtype) for a in arrays]
        + [pltpu.SemaphoreType.DMA((4,))],
        compiler_params=pltpu.CompilerParams(vmem_limit_bytes=32 * 1024 * 1024),
    )(in_hbm(positions), *[in_hbm(a) for a in arrays])


def query_kernel(normed_ref, w_ref, out_ref):
    rows = normed_ref.shape[0]
    heads = w_ref.shape[1] // HEAD_WIDTH
    queries = dot(normed_ref[...], w_ref[...]).astype(BF16)
    queries = queries * jnp.asarray(HEAD_WIDTH ** (-0.5), BF16)
    lane = lax.broadcasted_iota(jnp.int32, (rows, HEAD_WIDTH), 1)
    flag = jnp.where(lane == 0, 1.0, 0.0).astype(BF16)
    for head in range(heads):
        own = queries[:, head * HEAD_WIDTH:(head + 1) * HEAD_WIDTH]
        out_ref[head * rows:(head + 1) * rows, :] = jnp.concatenate([own, flag], axis=1)


def upright(ref):
    spare = jnp.zeros((8 - ref.shape[0], ref.shape[1]), F32)
    return jnp.concatenate([ref[...].astype(F32), spare], axis=0).T


def prepare_kernel(
    experts, slots, member_ref, ids_ref, weights_ref, tokens_ref, gain_ref,
    gather_ref, combine_ref, own_tokens_ref, own_gain_ref, gain_scratch,
):
    top, rows = ids_ref.shape
    cells = experts * slots
    ids, weights = upright(ids_ref), upright(weights_ref)
    expert_lane = lax.broadcasted_iota(jnp.int32, (rows, experts), 1).astype(F32)
    chosen = [(ids[:, k:k + 1] == expert_lane).astype(F32) for k in range(top)]
    named = functools.reduce(jnp.add, chosen)
    below = lax.broadcasted_iota(jnp.int32, (rows, rows), 1) < lax.broadcasted_iota(
        jnp.int32, (rows, rows), 0
    )
    place = dot(below.astype(BF16), named.astype(BF16)) + expert_lane * slots
    cell = lax.broadcasted_iota(jnp.int32, (rows, cells), 1).astype(F32)
    filled = jnp.zeros((rows, cells), F32)
    scaled = jnp.zeros((rows, cells), F32)
    for k in range(top):
        target = jnp.sum(chosen[k] * place, axis=1, keepdims=True)
        match = cell == target
        filled = jnp.where(match, 1.0, filled)
        scaled = jnp.where(match, weights[:, k:k + 1], scaled)
    gather_ref[...] = filled.T.astype(BF16)
    for part in range(3):
        rounded = scaled.astype(BF16)
        combine_ref[part * rows:(part + 1) * rows, :] = rounded
        scaled = scaled - rounded.astype(F32)

    width = tokens_ref.shape[0]
    full = width // CHUNK
    rest = width - full * CHUNK
    tails = tail_spans(width)
    spare = CHUNK - sum(size for _, size in tails)
    member = member_ref[0]
    is_last = jnp.full((1, 1), member, jnp.int32) == full
    start = pl.multiple_of(member * CHUNK, rest)
    second = pl.multiple_of(jnp.minimum(start + CHUNK - rest, full * CHUNK), rest)
    main = jnp.concatenate(
        [tokens_ref[pl.ds(start, rest), :], tokens_ref[pl.ds(second, CHUNK - rest), :]], axis=0
    ).astype(F32)
    tail = jnp.concatenate(
        [tokens_ref[first:first + size, :].astype(F32) for first, size in tails]
        + [jnp.zeros((spare, rows), F32)],
        axis=0,
    )
    feature = lax.broadcasted_iota(jnp.int32, main.shape, 0)
    own = jnp.where(is_last, tail, jnp.where(feature < MAIN, main, 0.0))
    own_tokens_ref[...] = own.T.astype(BF16)

    gain = gain_ref[...][None, :]
    gain_scratch[:, :width] = gain
    gain_scratch[:, width:] = jnp.zeros((1, gain_scratch.shape[1] - width), F32)
    main = gain_scratch[:, pl.ds(pl.multiple_of(member * CHUNK, 128), CHUNK)]
    tail = jnp.concatenate(
        [gain[:, first:first + size] for first, size in tails] + [jnp.zeros((1, spare), F32)], axis=1
    )
    feature = lax.broadcasted_iota(jnp.int32, main.shape, 1)
    own_gain_ref[...] = jnp.where(is_last, tail, jnp.where(feature < MAIN, main, 0.0))


def prepare(experts, slots, member, ids, weights, tokens, gain):
    width, rows = tokens.shape
    return pl.pallas_call(
        functools.partial(prepare_kernel, experts, slots),
        out_shape=[
            shape((experts * slots, rows)),
            shape((3 * rows, experts * slots)),
            shape((rows, CHUNK)),
            shape((1, CHUNK), F32),
        ],
        in_specs=[SMEM] + [VMEM] * 4,
        out_specs=[VMEM] * 4,
        scratch_shapes=[pltpu.VMEM((1, (width // CHUNK + 1) * CHUNK), F32)],
        compiler_params=pltpu.CompilerParams(vmem_limit_bytes=24 * 1024 * 1024),
    )(member.reshape(1), ids, weights, tokens, gain)


def attend(pos_ref, query_ref, kv_refs, carry, diagonal=False):
    rows = kv_refs[0].shape[1] - EXTRA
    mine = pos_ref[0].astype(F32)
    key_side = lax.broadcasted_iota(jnp.int32, (rows, 2 * HEAD_WIDTH), 1) < HEAD_WIDTH
    flag_lane = lax.broadcasted_iota(jnp.int32, (rows, 2 * HEAD_WIDTH), 1) == HEAD_WIDTH
    top, mixed = carry
    for _ in range(1):
        keys = []
        vals = []
        for kv_ref, block in [(ref, i) for ref in kv_refs for i in range(ref.shape[0])]:
            marks = kv_ref[block, rows:rows + EXTRA, :].astype(F32)
            base = marks[0:1, 0:1] * 128.0 + marks[0:1, 1:2]
            hidden = jnp.where(base <= mine, 0.0, -1e30)
            kv = kv_ref[block, :rows, :].astype(F32)
            keys.append(jnp.where(key_side, kv, jnp.where(flag_lane, hidden, 0.0)).astype(BF16))
            vals.append(jnp.where(key_side, 1.0, kv).astype(BF16))
        keys = jnp.concatenate(keys, axis=0)
        vals = jnp.concatenate(vals, axis=0)
        scores = dot(query_ref[...], keys, ((1,), (1,)))
        if diagonal:
            own = scores[:, :rows]
            query_row = lax.broadcasted_iota(jnp.int32, own.shape, 0) % rows
            key_row = lax.broadcasted_iota(jnp.int32, own.shape, 1)
            own = jnp.where(key_row <= query_row, own, -1e30)
            scores = jnp.concatenate([own, scores[:, rows:]], axis=1)
        top_new = jnp.maximum(top, jnp.max(scores, axis=1, keepdims=True))
        probs = jnp.exp(scores - top_new).astype(BF16)
        mixed = mixed * jnp.exp(top - top_new) + dot(probs, vals)
        top = top_new
    return top, mixed


def first_attention_kernel(pos_ref, sink_ref, query_ref, *refs):
    *kv_refs, top_ref, mixed_ref = refs
    columns = query_ref.shape[0]
    heads = sink_ref.shape[0]
    top = jnp.concatenate(
        [jnp.full((columns // heads, 1), sink_ref[head], F32) for head in range(heads)], axis=0
    )
    lane = lax.broadcasted_iota(jnp.int32, (columns, 2 * HEAD_WIDTH), 1)
    start = (top, jnp.where(lane < HEAD_WIDTH, 1.0, 0.0))
    top_ref[...], mixed_ref[...] = attend(pos_ref, query_ref, kv_refs, start, True)


def middle_attention_kernel(pos_ref, query_ref, old_top_ref, old_mixed_ref, *refs):
    *kv_refs, top_ref, mixed_ref = refs
    carry = (old_top_ref[...], old_mixed_ref[...])
    top_ref[...], mixed_ref[...] = attend(pos_ref, query_ref, kv_refs, carry)


def last_attention_kernel(pos_ref, query_ref, old_top_ref, old_mixed_ref, w_ref, *refs):
    *kv_refs, out_ref = refs
    width = w_ref.shape[0]
    columns = query_ref.shape[0]
    rows = out_ref.shape[1]
    _, mixed = attend(pos_ref, query_ref, kv_refs, (old_top_ref[...], old_mixed_ref[...]))
    heads = (mixed[:, HEAD_WIDTH:] / mixed[:, :HEAD_WIDTH]).astype(BF16)
    stacked = jnp.concatenate(
        [heads[head * rows:(head + 1) * rows] for head in range(columns // rows)], axis=1
    )
    full = width // CHUNK
    for place in range(full):
        part = dot(stacked, w_ref[place * CHUNK:(place + 1) * CHUNK, :], ((1,), (1,)))
        out_ref[place] = part.astype(BF16)
    tail = jnp.concatenate(
        [w_ref[first:first + size, :] for first, size in tail_spans(width)], axis=0
    )
    out_ref[full] = jnp.zeros((rows, CHUNK), BF16)
    out_ref[full, :, :tail.shape[0]] = dot(stacked, tail, ((1,), (1,))).astype(BF16)


def dispatch_kernel(
    parts_ref, tokens_ref, gain_ref, gather_ref, attended_ref, residual_ref, out_ref
):
    total = parts_ref[0].astype(F32)
    for index in range(1, parts_ref.shape[0]):
        total = total + parts_ref[index].astype(F32)
    lane = lax.broadcasted_iota(jnp.int32, total.shape, 1)
    attended = jnp.where(lane < MAIN, total, 0.0).astype(BF16)
    attended_ref[...] = attended
    residual = tokens_ref[...].astype(F32) + attended.astype(F32)
    residual_ref[...] = residual
    left = jnp.sum(residual * residual, axis=1, keepdims=True)
    moe_in = residual * gain_ref[...]
    for place in range(3):
        rounded = left.astype(BF16).astype(F32)
        moe_in = jnp.where(lane == MAIN + place, rounded, moe_in)
        left = left - rounded
    out_ref[...] = dot(gather_ref[...], moe_in.astype(BF16)).astype(BF16)


def expert_kernel(width, counts, rows_in_ref, *refs):
    *weights, out_ref, rows_ref = refs
    full = width // CHUNK
    split = CHUNK - 128
    count = rows_in_ref.shape[1]
    main_lane = lax.broadcasted_iota(jnp.int32, (count, 128), 1) < MAIN - split
    squares = jnp.zeros((count, 128), F32)
    for place in range(full + 1):
        last = rows_in_ref[place, :, split:].astype(F32)
        squares = squares + jnp.where(main_lane, 0.0, last)
        if place < full:
            first = place * CHUNK
            rows_ref[:, first:first + split] = rows_in_ref[place, :, :split]
            rows_ref[:, first + split:first + CHUNK] = jnp.where(main_lane, last, 0.0).astype(BF16)
    squares = jnp.sum(squares, axis=1, keepdims=True)
    scale = lax.rsqrt(squares / width + EPSILON)
    tails = tail_spans(width)
    tail_width = sum(size for _, size in tails)
    tail_rows = rows_in_ref[full, :, :tail_width]

    def columns(refs_in, first, size):
        start = 0
        for ref in refs_in:
            if start <= first < start + ref.shape[1]:
                return ref[:, first - start:first - start + size]
            start += ref.shape[1]

    def tail(refs_in):
        return jnp.concatenate([columns(refs_in, *span) for span in tails], axis=1)

    def product(ref):
        main = dot(rows_ref[...], ref[:, :full * CHUNK], ((1,), (1,)))
        return (main + dot(tail_rows, tail([ref]), ((1,), (1,)))) * scale

    hidden = []
    downs = []
    at = 0
    for number in counts:
        gate = product(weights[at])
        up = product(weights[at + 1])
        hidden.append((gate * jax.nn.sigmoid(1.702 * gate) * (up + 1.0)).astype(BF16))
        downs.append(weights[at + 2:at + number])
        at += number
    for place in range(full):
        part = 0.0
        for act, down in zip(hidden, downs):
            part = part + dot(act, columns(down, place * CHUNK, CHUNK))
        out_ref[place] = part.astype(BF16)
    part = 0.0
    for act, down in zip(hidden, downs):
        part = part + dot(act, tail(down))
    out_ref[full] = jnp.zeros(out_ref.shape[1:], BF16)
    out_ref[full, :, :tail_width] = part.astype(BF16)


def run_experts(width, expert_rows, sets):
    weights = [w for one in sets for w in one]
    count, rows, _ = expert_rows.shape
    return pl.pallas_call(
        functools.partial(expert_kernel, width, [len(one) for one in sets]),
        out_shape=shape(expert_rows.shape),
        in_specs=[VMEM] * (1 + len(weights)),
        out_specs=VMEM,
        scratch_shapes=[pltpu.VMEM((rows, width // CHUNK * CHUNK), BF16)],
        compiler_params=pltpu.CompilerParams(vmem_limit_bytes=24 * 1024 * 1024),
    )(expert_rows, *weights)


def sum_kernel(groups, parts_ref, out_ref):
    for half, members in enumerate(groups):
        total = parts_ref[members[0]].astype(F32)
        for index in members[1:]:
            total = total + parts_ref[index].astype(F32)
        out_ref[half] = total.astype(BF16)


def combine_kernel(returned_ref, combine_ref, residual_ref, attended_ref, out_ref):
    rows = residual_ref.shape[0]
    mixed = dot(combine_ref[...], returned_ref[...])
    total = mixed[:rows] + mixed[rows:2 * rows] + mixed[2 * rows:]
    out_ref[:, :CHUNK] = attended_ref[...]
    out_ref[:, CHUNK:] = (residual_ref[...] + total).astype(BF16)


def finish_kernel(parts_ref, attended_ref, layer_ref):
    width = attended_ref.shape[1]
    full = width // CHUNK
    for out_ref, at in ((attended_ref, 0), (layer_ref, CHUNK)):
        last = parts_ref[full, :, at:at + CHUNK].astype(F32)
        rest = width - full * CHUNK
        for place in range(full):
            start = rest + place * TAIL
            main = parts_ref[place, :, at:at + MAIN].astype(F32)
            whole = jnp.concatenate([main, last[:, start:start + TAIL]], axis=1)
            out_ref[:, place * CHUNK:(place + 1) * CHUNK] = whole.astype(BF16)
        out_ref[:, full * CHUNK:] = last[:, :rest].astype(BF16)


def exchange(block, axis, groups=None):
    return lax.all_to_all(
        block, axis, split_axis=0, concat_axis=0, tiled=True, axis_index_groups=groups
    )


def local(
    tokens,
    positions,
    norm_attn,
    norm_moe,
    w_query,
    key_matrix,
    value_matrix,
    w_out,
    sinks,
    expert_ids,
    expert_weights,
    w_gate,
    w_up,
    w_down,
):
    ctx_count = lax.axis_size("ctx")
    exp_count = lax.axis_size("exp")
    rows, width = tokens.shape
    heads = sinks.shape[0]
    top = expert_ids.shape[1]
    experts = ctx_count
    slots = rows * top * 3 // (2 * experts)
    member = lax.axis_index("exp")

    swap = [(i, i ^ 2) for i in range(exp_count)]
    gate, up, down = w_gate[0].T, w_up[0].T, w_down[0]

    normed, payload = project_kv(
        positions, tokens.T, norm_attn, key_matrix.T, value_matrix.T
    )
    far_gate = lax.ppermute(gate, "exp", swap)

    def moved(block, x, z, core):
        route = []
        for i in range(ctx_count):
            there = (i // 8 + x) % 4 * 8 + (i // 2 % 4 + z) % 4 * 2 + (i % 2 + core) % 2
            route.append((i, there))
        return lax.ppermute(block, "ctx", route)

    queries = call(query_kernel, shape((heads * rows, 2 * HEAD_WIDTH)), [VMEM, VMEM])(normed, w_query)
    stops = [moved(payload, 0, z, 0) for z in range(1, 4)]
    *stops, queries = lax.optimization_barrier((*stops, queries))
    column = jnp.stack([payload] + stops)
    column_far = moved(column, 0, 0, 1)
    planes = [moved(column, x, 0, 0) for x in range(1, 4)]
    state = [shape((heads * rows, 1), F32), shape((heads * rows, 2 * HEAD_WIDTH), F32)]
    carried = call(first_attention_kernel, state, [SMEM, SMEM] + [VMEM] * 3)(
        positions, sinks, queries, column, column_far
    )
    prepared = prepare(
        experts, slots, member, expert_ids.T, expert_weights.T, tokens.T, norm_moe
    )
    *planes, top_row, mixed, gather_table, combine_table, own_tokens, own_gain = (
        lax.optimization_barrier((*planes, *carried, *prepared))
    )
    planes_far = [moved(plane, 0, 0, 1) for plane in planes]
    carried = call(middle_attention_kernel, state, [SMEM] + [VMEM] * 6)(
        positions, queries, top_row, mixed, *planes
    )
    top_row, mixed, far_gate = lax.optimization_barrier((*carried, far_gate))
    far_up = lax.ppermute(up, "exp", swap)
    partial_sums = call(
        last_attention_kernel, shape((exp_count, rows, CHUNK)), [SMEM] + [VMEM] * 7
    )(positions, queries, top_row, mixed, w_out.T, *planes_far)
    partial_sums, far_up = lax.optimization_barrier((partial_sums, far_up))
    parts = exchange(partial_sums, "exp")
    parts, down = lax.optimization_barrier((parts, down))
    attended, residual, outgoing = call(
        dispatch_kernel,
        [shape((rows, CHUNK)), shape((rows, CHUNK), F32), shape((experts * slots, CHUNK))],
        [VMEM] * 4,
    )(parts, own_tokens, own_gain, gather_table)
    arrived = exchange(outgoing.reshape(ctx_count, slots, CHUNK), "ctx")
    far_down = lax.ppermute(down, "exp", swap)
    arrived, far_down = lax.optimization_barrier((arrived, far_down))
    halves = arrived.reshape(1, 2, 1, ctx_count * slots // 2, CHUNK)
    spread = jnp.broadcast_to(halves, (exp_count // 4, 2, 2) + halves.shape[3:])
    expert_rows = exchange(spread.reshape((exp_count,) + halves.shape[3:]), "exp")
    sets = [(gate, up, down), (far_gate, far_up, far_down)]
    products = run_experts(width, expert_rows, sets)
    product_parts = exchange(products, "exp")
    groups = [[i for i in range(exp_count) if (i >> 1) & 1 == half] for half in range(2)]
    summed = call(
        functools.partial(sum_kernel, groups),
        shape((2, ctx_count * slots // 2, CHUNK)),
        [VMEM],
    )(product_parts)
    returned = exchange(summed.reshape(ctx_count, slots, CHUNK), "ctx")
    final = call(combine_kernel, shape((rows, 2 * CHUNK)), [VMEM] * 4)(
        returned.reshape(experts * slots, CHUNK), combine_table, residual, attended
    )
    final = exchange(final.reshape(exp_count, rows // exp_count, 2 * CHUNK), "exp")
    out = shape((rows // exp_count, width))
    return tuple(call(finish_kernel, [out, out], [VMEM])(final))


def solution(mesh):
    in_specs = (
        P("ctx", None),
        P("ctx"),
        P(),
        P(),
        P(None, "exp"),
        P(None, "exp"),
        P(None, "exp"),
        P("exp", None),
        P("exp"),
        P("ctx", None),
        P("ctx", None),
        P("ctx", None, "exp"),
        P("ctx", None, "exp"),
        P("ctx", "exp", None),
    )
    out_specs = (P(("ctx", "exp"), None), P(("ctx", "exp"), None))
    return jax.shard_map(local, mesh=mesh, in_specs=in_specs, out_specs=out_specs, check_vma=False)
```

time: 307 us -> 216 us (0.70)
  waiting for transfers between devices: 123 us -> 31.4 us
  local copies, waits for them, and re-layouts: 29.2 us -> 5.59 us
  blocking collectives: 95.9 us -> 119 us
    ppermute x3 -> x13, waiting for transfers between devices: 85 us -> 31.4 us  [the longest x1 25.3 us: local(): far_down = lax.ppermute(down, 'exp', swap)]
    all_to_all x4 -> x1, waiting for transfers between devices: 37.7 us -> 0.01 us  [exchange(): lax.all_to_all(block, axis, split_axis=0, concat_axis=0, tiled=True, axis...]
    all_to_all x4 -> x5, blocking collectives: 95.9 us -> 119 us  [exchange(): lax.all_to_all(block, axis, split_axis=0, concat_axis=0, tiled=True, axis...]
    ppermute x3 -> x13, starting transfers between devices: 2.8 us -> 19.2 us  [the longest x10 16.8 us: moved(): return lax.ppermute(block, 'ctx', route)]
    unnamed x43 -> x30, local copies, waits for them, and re-layouts: 20.4 us -> 5.38 us
    all_to_all x4 -> x1, starting transfers between devices: 27.8 us -> 12.9 us  [exchange(): lax.all_to_all(block, axis, split_axis=0, concat_axis=0, tiled=True, axis...]
    ppermute x2 -> x0, local copies, waits for them, and re-layouts: 5.05 us -> none  [local(): other = tuple((lax.ppermute(w, 'exp', swap) for w in own))]
    pallas_call x8 -> x9, Pallas kernels: 25.7 us -> 25.2 us  [the longest x1 6.29 us: run_experts(): pl.pallas_call(functools.partial(expert_kernel, width, [len(one) for one...]
  transfers between devices with their start and end apart: 7 -> 14, of which waited for: 6 -> 4; matrix products, arithmetic and copies ran while one was open for 4% -> 0% of each run, Pallas kernels for 0% -> 8%
where the time goes in v2:
time: 216 us
  blocking collectives  119 us (55%)
  starting transfers between devices  32.1 us (15%)
  waiting for transfers between devices  31.4 us (15%)
  Pallas kernels  26.4 us (12%)
  local copies, waits for them, and re-layouts  5.59 us (3%)
    all_to_all x5, blocking collectives, exchange(): lax.all_to_all(block, axis, split_axis=0, concat_axis=0, tiled=True, axis...  119 us
    ppermute x1, waiting for transfers between devices, local(): far_down = lax.ppermute(down, 'exp', swap)  25.3 us
    ppermute x10, starting transfers between devices, moved(): return lax.ppermute(block, 'ctx', route)  16.8 us
    all_to_all x1, starting transfers between devices, exchange(): lax.all_to_all(block, axis, split_axis=0, concat_axis=0, tiled=True, axis...  12.9 us
    pallas_call x1, Pallas kernels, run_experts(): pl.pallas_call(functools.partial(expert_kernel, width, [len(one) for one...  6.29 us
    unnamed x30, local copies, waits for them, and re-layouts  5.38 us
    pallas_call x1, Pallas kernels, local(): call(last_attention_kernel, shape((exp_count, rows, CHUNK)), [SMEM] + [VM...  4.84 us
  transfers between devices with their start and end apart: 14, of which 4 were waited for; matrix products, arithmetic and copies ran while one was open for 0% of the time, Pallas kernels for 8%

profile of v2, /device:TPU:1, one launch (start us, length us, event | category | flops | bytes accessed | tf_op | source)
XLA Modules:
  0.0 215.5 jit_solution(11936844272525830801)
XLA Ops:
  0.6 2.2 %collective-permute-start.7 = (bf16[180,2880]{1,0:T(8,128)(2,1)}, bf16[180,2880]{1,0:T(8,128)(2,1)}, u32[]{:S(2)}, u32[]{:S(2)}) collective-permute-start(bf16[180,2880]{1,0:T(8,128)(2,1)} %bitcast.29), channel_id=1, source_target_pairs={{0,2},{1,3},{2,0},{3,1},{4,6},{5,7},{6,4},{7,5},{8,10},{9,11},{10,... | collective-permute-start | bytes 3110408 | tf_op jit(solution)/shard_map/ppermute | solution.py:426
  3.0 3.6 %shard_map.149 = (bf16[128,2880]{1,0:T(8,128)(2,1)S(1)}, bf16[144,128]{1,0:T(8,128)(2,1)S(1)}) custom-call(s32[128]{0:T(128)} %pos_ref.7, bf16[2880,128]{1,0:T(8,128)(2,1)} %bitcast.25, f32[2880]{0:T(1024)} %gain_hbm.1, bf16[64,2880]{1,0:T(8,128)(2,1)} %bitcast.41, bf16[64,2880]{1,0:T(8,128)(2,1)} %bitcast.42), custom_call_target="tpu_custom_call" | custom-call | tf_op jit(solution)/shard_map/pallas_call | solution.py:95
  6.6 6.2 %collective-permute-start.2 = (bf16[144,128]{1,0:T(8,128)(2,1)S(1)}, bf16[144,128]{1,0:T(8,128)(2,1)S(1)}, u32[]{:S(2)}, u32[]{:S(2)}) collective-permute-start(bf16[144,128]{1,0:T(8,128)(2,1)S(1)} %get-tuple-element.37), channel_id=1, source_target_pairs={{0,48},{8,56},{16,0},{24,8},{32,16},{40,24},{48,32},{56,40},{64,11... | collective-permute-start | bytes 110600 | tf_op jit(solution)/shard_map/ppermute | solution.py:433
  12.7 1.0 collective-permute-start.1
  13.7 2.3 %collective-permute-start = (bf16[144,128]{1,0:T(8,128)(2,1)S(1)}, bf16[144,128]{1,0:T(8,128)(2,1)S(1)}, u32[]{:S(2)}, u32[]{:S(2)}) collective-permute-start(bf16[144,128]{1,0:T(8,128)(2,1)S(1)} %get-tuple-element.37), channel_id=1, source_target_pairs={{0,16},{8,24},{16,32},{24,40},{32,48},{40,56},{48,0},{56,8},{64,80... | collective-permute-start | bytes 110600 | tf_op jit(solution)/shard_map/ppermute | solution.py:433
  16.0 1.8 copy-done
  18.5 0.9 collective-permute-done.1
  19.5 2.8 %collective-permute-start.6 = (bf16[4,144,128]{2,1,0:T(8,128)(2,1)S(1)}, bf16[4,144,128]{2,1,0:T(8,128)(2,1)S(1)}, u32[]{:S(2)}, u32[]{:S(2)}) collective-permute-start(bf16[4,144,128]{2,1,0:T(8,128)(2,1)S(1)} %pad_maximum_fusion.refs_0_), channel_id=1, source_target_pairs={{0,8},{8,0},{16,24},{24,16},{32,40},{40,32},{48,56},{56,48},{64,72... | collective-permute-start | bytes 442376 | tf_op jit(solution)/shard_map/ppermute | solution.py:433
  22.2 2.5 %collective-permute-start.5 = (bf16[4,144,128]{2,1,0:T(8,128)(2,1)S(1)}, bf16[4,144,128]{2,1,0:T(8,128)(2,1)S(1)}, u32[]{:S(2)}, u32[]{:S(2)}) collective-permute-start(bf16[4,144,128]{2,1,0:T(8,128)(2,1)S(1)} %pad_maximum_fusion.refs_0_), channel_id=1, source_target_pairs={{0,192},{8,200},{16,208},{24,216},{32,224},{40,232},{48,240},{56,2... | collective-permute-start | bytes 442376 | tf_op jit(solution)/shard_map/ppermute | solution.py:433
  26.5 1.1 copy-done.2
  30.2 3.1 %shard_map.151 = (f32[1024,1]{1,0:T(8,128)S(1)}, f32[1024,128]{1,0:T(8,128)S(1)}) custom-call(s32[128]{0:T(128)S(1)} %copy-done.11, f32[8]{0:T(128)S(1)} %copy-done.14, bf16[1024,128]{1,0:T(8,128)(2,1)S(1)} %shard_map.150.query_ref, bf16[4,144,128]{2,1,0:T(8,128)(2,1)S(1)} %pad_maximum_fusion.refs_0_, bf16[4,144,128]{2,1,0:T(8,128)(2,1)S(1)} %copy-done.9), custom_call_target="tpu_custom_call" | custom-call | tf_op jit(solution)/shard_map/pallas_call | solution.py:442
  33.4 1.9 collective-permute-done.3.refs_0_
  36.3 4.3 %shard_map.153 = (f32[1024,1]{1,0:T(8,128)S(1)}, f32[1024,128]{1,0:T(8,128)S(1)}) custom-call(s32[128]{0:T(128)S(1)} %copy-done.11, bf16[1024,128]{1,0:T(8,128)(2,1)S(1)} %shard_map.150.query_ref, f32[1024,1]{1,0:T(8,128)S(1)} %get-tuple-element.49.old_top_ref, f32[1024,128]{1,0:T(8,128)S(1)} %get-tuple-element.50.old_mixed_ref, ...), custom_call_target="tpu_custom_call" | custom-call | tf_op jit(solution)/shard_map/pallas_call | solution.py:452
  40.6 4.8 %shard_map.154 = bf16[8,128,384]{2,1,0:T(8,128)(2,1)S(1)} custom-call(s32[128]{0:T(128)S(1)} %copy-done.11, bf16[1024,128]{1,0:T(8,128)(2,1)S(1)} %shard_map.150.query_ref, f32[1024,1]{1,0:T(8,128)S(1)} %get-tuple-element.56.old_top_ref, f32[1024,128]{1,0:T(8,128)S(1)} %get-tuple-element.57.old_mixed_ref, bf16[2880,512]{1,0:T(8,128)(2,1)S(1)} %bitcast.24, ...), custom_call_target="tpu_custom_call" | custom-call | tf_op jit(solution)/shard_map/pallas_call | solution.py:457
  45.5 3.3 %collective-permute-done.11.refs_4_ = bf16[180,2880]{1,0:T(8,128)(2,1)} collective-permute-done((bf16[180,2880]{1,0:T(8,128)(2,1)}, bf16[180,2880]{1,0:T(8,128)(2,1)}, u32[]{:S(2)}, u32[]{:S(2)}) %collective-permute-start.11) | collective-permute-done | bytes 1036832 | tf_op jit(solution)/shard_map/ppermute | solution.py:456
  48.8 17.5 %all_to_all.30.parts_ref = bf16[8,128,384]{2,1,0:T(8,128)(2,1)S(1)} all-to-all(bf16[8,128,384]{2,1,0:T(8,128)(2,1)S(1)} %shard_map.154), channel_id=1, replica_groups=mesh['ctx'=32,'exp'=8] {'exp'}, dimensions={0} | all-to-all | bytes 1572864 | tf_op jit(solution)/shard_map/all_to_all | solution.py:390
  66.3 1.3 shard_map.155
  67.6 12.9 %all-to-all-start.1 = ((bf16[32,24,384]{2,1,0:T(8,128)(2,1)}), bf16[32,24,384]{2,1,0:T(8,128)(2,1)S(1)}, u32[]{:S(2)}, u32[]{:S(2)}) async-start(bf16[32,24,384]{2,1,0:T(8,128)(2,1)} %bitcast.16), calls=%async_computation.1 | async-start | bytes 1179648 | tf_op jit(solution)/shard_map/all_to_all | solution.py:390
  80.6 25.3 %collective-permute-done.12.refs_5_ = bf16[180,2880]{1,0:T(8,128)(2,1)S(1)} collective-permute-done((bf16[180,2880]{1,0:T(8,128)(2,1)S(1)}, bf16[180,2880]{1,0:T(8,128)(2,1)S(1)}, u32[]{:S(2)}, u32[]{:S(2)}) %collective-permute-start.12) | collective-permute-done | bytes 1036832 | tf_op jit(solution)/shard_map/ppermute | solution.py:469
  106.1 31.2 %all_to_all.31.rows_in_ref = bf16[8,384,384]{2,1,0:T(8,128)(2,1)S(1)} all-to-all(bf16[8,384,384]{2,1,0:T(8,128)(2,1)S(1)} %bitcast.39), channel_id=1, replica_groups=mesh['ctx'=32,'exp'=8] {'exp'}, dimensions={0} | all-to-all | bytes 4718592 | tf_op jit(solution)/shard_map/all_to_all | solution.py:390
  137.3 6.3 %shard_map.156 = bf16[8,384,384]{2,1,0:T(8,128)(2,1)S(1)} custom-call(bf16[8,384,384]{2,1,0:T(8,128)(2,1)S(1)} %all_to_all.31.rows_in_ref, bf16[180,2880]{1,0:T(8,128)(2,1)S(1)} %bitcast.30, bf16[180,2880]{1,0:T(8,128)(2,1)S(1)} %bitcast.32, bf16[180,2880]{1,0:T(8,128)(2,1)S(1)} %bitcast.34, bf16[180,2880]{1,0:T(8,128)(2,1)} %collective-permute-done.7.refs_3_, ...), custom_call_target="tpu_custom_call" | custom-call | tf_op jit(solution)/shard_map/pallas_call | solution.py:349
  143.6 30.4 %all_to_all.32.parts_ref = bf16[8,384,384]{2,1,0:T(8,128)(2,1)S(1)} all-to-all(bf16[8,384,384]{2,1,0:T(8,128)(2,1)S(1)} %shard_map.156), channel_id=1, replica_groups=mesh['ctx'=32,'exp'=8] {'exp'}, dimensions={0} | all-to-all | bytes 4718592 | tf_op jit(solution)/shard_map/all_to_all | solution.py:390
  174.3 31.4 %all_to_all.33 = bf16[32,24,384]{2,1,0:T(8,128)(2,1)S(1)} all-to-all(bf16[32,24,384]{2,1,0:T(8,128)(2,1)S(1)} %bitcast.28), channel_id=1, replica_groups=mesh['ctx'=32,'exp'=8] {'ctx'}, dimensions={0} | all-to-all | bytes 1179648 | tf_op jit(solution)/shard_map/all_to_all | solution.py:390
  206.2 8.6 %all_to_all.34.parts_ref = bf16[8,16,768]{2,1,0:T(8,128)(2,1)S(1)} all-to-all(bf16[8,16,768]{2,1,0:T(8,128)(2,1)S(1)} %bitcast.35), channel_id=1, replica_groups=mesh['ctx'=32,'exp'=8] {'exp'}, dimensions={0} | all-to-all | bytes 393216 | tf_op jit(solution)/shard_map/all_to_all | solution.py:390
  (52 shorter events, 8.0 us)
Async XLA Ops:
  0.6 39.9 %collective-permute-start.7 = (bf16[180,2880]{1,0:T(8,128)(2,1)}, bf16[180,2880]{1,0:T(8,128)(2,1)}, u32[]{:S(2)}, u32[]{:S(2)}) collective-permute-start(bf16[180,2880]{1,0:T(8,128)(2,1)} %bitcast.29), channel_id=1, source_target_pairs={{0,2},{1,3},{2,0},{3,1},{4,6},{5,7},{6,4},{7,5},{8,10},{9,11},{10,... | collective-permute-start | bytes 3110408 | tf_op jit(solution)/shard_map/ppermute | solution.py:426
  2.8 45.9 %collective-permute-start.11 = (bf16[180,2880]{1,0:T(8,128)(2,1)}, bf16[180,2880]{1,0:T(8,128)(2,1)}, u32[]{:S(2)}, u32[]{:S(2)}) collective-permute-start(bf16[180,2880]{1,0:T(8,128)(2,1)} %bitcast.31), channel_id=1, source_target_pairs={{0,2},{1,3},{2,0},{3,1},{4,6},{5,7},{6,4},{7,5},{8,10},{9,11},{10,... | collective-permute-start | bytes 3110408 | tf_op jit(solution)/shard_map/ppermute | solution.py:456
  2.9 23.6 %copy-start.10 = (f32[2880]{0:T(1024)S(1)}, f32[2880]{0:T(1024)}, u32[]{:S(2)}) copy-start(f32[2880]{0:T(1024)} %gain_ref.1) | copy-start | bytes 34564
  3.0 23.6 %copy-start.13 = (f32[128,4]{0,1:T(4,128)S(1)}, f32[128,4]{0,1:T(4,128)}, u32[]{:S(2)}) copy-start(f32[128,4]{0,1:T(4,128)} %param.24) | copy-start | bytes 6148
  6.5 20.0 %copy-start.12 = (s32[128,4]{0,1:T(4,128)S(1)}, s32[128,4]{0,1:T(4,128)}, u32[]{:S(2)}) copy-start(s32[128,4]{0,1:T(4,128)} %param.23) | copy-start | bytes 6148
  6.6 11.9 %collective-permute-start.2 = (bf16[144,128]{1,0:T(8,128)(2,1)S(1)}, bf16[144,128]{1,0:T(8,128)(2,1)S(1)}, u32[]{:S(2)}, u32[]{:S(2)}) collective-permute-start(bf16[144,128]{1,0:T(8,128)(2,1)S(1)} %get-tuple-element.37), channel_id=1, source_target_pairs={{0,48},{8,56},{16,0},{24,8},{32,16},{40,24},{48,32},{56,40},{64,11... | collective-permute-start | bytes 110600 | tf_op jit(solution)/shard_map/ppermute | solution.py:433
  12.7 6.7 %collective-permute-start.1 = (bf16[144,128]{1,0:T(8,128)(2,1)S(1)}, bf16[144,128]{1,0:T(8,128)(2,1)S(1)}, u32[]{:S(2)}, u32[]{:S(2)}) collective-permute-start(bf16[144,128]{1,0:T(8,128)(2,1)S(1)} %get-tuple-element.37), channel_id=1, source_target_pairs={{0,32},{8,40},{16,48},{24,56},{32,0},{40,8},{48,16},{56,24},{64,96... | collective-permute-start | bytes 110600 | tf_op jit(solution)/shard_map/ppermute | solution.py:433
  13.7 5.7 %collective-permute-start = (bf16[144,128]{1,0:T(8,128)(2,1)S(1)}, bf16[144,128]{1,0:T(8,128)(2,1)S(1)}, u32[]{:S(2)}, u32[]{:S(2)}) collective-permute-start(bf16[144,128]{1,0:T(8,128)(2,1)S(1)} %get-tuple-element.37), channel_id=1, source_target_pairs={{0,16},{8,24},{16,32},{24,40},{32,48},{40,56},{48,0},{56,8},{64,80... | collective-permute-start | bytes 110600 | tf_op jit(solution)/shard_map/ppermute | solution.py:433
  17.8 11.5 %copy-start.11 = (s32[128]{0:T(128)S(1)}, s32[128]{0:T(128)}, u32[]{:S(2)}) copy-start(s32[128]{0:T(128)} %pos_ref.7) | copy-start | bytes 1540
  17.8 11.5 %copy-start.14 = (f32[8]{0:T(128)S(1)}, f32[8]{0:T(128)}, u32[]{:S(2)}) copy-start(f32[8]{0:T(128)} %sink_ref.1) | copy-start | bytes 100
  18.5 22.1 %copy-start.1 = (bf16[512,2880]{0,1:T(8,128)(2,1)S(1)}, bf16[512,2880]{0,1:T(8,128)(2,1)}, u32[]{:S(2)}) copy-start(bf16[512,2880]{0,1:T(8,128)(2,1)} %param.21) | copy-start | bytes 8847364
  19.5 5.8 %collective-permute-start.6 = (bf16[4,144,128]{2,1,0:T(8,128)(2,1)S(1)}, bf16[4,144,128]{2,1,0:T(8,128)(2,1)S(1)}, u32[]{:S(2)}, u32[]{:S(2)}) collective-permute-start(bf16[4,144,128]{2,1,0:T(8,128)(2,1)S(1)} %pad_maximum_fusion.refs_0_), channel_id=1, source_target_pairs={{0,8},{8,0},{16,24},{24,16},{32,40},{40,32},{48,56},{56,48},{64,72... | collective-permute-start | bytes 442376 | tf_op jit(solution)/shard_map/ppermute | solution.py:433
  22.2 11.1 %collective-permute-start.5 = (bf16[4,144,128]{2,1,0:T(8,128)(2,1)S(1)}, bf16[4,144,128]{2,1,0:T(8,128)(2,1)S(1)}, u32[]{:S(2)}, u32[]{:S(2)}) collective-permute-start(bf16[4,144,128]{2,1,0:T(8,128)(2,1)S(1)} %pad_maximum_fusion.refs_0_), channel_id=1, source_target_pairs={{0,192},{8,200},{16,208},{24,216},{32,224},{40,232},{48,240},{56,2... | collective-permute-start | bytes 442376 | tf_op jit(solution)/shard_map/ppermute | solution.py:433
  24.7 8.6 %collective-permute-start.4 = (bf16[4,144,128]{2,1,0:T(8,128)(2,1)S(1)}, bf16[4,144,128]{2,1,0:T(8,128)(2,1)}, u32[]{:S(2)}, u32[]{:S(2)}) collective-permute-start(bf16[4,144,128]{2,1,0:T(8,128)(2,1)S(1)} %pad_maximum_fusion.refs_0_), channel_id=1, source_target_pairs={{0,128},{8,136},{16,144},{24,152},{32,160},{40,168},{48,176},{56,1... | collective-permute-start | bytes 442376 | tf_op jit(solution)/shard_map/ppermute | solution.py:433
  25.9 9.4 %collective-permute-start.3 = (bf16[4,144,128]{2,1,0:T(8,128)(2,1)S(1)}, bf16[4,144,128]{2,1,0:T(8,128)(2,1)}, u32[]{:S(2)}, u32[]{:S(2)}) collective-permute-start(bf16[4,144,128]{2,1,0:T(8,128)(2,1)S(1)} %pad_maximum_fusion.refs_0_), channel_id=1, source_target_pairs={{0,64},{8,72},{16,80},{24,88},{32,96},{40,104},{48,112},{56,120},{... | collective-permute-start | bytes 442376 | tf_op jit(solution)/shard_map/ppermute | solution.py:433
  35.3 5.3 %collective-permute-start.8 = (bf16[4,144,128]{2,1,0:T(8,128)(2,1)}, bf16[4,144,128]{2,1,0:T(8,128)(2,1)S(1)}, u32[]{:S(2)}, u32[]{:S(2)}) collective-permute-start(bf16[4,144,128]{2,1,0:T(8,128)(2,1)} %collective-permute-done.3.refs_0_), channel_id=1, source_target_pairs={{0,8},{8,0},{16,24},{24,16},{32,40},{40,32},{48,56},{56,48},{64,72... | collective-permute-start | bytes 442376 | tf_op jit(solution)/shard_map/ppermute | solution.py:433
  35.8 4.8 %collective-permute-start.9 = (bf16[4,144,128]{2,1,0:T(8,128)(2,1)}, bf16[4,144,128]{2,1,0:T(8,128)(2,1)S(1)}, u32[]{:S(2)}, u32[]{:S(2)}) collective-permute-start(bf16[4,144,128]{2,1,0:T(8,128)(2,1)} %collective-permute-done.4.refs_1_), channel_id=1, source_target_pairs={{0,8},{8,0},{16,24},{24,16},{32,40},{40,32},{48,56},{56,48},{64,72... | collective-permute-start | bytes 442376 | tf_op jit(solution)/shard_map/ppermute | solution.py:433
  35.8 4.8 %collective-permute-start.10 = (bf16[4,144,128]{2,1,0:T(8,128)(2,1)S(1)}, bf16[4,144,128]{2,1,0:T(8,128)(2,1)S(1)}, u32[]{:S(2)}, u32[]{:S(2)}) collective-permute-start(bf16[4,144,128]{2,1,0:T(8,128)(2,1)S(1)} %collective-permute-done.5.refs_2_), channel_id=1, source_target_pairs={{0,8},{8,0},{16,24},{24,16},{32,40},{40,32},{48,56},{56,48},{64,72... | collective-permute-start | bytes 442376 | tf_op jit(solution)/shard_map/ppermute | solution.py:433
  45.5 35.0 %copy-start.5 = (bf16[1,180,2880]{2,1,0:T(8,128)(2,1)S(1)}, bf16[1,180,2880]{2,1,0:T(8,128)(2,1)}, u32[]{:S(2)}) copy-start(bf16[1,180,2880]{2,1,0:T(8,128)(2,1)} %param.27) | copy-start | bytes 3110404
  67.6 38.3 %all-to-all-start.1 = ((bf16[32,24,384]{2,1,0:T(8,128)(2,1)}), bf16[32,24,384]{2,1,0:T(8,128)(2,1)S(1)}, u32[]{:S(2)}, u32[]{:S(2)}) async-start(bf16[32,24,384]{2,1,0:T(8,128)(2,1)} %bitcast.16), calls=%async_computation.1 | async-start | bytes 1179648 | tf_op jit(solution)/shard_map/all_to_all | solution.py:390
  80.5 25.4 %collective-permute-start.12 = (bf16[180,2880]{1,0:T(8,128)(2,1)S(1)}, bf16[180,2880]{1,0:T(8,128)(2,1)S(1)}, u32[]{:S(2)}, u32[]{:S(2)}) collective-permute-start(bf16[180,2880]{1,0:T(8,128)(2,1)S(1)} %bitcast.33), channel_id=1, source_target_pairs={{0,2},{1,3},{2,0},{3,1},{4,6},{5,7},{6,4},{7,5},{8,10},{9,11},{10,... | collective-permute-start | bytes 3110408 | tf_op jit(solution)/shard_map/ppermute | solution.py:469
  106.1 31.3 %copy-start.3 = (bf16[1,2880,180]{1,2,0:T(8,128)(2,1)S(1)}, bf16[1,2880,180]{1,2,0:T(8,128)(2,1)}, u32[]{:S(2)}) copy-start(bf16[1,2880,180]{1,2,0:T(8,128)(2,1)} %param.25) | copy-start | bytes 3110404
  106.1 31.2 %copy-start.4 = (bf16[1,2880,180]{1,2,0:T(8,128)(2,1)S(1)}, bf16[1,2880,180]{1,2,0:T(8,128)(2,1)}, u32[]{:S(2)}) copy-start(bf16[1,2880,180]{1,2,0:T(8,128)(2,1)} %param.26) | copy-start | bytes 3110404
  174.0 31.7 %copy-start.7 = (bf16[384,768]{1,0:T(8,128)(2,1)S(1)}, bf16[384,768]{1,0:T(8,128)(2,1)}, u32[]{:S(2)}) copy-start(bf16[384,768]{1,0:T(8,128)(2,1)} %copy-done.6) | copy-start | bytes 1769476
  (5 other events, 5.3 us)

commit v3 on v2

--- a/solution.py
+++ b/solution.py
@@ -11,6 +11,7 @@
 EPSILON = 1e-05
 CHUNK = 384
 TAIL = 16
+LATE = 64
 MAIN = CHUNK - TAIL
 EXTRA = 16
 BF16 = jnp.bfloat16
@@ -288,8 +289,15 @@
     out_ref[...] = dot(gather_ref[...], moe_in.astype(BF16)).astype(BF16)
 
 
-def expert_kernel(width, counts, rows_in_ref, *refs):
-    *weights, out_ref, rows_ref = refs
+def expert_kernel(
+    width, rows_in_ref, gate_ref, up_ref, down_ref, far_gate_ref, far_up_ref, late_ref,
+    out_ref, rows_ref, held_ref,
+):
+    units = gate_ref.shape[0]
+    held_ref[:LATE, :] = late_ref[:LATE, :]
+    held_ref[LATE:, :] = far_up_ref[...]
+    own = (gate_ref, up_ref, down_ref)
+    far = (far_gate_ref, held_ref, late_ref.at[pl.ds(LATE, units)])
     full = width // CHUNK
     split = CHUNK - 128
     count = rows_in_ref.shape[1]
@@ -324,13 +332,11 @@
 
     hidden = []
     downs = []
-    at = 0
-    for number in counts:
-        gate = product(weights[at])
-        up = product(weights[at + 1])
+    for gate_ref, up_ref, down_ref in (own, far):
+        gate = product(gate_ref)
+        up = product(up_ref)
         hidden.append((gate * jax.nn.sigmoid(1.702 * gate) * (up + 1.0)).astype(BF16))
-        downs.append(weights[at + 2:at + number])
-        at += number
+        downs.append([down_ref])
     for place in range(full):
         part = 0.0
         for act, down in zip(hidden, downs):
@@ -343,17 +349,19 @@
     out_ref[full, :, :tail_width] = part.astype(BF16)
 
 
-def run_experts(width, expert_rows, sets):
-    weights = [w for one in sets for w in one]
-    count, rows, _ = expert_rows.shape
+def run_experts(width, expert_rows, own, far):
+    rows = expert_rows.shape[1]
     return pl.pallas_call(
-        functools.partial(expert_kernel, width, [len(one) for one in sets]),
+        functools.partial(expert_kernel, width),
         out_shape=shape(expert_rows.shape),
-        in_specs=[VMEM] * (1 + len(weights)),
+        in_specs=[VMEM] * 7,
         out_specs=VMEM,
-        scratch_shapes=[pltpu.VMEM((rows, width // CHUNK * CHUNK), BF16)],
-        compiler_params=pltpu.CompilerParams(vmem_limit_bytes=24 * 1024 * 1024),
-    )(expert_rows, *weights)
+        scratch_shapes=[
+            pltpu.VMEM((rows, width // CHUNK * CHUNK), BF16),
+            pltpu.VMEM(own[1].shape, BF16),
+        ],
+        compiler_params=pltpu.CompilerParams(vmem_limit_bytes=20 * 1024 * 1024),
+    )(expert_rows, *own, *far)
 
 
 def sum_kernel(groups, parts_ref, out_ref):
@@ -424,6 +432,7 @@
         positions, tokens.T, norm_attn, key_matrix.T, value_matrix.T
     )
     far_gate = lax.ppermute(gate, "exp", swap)
+    late = jnp.concatenate([up[:LATE], down], axis=0)
 
     def moved(block, x, z, core):
         route = []
@@ -445,34 +454,32 @@
     prepared = prepare(
         experts, slots, member, expert_ids.T, expert_weights.T, tokens.T, norm_moe
     )
-    *planes, top_row, mixed, gather_table, combine_table, own_tokens, own_gain = (
-        lax.optimization_barrier((*planes, *carried, *prepared))
+    *planes, top_row, mixed, gather_table, combine_table, own_tokens, own_gain, late = (
+        lax.optimization_barrier((*planes, *carried, *prepared, late))
     )
     planes_far = [moved(plane, 0, 0, 1) for plane in planes]
     carried = call(middle_attention_kernel, state, [SMEM] + [VMEM] * 6)(
         positions, queries, top_row, mixed, *planes
     )
     top_row, mixed, far_gate = lax.optimization_barrier((*carried, far_gate))
-    far_up = lax.ppermute(up, "exp", swap)
+    far_up = lax.ppermute(up[LATE:], "exp", swap)
     partial_sums = call(
         last_attention_kernel, shape((exp_count, rows, CHUNK)), [SMEM] + [VMEM] * 7
     )(positions, queries, top_row, mixed, w_out.T, *planes_far)
-    partial_sums, far_up = lax.optimization_barrier((partial_sums, far_up))
+    partial_sums, far_up, late = lax.optimization_barrier((partial_sums, far_up, late))
     parts = exchange(partial_sums, "exp")
-    parts, down = lax.optimization_barrier((parts, down))
     attended, residual, outgoing = call(
         dispatch_kernel,
         [shape((rows, CHUNK)), shape((rows, CHUNK), F32), shape((experts * slots, CHUNK))],
         [VMEM] * 4,
     )(parts, own_tokens, own_gain, gather_table)
     arrived = exchange(outgoing.reshape(ctx_count, slots, CHUNK), "ctx")
-    far_down = lax.ppermute(down, "exp", swap)
-    arrived, far_down = lax.optimization_barrier((arrived, far_down))
+    far_late = lax.ppermute(late, "exp", swap)
+    arrived, far_late = lax.optimization_barrier((arrived, far_late))
     halves = arrived.reshape(1, 2, 1, ctx_count * slots // 2, CHUNK)
     spread = jnp.broadcast_to(halves, (exp_count // 4, 2, 2) + halves.shape[3:])
     expert_rows = exchange(spread.reshape((exp_count,) + halves.shape[3:]), "exp")
-    sets = [(gate, up, down), (far_gate, far_up, far_down)]
-    products = run_experts(width, expert_rows, sets)
+    products = run_experts(width, expert_rows, (gate, up, down), (far_gate, far_up, far_late))
     product_parts = exchange(products, "exp")
     groups = [[i for i in range(exp_count) if (i >> 1) & 1 == half] for half in range(2)]
     summed = call(

time: 216 us -> 206 us (0.954)
  blocking collectives: 119 us -> 103 us
    all_to_all x5 -> x4, blocking collectives: 119 us -> 103 us  [exchange(): lax.all_to_all(block, axis, split_axis=0, concat_axis=0, tiled=True, axis...]
    all_to_all x1 -> x2, waiting for transfers between devices: 0.01 us -> 11.5 us  [exchange(): lax.all_to_all(block, axis, split_axis=0, concat_axis=0, tiled=True, axis...]
    ppermute x2, waiting for transfers between devices: 28.5 us -> 18.8 us  [the longest x1 18.8 us: local(): far_late = lax.ppermute(late, 'exp', swap)]
    unnamed x30 -> x40, local copies, waits for them, and re-layouts: 5.38 us -> 6.46 us
    all_to_all x1 -> x2, starting transfers between devices: 12.9 us -> 13.2 us  [exchange(): lax.all_to_all(block, axis, split_axis=0, concat_axis=0, tiled=True, axis...]
  transfers between devices with their start and end apart: 14 -> 15, of which waited for: 4 -> 5; matrix products, arithmetic and copies ran while one was open for 0% -> 1% of each run, Pallas kernels for 8% -> 9%
where the time goes in v3:
time: 206 us; the launch traced here: 205 us
  blocking collectives  103 us (50%)
  starting transfers between devices  33.6 us (16%)
  waiting for transfers between devices  32.4 us (16%)
  Pallas kernels  26.7 us (13%)
  local copies, waits for them, and re-layouts  7.6 us (4%)
    all_to_all x4, blocking collectives, exchange(): lax.all_to_all(block, axis, split_axis=0, concat_axis=0, tiled=True, axis...  103 us
    ppermute x1, waiting for transfers between devices, local(): far_late = lax.ppermute(late, 'exp', swap)  18.8 us
    ppermute x10, starting transfers between devices, moved(): return lax.ppermute(block, 'ctx', route)  16.6 us
    all_to_all x2, starting transfers between devices, exchange(): lax.all_to_all(block, axis, split_axis=0, concat_axis=0, tiled=True, axis...  13.2 us
    all_to_all x2, waiting for transfers between devices, exchange(): lax.all_to_all(block, axis, split_axis=0, concat_axis=0, tiled=True, axis...  11.5 us
    pallas_call x1, Pallas kernels, run_experts(): pl.pallas_call(functools.partial(expert_kernel, width), out_shape=shape(e...  6.63 us
    unnamed x40, local copies, waits for them, and re-layouts  6.46 us
    pallas_call x1, Pallas kernels, local(): call(last_attention_kernel, shape((exp_count, rows, CHUNK)), [SMEM] + [VM...  4.84 us
  transfers between devices with their start and end apart: 15, of which 5 were waited for; matrix products, arithmetic and copies ran while one was open for 1% of the time, Pallas kernels for 9%

profile of v3, /device:TPU:1, one launch (start us, length us, event | category | flops | bytes accessed | tf_op | source)
XLA Modules:
  0.0 205.4 jit_solution(6205937205080640584)
XLA Ops:
  0.6 2.2 %collective-permute-start.7 = (bf16[180,2880]{1,0:T(8,128)(2,1)}, bf16[180,2880]{1,0:T(8,128)(2,1)}, u32[]{:S(2)}, u32[]{:S(2)}) collective-permute-start(bf16[180,2880]{1,0:T(8,128)(2,1)} %bitcast.34), channel_id=1, source_target_pairs={{0,2},{1,3},{2,0},{3,1},{4,6},{5,7},{6,4},{7,5},{8,10},{9,11},{10,... | collective-permute-start | bytes 3110408 | tf_op jit(solution)/shard_map/ppermute | solution.py:434
  2.8 3.5 %shard_map.149 = (bf16[128,2880]{1,0:T(8,128)(2,1)S(1)}, bf16[144,128]{1,0:T(8,128)(2,1)S(1)}) custom-call(s32[128]{0:T(128)} %pos_ref.7, bf16[2880,128]{1,0:T(8,128)(2,1)} %bitcast.30, f32[2880]{0:T(1024)} %gain_hbm.1, bf16[64,2880]{1,0:T(8,128)(2,1)} %bitcast.42, bf16[64,2880]{1,0:T(8,128)(2,1)} %bitcast.43), custom_call_target="tpu_custom_call" | custom-call | tf_op jit(solution)/shard_map/pallas_call | solution.py:96
  6.3 6.1 %collective-permute-start.2 = (bf16[144,128]{1,0:T(8,128)(2,1)S(1)}, bf16[144,128]{1,0:T(8,128)(2,1)S(1)}, u32[]{:S(2)}, u32[]{:S(2)}) collective-permute-start(bf16[144,128]{1,0:T(8,128)(2,1)S(1)} %get-tuple-element.37), channel_id=1, source_target_pairs={{0,48},{8,56},{16,0},{24,8},{32,16},{40,24},{48,32},{56,40},{64,11... | collective-permute-start | bytes 110600 | tf_op jit(solution)/shard_map/ppermute | solution.py:442
  12.4 1.0 collective-permute-start.1
  13.4 2.3 %collective-permute-start = (bf16[144,128]{1,0:T(8,128)(2,1)S(1)}, bf16[144,128]{1,0:T(8,128)(2,1)S(1)}, u32[]{:S(2)}, u32[]{:S(2)}) collective-permute-start(bf16[144,128]{1,0:T(8,128)(2,1)S(1)} %get-tuple-element.37), channel_id=1, source_target_pairs={{0,16},{8,24},{16,32},{24,40},{32,48},{40,56},{48,0},{56,8},{64,80... | collective-permute-start | bytes 110600 | tf_op jit(solution)/shard_map/ppermute | solution.py:442
  15.7 1.8 copy-done.3
  19.2 2.5 %collective-permute-start.6 = (bf16[4,144,128]{2,1,0:T(8,128)(2,1)S(1)}, bf16[4,144,128]{2,1,0:T(8,128)(2,1)S(1)}, u32[]{:S(2)}, u32[]{:S(2)}) collective-permute-start(bf16[4,144,128]{2,1,0:T(8,128)(2,1)S(1)} %pad_maximum_fusion.1.refs_0_), channel_id=1, source_target_pairs={{0,8},{8,0},{16,24},{24,16},{32,40},{40,32},{48,56},{56,48},{64,72... | collective-permute-start | bytes 442376 | tf_op jit(solution)/shard_map/ppermute | solution.py:442
  22.8 2.6 %collective-permute-start.5 = (bf16[4,144,128]{2,1,0:T(8,128)(2,1)S(1)}, bf16[4,144,128]{2,1,0:T(8,128)(2,1)}, u32[]{:S(2)}, u32[]{:S(2)}) collective-permute-start(bf16[4,144,128]{2,1,0:T(8,128)(2,1)S(1)} %pad_maximum_fusion.1.refs_0_), channel_id=1, source_target_pairs={{0,192},{8,200},{16,208},{24,216},{32,224},{40,232},{48,240},{56,2... | collective-permute-start | bytes 442376 | tf_op jit(solution)/shard_map/ppermute | solution.py:442
  27.2 1.3 pad_maximum_fusion
  31.7 3.1 %shard_map.151 = (f32[1024,1]{1,0:T(8,128)S(1)}, f32[1024,128]{1,0:T(8,128)S(1)}) custom-call(s32[128]{0:T(128)S(1)} %copy-done.16, f32[8]{0:T(128)S(1)} %copy-done.19, bf16[1024,128]{1,0:T(8,128)(2,1)S(1)} %shard_map.150.query_ref, bf16[4,144,128]{2,1,0:T(8,128)(2,1)S(1)} %pad_maximum_fusion.1.refs_0_, bf16[4,144,128]{2,1,0:T(8,128)(2,1)S(1)} %copy-done.10), custom_call_target="tpu_custom_call" | custom-call | tf_op jit(solution)/shard_map/pallas_call | solution.py:451
  34.9 1.0 collective-permute-done.3.refs_0_
  36.9 4.4 %shard_map.153 = (f32[1024,1]{1,0:T(8,128)S(1)}, f32[1024,128]{1,0:T(8,128)S(1)}) custom-call(s32[128]{0:T(128)S(1)} %copy-done.16, bf16[1024,128]{1,0:T(8,128)(2,1)S(1)} %shard_map.150.query_ref, f32[1024,1]{1,0:T(8,128)S(1)} %get-tuple-element.49.old_top_ref, f32[1024,128]{1,0:T(8,128)S(1)} %get-tuple-element.50.old_mixed_ref, ...), custom_call_target="tpu_custom_call" | custom-call | tf_op jit(solution)/shard_map/pallas_call | solution.py:461
  41.3 4.8 %shard_map.154 = bf16[8,128,384]{2,1,0:T(8,128)(2,1)S(1)} custom-call(s32[128]{0:T(128)S(1)} %copy-done.16, bf16[1024,128]{1,0:T(8,128)(2,1)S(1)} %shard_map.150.query_ref, f32[1024,1]{1,0:T(8,128)S(1)} %get-tuple-element.56.old_top_ref, f32[1024,128]{1,0:T(8,128)S(1)} %get-tuple-element.57.old_mixed_ref, bf16[2880,512]{1,0:T(8,128)(2,1)S(1)} %bitcast.29, ...), custom_call_target="tpu_custom_call" | custom-call | tf_op jit(solution)/shard_map/pallas_call | solution.py:466
  47.1 4.7 %all-to-all-start = ((bf16[8,128,384]{2,1,0:T(8,128)(2,1)}), bf16[8,128,384]{2,1,0:T(8,128)(2,1)S(1)}, u32[]{:S(2)}, u32[]{:S(2)}) async-start(bf16[8,128,384]{2,1,0:T(8,128)(2,1)} %copy-done.2), calls=%async_computation | async-start | bytes 1572864 | tf_op jit(solution)/shard_map/all_to_all | solution.py:398
  51.8 1.5 collective-permute-start.12
  53.3 11.3 %all-to-all-done.parts_ref = bf16[8,128,384]{2,1,0:T(8,128)(2,1)S(1)} async-done(((bf16[8,128,384]{2,1,0:T(8,128)(2,1)}), bf16[8,128,384]{2,1,0:T(8,128)(2,1)S(1)}, u32[]{:S(2)}, u32[]{:S(2)}) %all-to-all-start) | async-done | bytes 786464 | tf_op jit(solution)/shard_map/all_to_all | solution.py:398
  64.6 1.3 shard_map.155
  66.5 8.5 %all-to-all-start.1 = ((bf16[32,24,384]{2,1,0:T(8,128)(2,1)}), bf16[32,24,384]{2,1,0:T(8,128)(2,1)S(1)}, u32[]{:S(2)}, u32[]{:S(2)}) async-start(bf16[32,24,384]{2,1,0:T(8,128)(2,1)} %bitcast.17), calls=%async_computation.1 | async-start | bytes 1179648 | tf_op jit(solution)/shard_map/all_to_all | solution.py:398
  75.0 18.8 %collective-permute-done.12.late_ref = bf16[244,2880]{1,0:T(8,128)(2,1)} collective-permute-done((bf16[244,2880]{1,0:T(8,128)(2,1)}, bf16[244,2880]{1,0:T(8,128)(2,1)}, u32[]{:S(2)}, u32[]{:S(2)}) %collective-permute-start.12) | collective-permute-done | bytes 1405472 | tf_op jit(solution)/shard_map/ppermute | solution.py:477
  94.3 34.0 %all_to_all.30.rows_in_ref = bf16[8,384,384]{2,1,0:T(8,128)(2,1)S(1)} all-to-all(bf16[8,384,384]{2,1,0:T(8,128)(2,1)S(1)} %bitcast.40), channel_id=1, replica_groups=mesh['ctx'=32,'exp'=8] {'exp'}, dimensions={0} | all-to-all | bytes 4718592 | tf_op jit(solution)/shard_map/all_to_all | solution.py:398
  128.4 6.6 %shard_map.156 = bf16[8,384,384]{2,1,0:T(8,128)(2,1)S(1)} custom-call(bf16[8,384,384]{2,1,0:T(8,128)(2,1)S(1)} %all_to_all.30.rows_in_ref, bf16[180,2880]{1,0:T(8,128)(2,1)S(1)} %bitcast.35, bf16[180,2880]{1,0:T(8,128)(2,1)S(1)} %bitcast.28, bf16[180,2880]{1,0:T(8,128)(2,1)S(1)} %bitcast.25, bf16[180,2880]{1,0:T(8,128)(2,1)} %collective-permute-done.7.far_gate_ref, ...), custom_call_target="tpu_custom_call" | custom-call | tf_op jit(solution)/shard_map/pallas_call | solution.py:354
  135.0 30.3 %all_to_all.31.parts_ref = bf16[8,384,384]{2,1,0:T(8,128)(2,1)S(1)} all-to-all(bf16[8,384,384]{2,1,0:T(8,128)(2,1)S(1)} %shard_map.156), channel_id=1, replica_groups=mesh['ctx'=32,'exp'=8] {'exp'}, dimensions={0} | all-to-all | bytes 4718592 | tf_op jit(solution)/shard_map/all_to_all | solution.py:398
  165.6 29.2 %all_to_all.32 = bf16[32,24,384]{2,1,0:T(8,128)(2,1)S(1)} all-to-all(bf16[32,24,384]{2,1,0:T(8,128)(2,1)S(1)} %bitcast.33), channel_id=1, replica_groups=mesh['ctx'=32,'exp'=8] {'ctx'}, dimensions={0} | all-to-all | bytes 1179648 | tf_op jit(solution)/shard_map/all_to_all | solution.py:398
  195.3 9.4 %all_to_all.33.parts_ref = bf16[8,16,768]{2,1,0:T(8,128)(2,1)S(1)} all-to-all(bf16[8,16,768]{2,1,0:T(8,128)(2,1)S(1)} %bitcast.36), channel_id=1, replica_groups=mesh['ctx'=32,'exp'=8] {'exp'}, dimensions={0} | all-to-all | bytes 393216 | tf_op jit(solution)/shard_map/all_to_all | solution.py:398
  (66 shorter events, 12.3 us)
Async XLA Ops:
  0.6 40.7 %collective-permute-start.7 = (bf16[180,2880]{1,0:T(8,128)(2,1)}, bf16[180,2880]{1,0:T(8,128)(2,1)}, u32[]{:S(2)}, u32[]{:S(2)}) collective-permute-start(bf16[180,2880]{1,0:T(8,128)(2,1)} %bitcast.34), channel_id=1, source_target_pairs={{0,2},{1,3},{2,0},{3,1},{4,6},{5,7},{6,4},{7,5},{8,10},{9,11},{10,... | collective-permute-start | bytes 3110408 | tf_op jit(solution)/shard_map/ppermute | solution.py:434
  6.3 11.9 %collective-permute-start.2 = (bf16[144,128]{1,0:T(8,128)(2,1)S(1)}, bf16[144,128]{1,0:T(8,128)(2,1)S(1)}, u32[]{:S(2)}, u32[]{:S(2)}) collective-permute-start(bf16[144,128]{1,0:T(8,128)(2,1)S(1)} %get-tuple-element.37), channel_id=1, source_target_pairs={{0,48},{8,56},{16,0},{24,8},{32,16},{40,24},{48,32},{56,40},{64,11... | collective-permute-start | bytes 110600 | tf_op jit(solution)/shard_map/ppermute | solution.py:442
  12.4 6.7 %collective-permute-start.1 = (bf16[144,128]{1,0:T(8,128)(2,1)S(1)}, bf16[144,128]{1,0:T(8,128)(2,1)S(1)}, u32[]{:S(2)}, u32[]{:S(2)}) collective-permute-start(bf16[144,128]{1,0:T(8,128)(2,1)S(1)} %get-tuple-element.37), channel_id=1, source_target_pairs={{0,32},{8,40},{16,48},{24,56},{32,0},{40,8},{48,16},{56,24},{64,96... | collective-permute-start | bytes 110600 | tf_op jit(solution)/shard_map/ppermute | solution.py:442
  13.4 5.7 %collective-permute-start = (bf16[144,128]{1,0:T(8,128)(2,1)S(1)}, bf16[144,128]{1,0:T(8,128)(2,1)S(1)}, u32[]{:S(2)}, u32[]{:S(2)}) collective-permute-start(bf16[144,128]{1,0:T(8,128)(2,1)S(1)} %get-tuple-element.37), channel_id=1, source_target_pairs={{0,16},{8,24},{16,32},{24,40},{32,48},{40,56},{48,0},{56,8},{64,80... | collective-permute-start | bytes 110600 | tf_op jit(solution)/shard_map/ppermute | solution.py:442
  17.5 4.2 %copy-start.1 = (bf16[1,2880,180]{1,2,0:T(8,128)(2,1)S(1)}, bf16[1,2880,180]{1,2,0:T(8,128)(2,1)}, u32[]{:S(2)}) copy-start(bf16[1,2880,180]{1,2,0:T(8,128)(2,1)} %param.26) | copy-start | bytes 3110404
  18.2 9.0 %copy-start = (bf16[1,180,2880]{2,1,0:T(8,128)(2,1)S(1)}, bf16[1,180,2880]{2,1,0:T(8,128)(2,1)}, u32[]{:S(2)}) copy-start(bf16[1,180,2880]{2,1,0:T(8,128)(2,1)} %param.27) | copy-start | bytes 3110404
  19.2 6.7 %collective-permute-start.6 = (bf16[4,144,128]{2,1,0:T(8,128)(2,1)S(1)}, bf16[4,144,128]{2,1,0:T(8,128)(2,1)S(1)}, u32[]{:S(2)}, u32[]{:S(2)}) collective-permute-start(bf16[4,144,128]{2,1,0:T(8,128)(2,1)S(1)} %pad_maximum_fusion.1.refs_0_), channel_id=1, source_target_pairs={{0,8},{8,0},{16,24},{24,16},{32,40},{40,32},{48,56},{56,48},{64,72... | collective-permute-start | bytes 442376 | tf_op jit(solution)/shard_map/ppermute | solution.py:442
  22.6 24.5 %collective-permute-start.11 = (bf16[116,2880]{1,0:T(8,128)(2,1)}, bf16[116,2880]{1,0:T(8,128)(2,1)}, u32[]{:S(2)}, u32[]{:S(2)}) collective-permute-start(bf16[116,2880]{1,0:T(8,128)(2,1)} %slice.9), channel_id=1, source_target_pairs={{0,2},{1,3},{2,0},{3,1},{4,6},{5,7},{6,4},{7,5},{8,10},{9,11},{10,... | collective-permute-start | bytes 2004488 | tf_op jit(solution)/shard_map/ppermute | solution.py:465
  22.8 12.0 %collective-permute-start.5 = (bf16[4,144,128]{2,1,0:T(8,128)(2,1)S(1)}, bf16[4,144,128]{2,1,0:T(8,128)(2,1)}, u32[]{:S(2)}, u32[]{:S(2)}) collective-permute-start(bf16[4,144,128]{2,1,0:T(8,128)(2,1)S(1)} %pad_maximum_fusion.1.refs_0_), channel_id=1, source_target_pairs={{0,192},{8,200},{16,208},{24,216},{32,224},{40,232},{48,240},{56,2... | collective-permute-start | bytes 442376 | tf_op jit(solution)/shard_map/ppermute | solution.py:442
  25.4 9.5 %collective-permute-start.4 = (bf16[4,144,128]{2,1,0:T(8,128)(2,1)S(1)}, bf16[4,144,128]{2,1,0:T(8,128)(2,1)}, u32[]{:S(2)}, u32[]{:S(2)}) collective-permute-start(bf16[4,144,128]{2,1,0:T(8,128)(2,1)S(1)} %pad_maximum_fusion.1.refs_0_), channel_id=1, source_target_pairs={{0,128},{8,136},{16,144},{24,152},{32,160},{40,168},{48,176},{56,1... | collective-permute-start | bytes 442376 | tf_op jit(solution)/shard_map/ppermute | solution.py:442
  26.5 9.4 %collective-permute-start.3 = (bf16[4,144,128]{2,1,0:T(8,128)(2,1)S(1)}, bf16[4,144,128]{2,1,0:T(8,128)(2,1)}, u32[]{:S(2)}, u32[]{:S(2)}) collective-permute-start(bf16[4,144,128]{2,1,0:T(8,128)(2,1)S(1)} %pad_maximum_fusion.1.refs_0_), channel_id=1, source_target_pairs={{0,64},{8,72},{16,80},{24,88},{32,96},{40,104},{48,112},{56,120},{... | collective-permute-start | bytes 442376 | tf_op jit(solution)/shard_map/ppermute | solution.py:442
  27.2 3.6 %copy-start.16 = (s32[128]{0:T(128)S(1)}, s32[128]{0:T(128)}, u32[]{:S(2)}) copy-start(s32[128]{0:T(128)} %pos_ref.7) | copy-start | bytes 1540
  27.2 3.6 %copy-start.19 = (f32[8]{0:T(128)S(1)}, f32[8]{0:T(128)}, u32[]{:S(2)}) copy-start(f32[8]{0:T(128)} %sink_ref.1) | copy-start | bytes 100
  28.5 12.9 %copy-start.4 = (bf16[512,2880]{0,1:T(8,128)(2,1)S(1)}, bf16[512,2880]{0,1:T(8,128)(2,1)}, u32[]{:S(2)}) copy-start(bf16[512,2880]{0,1:T(8,128)(2,1)} %param.21) | copy-start | bytes 8847364
  35.9 5.4 %collective-permute-start.8 = (bf16[4,144,128]{2,1,0:T(8,128)(2,1)}, bf16[4,144,128]{2,1,0:T(8,128)(2,1)S(1)}, u32[]{:S(2)}, u32[]{:S(2)}) collective-permute-start(bf16[4,144,128]{2,1,0:T(8,128)(2,1)} %collective-permute-done.3.refs_0_), channel_id=1, source_target_pairs={{0,8},{8,0},{16,24},{24,16},{32,40},{40,32},{48,56},{56,48},{64,72... | collective-permute-start | bytes 442376 | tf_op jit(solution)/shard_map/ppermute | solution.py:442
  36.4 4.9 %collective-permute-start.9 = (bf16[4,144,128]{2,1,0:T(8,128)(2,1)}, bf16[4,144,128]{2,1,0:T(8,128)(2,1)S(1)}, u32[]{:S(2)}, u32[]{:S(2)}) collective-permute-start(bf16[4,144,128]{2,1,0:T(8,128)(2,1)} %collective-permute-done.4.refs_1_), channel_id=1, source_target_pairs={{0,8},{8,0},{16,24},{24,16},{32,40},{40,32},{48,56},{56,48},{64,72... | collective-permute-start | bytes 442376 | tf_op jit(solution)/shard_map/ppermute | solution.py:442
  36.4 4.9 %collective-permute-start.10 = (bf16[4,144,128]{2,1,0:T(8,128)(2,1)}, bf16[4,144,128]{2,1,0:T(8,128)(2,1)S(1)}, u32[]{:S(2)}, u32[]{:S(2)}) collective-permute-start(bf16[4,144,128]{2,1,0:T(8,128)(2,1)} %collective-permute-done.5.refs_2_), channel_id=1, source_target_pairs={{0,8},{8,0},{16,24},{24,16},{32,40},{40,32},{48,56},{56,48},{64,72... | collective-permute-start | bytes 442376 | tf_op jit(solution)/shard_map/ppermute | solution.py:442
  47.1 17.5 %copy-start.12 = (bf16[128,384]{1,0:T(8,128)(2,1)S(1)}, bf16[128,384]{1,0:T(8,128)(2,1)}, u32[]{:S(2)}) copy-start(bf16[128,384]{1,0:T(8,128)(2,1)} %copy-done.11) | copy-start | bytes 294916
  47.1 17.5 %all-to-all-start = ((bf16[8,128,384]{2,1,0:T(8,128)(2,1)}), bf16[8,128,384]{2,1,0:T(8,128)(2,1)S(1)}, u32[]{:S(2)}, u32[]{:S(2)}) async-start(bf16[8,128,384]{2,1,0:T(8,128)(2,1)} %copy-done.2), calls=%async_computation | async-start | bytes 1572864 | tf_op jit(solution)/shard_map/all_to_all | solution.py:398
  51.8 42.0 %collective-permute-start.12 = (bf16[244,2880]{1,0:T(8,128)(2,1)}, bf16[244,2880]{1,0:T(8,128)(2,1)}, u32[]{:S(2)}, u32[]{:S(2)}) collective-permute-start(bf16[244,2880]{1,0:T(8,128)(2,1)} %pad_maximum_fusion), channel_id=1, source_target_pairs={{0,2},{1,3},{2,0},{3,1},{4,6},{5,7},{6,4},{7,5},{8,10},{9,11},{10,... | collective-permute-start | bytes 4216328 | tf_op jit(solution)/shard_map/ppermute | solution.py:477
  66.5 27.5 %all-to-all-start.1 = ((bf16[32,24,384]{2,1,0:T(8,128)(2,1)}), bf16[32,24,384]{2,1,0:T(8,128)(2,1)S(1)}, u32[]{:S(2)}, u32[]{:S(2)}) async-start(bf16[32,24,384]{2,1,0:T(8,128)(2,1)} %bitcast.17), calls=%async_computation.1 | async-start | bytes 1179648 | tf_op jit(solution)/shard_map/all_to_all | solution.py:398
  94.3 34.1 %copy-start.6 = (bf16[1,2880,180]{1,2,0:T(8,128)(2,1)S(1)}, bf16[1,2880,180]{1,2,0:T(8,128)(2,1)}, u32[]{:S(2)}) copy-start(bf16[1,2880,180]{1,2,0:T(8,128)(2,1)} %param.25) | copy-start | bytes 3110404
  165.3 29.5 %copy-start.8 = (bf16[384,768]{1,0:T(8,128)(2,1)S(1)}, bf16[384,768]{1,0:T(8,128)(2,1)}, u32[]{:S(2)}) copy-start(bf16[384,768]{1,0:T(8,128)(2,1)} %copy-done.7) | copy-start | bytes 1769476
  165.3 29.5 %copy-start.14 = (bf16[128,384]{1,0:T(8,128)(2,1)S(1)}, bf16[128,384]{1,0:T(8,128)(2,1)}, u32[]{:S(2)}) copy-start(bf16[128,384]{1,0:T(8,128)(2,1)} %copy-done.13) | copy-start | bytes 294916
  (11 other events, 11.6 us)

commit v4 on v3

--- a/solution.py
+++ b/solution.py
@@ -11,7 +11,7 @@
 EPSILON = 1e-05
 CHUNK = 384
 TAIL = 16
-LATE = 64
+LATE = 48
 MAIN = CHUNK - TAIL
 EXTRA = 16
 BF16 = jnp.bfloat16

time: 206 us -> 204 us (level)
  blocking collectives: 103 us -> 98.7 us
  starting transfers between devices: 33.6 us -> 36.6 us
    ppermute x1, waiting for transfers between devices: 18.8 us -> 13.5 us  [local(): far_late = lax.ppermute(late, 'exp', swap)]
    all_to_all x2, waiting for transfers between devices: 11.5 us -> 16.8 us  [exchange(): lax.all_to_all(block, axis, split_axis=0, concat_axis=0, tiled=True, axis...]
    all_to_all x4, blocking collectives: 103 us -> 98.7 us  [exchange(): lax.all_to_all(block, axis, split_axis=0, concat_axis=0, tiled=True, axis...]
    all_to_all x2, starting transfers between devices: 13.2 us -> 16.4 us  [exchange(): lax.all_to_all(block, axis, split_axis=0, concat_axis=0, tiled=True, axis...]
  transfers between devices with their start and end apart: 15 -> 15, of which waited for: 5 -> 4; matrix products, arithmetic and copies ran while one was open for 1% -> 1% of each run, Pallas kernels for 9% -> 9%
where the time goes in v4:
time: 204 us; the launch traced here: 203 us
  blocking collectives  98.7 us (48%)
  starting transfers between devices  36.6 us (18%)
  waiting for transfers between devices  31.4 us (15%)
  Pallas kernels  26.7 us (13%)
  local copies, waits for them, and re-layouts  7.66 us (4%)
    all_to_all x4, blocking collectives, exchange(): lax.all_to_all(block, axis, split_axis=0, concat_axis=0, tiled=True, axis...  98.7 us
    all_to_all x2, waiting for transfers between devices, exchange(): lax.all_to_all(block, axis, split_axis=0, concat_axis=0, tiled=True, axis...  16.8 us
    all_to_all x2, starting transfers between devices, exchange(): lax.all_to_all(block, axis, split_axis=0, concat_axis=0, tiled=True, axis...  16.4 us
    ppermute x10, starting transfers between devices, moved(): return lax.ppermute(block, 'ctx', route)  16.3 us
    ppermute x1, waiting for transfers between devices, local(): far_late = lax.ppermute(late, 'exp', swap)  13.5 us
    pallas_call x1, Pallas kernels, run_experts(): pl.pallas_call(functools.partial(expert_kernel, width), out_shape=shape(e...  6.62 us
    unnamed x40, local copies, waits for them, and re-layouts  6.47 us
    pallas_call x1, Pallas kernels, local(): call(last_attention_kernel, shape((exp_count, rows, CHUNK)), [SMEM] + [VM...  4.84 us
  transfers between devices with their start and end apart: 15, of which 4 were waited for; matrix products, arithmetic and copies ran while one was open for 1% of the time, Pallas kernels for 9%

profile of v4, /device:TPU:1, one launch (start us, length us, event | category | flops | bytes accessed | tf_op | source)
XLA Modules:
  0.0 203.1 jit_solution(8499366379183114166)
XLA Ops:
  0.6 2.2 %collective-permute-start.7 = (bf16[180,2880]{1,0:T(8,128)(2,1)}, bf16[180,2880]{1,0:T(8,128)(2,1)}, u32[]{:S(2)}, u32[]{:S(2)}) collective-permute-start(bf16[180,2880]{1,0:T(8,128)(2,1)} %bitcast.34), channel_id=1, source_target_pairs={{0,2},{1,3},{2,0},{3,1},{4,6},{5,7},{6,4},{7,5},{8,10},{9,11},{10,... | collective-permute-start | bytes 3110408 | tf_op jit(solution)/shard_map/ppermute | solution.py:434
  2.9 3.5 %shard_map.149 = (bf16[128,2880]{1,0:T(8,128)(2,1)S(1)}, bf16[144,128]{1,0:T(8,128)(2,1)S(1)}) custom-call(s32[128]{0:T(128)} %pos_ref.7, bf16[2880,128]{1,0:T(8,128)(2,1)} %bitcast.30, f32[2880]{0:T(1024)} %gain_hbm.1, bf16[64,2880]{1,0:T(8,128)(2,1)} %bitcast.42, bf16[64,2880]{1,0:T(8,128)(2,1)} %bitcast.43), custom_call_target="tpu_custom_call" | custom-call | tf_op jit(solution)/shard_map/pallas_call | solution.py:96
  6.3 6.1 %collective-permute-start.2 = (bf16[144,128]{1,0:T(8,128)(2,1)S(1)}, bf16[144,128]{1,0:T(8,128)(2,1)S(1)}, u32[]{:S(2)}, u32[]{:S(2)}) collective-permute-start(bf16[144,128]{1,0:T(8,128)(2,1)S(1)} %get-tuple-element.37), channel_id=1, source_target_pairs={{0,48},{8,56},{16,0},{24,8},{32,16},{40,24},{48,32},{56,40},{64,11... | collective-permute-start | bytes 110600 | tf_op jit(solution)/shard_map/ppermute | solution.py:442
  13.4 2.3 %collective-permute-start = (bf16[144,128]{1,0:T(8,128)(2,1)S(1)}, bf16[144,128]{1,0:T(8,128)(2,1)S(1)}, u32[]{:S(2)}, u32[]{:S(2)}) collective-permute-start(bf16[144,128]{1,0:T(8,128)(2,1)S(1)} %get-tuple-element.37), channel_id=1, source_target_pairs={{0,16},{8,24},{16,32},{24,40},{32,48},{40,56},{48,0},{56,8},{64,80... | collective-permute-start | bytes 110600 | tf_op jit(solution)/shard_map/ppermute | solution.py:442
  16.9 1.8 copy-done.3
  19.5 2.2 %collective-permute-start.6 = (bf16[4,144,128]{2,1,0:T(8,128)(2,1)S(1)}, bf16[4,144,128]{2,1,0:T(8,128)(2,1)S(1)}, u32[]{:S(2)}, u32[]{:S(2)}) collective-permute-start(bf16[4,144,128]{2,1,0:T(8,128)(2,1)S(1)} %pad_maximum_fusion.1.refs_0_), channel_id=1, source_target_pairs={{0,8},{8,0},{16,24},{24,16},{32,40},{40,32},{48,56},{56,48},{64,72... | collective-permute-start | bytes 442376 | tf_op jit(solution)/shard_map/ppermute | solution.py:442
  21.7 2.6 %collective-permute-start.5 = (bf16[4,144,128]{2,1,0:T(8,128)(2,1)S(1)}, bf16[4,144,128]{2,1,0:T(8,128)(2,1)}, u32[]{:S(2)}, u32[]{:S(2)}) collective-permute-start(bf16[4,144,128]{2,1,0:T(8,128)(2,1)S(1)} %pad_maximum_fusion.1.refs_0_), channel_id=1, source_target_pairs={{0,192},{8,200},{16,208},{24,216},{32,224},{40,232},{48,240},{56,2... | collective-permute-start | bytes 442376 | tf_op jit(solution)/shard_map/ppermute | solution.py:442
  26.1 1.2 pad_maximum_fusion
  30.6 3.1 %shard_map.151 = (f32[1024,1]{1,0:T(8,128)S(1)}, f32[1024,128]{1,0:T(8,128)S(1)}) custom-call(s32[128]{0:T(128)S(1)} %copy-done.16, f32[8]{0:T(128)S(1)} %copy-done.19, bf16[1024,128]{1,0:T(8,128)(2,1)S(1)} %shard_map.150.query_ref, bf16[4,144,128]{2,1,0:T(8,128)(2,1)S(1)} %pad_maximum_fusion.1.refs_0_, bf16[4,144,128]{2,1,0:T(8,128)(2,1)S(1)} %copy-done.10), custom_call_target="tpu_custom_call" | custom-call | tf_op jit(solution)/shard_map/pallas_call | solution.py:451
  33.7 1.1 collective-permute-done.3.refs_0_
  35.8 4.4 %shard_map.153 = (f32[1024,1]{1,0:T(8,128)S(1)}, f32[1024,128]{1,0:T(8,128)S(1)}) custom-call(s32[128]{0:T(128)S(1)} %copy-done.16, bf16[1024,128]{1,0:T(8,128)(2,1)S(1)} %shard_map.150.query_ref, f32[1024,1]{1,0:T(8,128)S(1)} %get-tuple-element.49.old_top_ref, f32[1024,128]{1,0:T(8,128)S(1)} %get-tuple-element.50.old_mixed_ref, ...), custom_call_target="tpu_custom_call" | custom-call | tf_op jit(solution)/shard_map/pallas_call | solution.py:461
  40.3 4.8 %shard_map.154 = bf16[8,128,384]{2,1,0:T(8,128)(2,1)S(1)} custom-call(s32[128]{0:T(128)S(1)} %copy-done.16, bf16[1024,128]{1,0:T(8,128)(2,1)S(1)} %shard_map.150.query_ref, f32[1024,1]{1,0:T(8,128)S(1)} %get-tuple-element.56.old_top_ref, f32[1024,128]{1,0:T(8,128)S(1)} %get-tuple-element.57.old_mixed_ref, bf16[2880,512]{1,0:T(8,128)(2,1)S(1)} %bitcast.29, ...), custom_call_target="tpu_custom_call" | custom-call | tf_op jit(solution)/shard_map/pallas_call | solution.py:466
  46.0 4.6 %all-to-all-start = ((bf16[8,128,384]{2,1,0:T(8,128)(2,1)}), bf16[8,128,384]{2,1,0:T(8,128)(2,1)S(1)}, u32[]{:S(2)}, u32[]{:S(2)}) async-start(bf16[8,128,384]{2,1,0:T(8,128)(2,1)} %copy-done.2), calls=%async_computation | async-start | bytes 1572864 | tf_op jit(solution)/shard_map/all_to_all | solution.py:398
  50.6 1.5 collective-permute-start.12
  52.1 11.0 %all-to-all-done.parts_ref = bf16[8,128,384]{2,1,0:T(8,128)(2,1)S(1)} async-done(((bf16[8,128,384]{2,1,0:T(8,128)(2,1)}), bf16[8,128,384]{2,1,0:T(8,128)(2,1)S(1)}, u32[]{:S(2)}, u32[]{:S(2)}) %all-to-all-start) | async-done | bytes 786464 | tf_op jit(solution)/shard_map/all_to_all | solution.py:398
  63.1 1.3 shard_map.155
  65.0 11.8 %all-to-all-start.1 = ((bf16[32,24,384]{2,1,0:T(8,128)(2,1)}), bf16[32,24,384]{2,1,0:T(8,128)(2,1)S(1)}, u32[]{:S(2)}, u32[]{:S(2)}) async-start(bf16[32,24,384]{2,1,0:T(8,128)(2,1)} %bitcast.17), calls=%async_computation.1 | async-start | bytes 1179648 | tf_op jit(solution)/shard_map/all_to_all | solution.py:398
  76.8 13.5 %collective-permute-done.12.late_ref = bf16[228,2880]{1,0:T(8,128)(2,1)} collective-permute-done((bf16[228,2880]{1,0:T(8,128)(2,1)}, bf16[228,2880]{1,0:T(8,128)(2,1)}, u32[]{:S(2)}, u32[]{:S(2)}) %collective-permute-start.12) | collective-permute-done | bytes 1313312 | tf_op jit(solution)/shard_map/ppermute | solution.py:477
  90.3 5.7 %all-to-all-done.1 = bf16[32,24,384]{2,1,0:T(8,128)(2,1)S(1)} async-done(((bf16[32,24,384]{2,1,0:T(8,128)(2,1)}), bf16[32,24,384]{2,1,0:T(8,128)(2,1)S(1)}, u32[]{:S(2)}, u32[]{:S(2)}) %all-to-all-start.1) | async-done | bytes 589856 | tf_op jit(solution)/shard_map/all_to_all | solution.py:398
  96.3 31.2 %all_to_all.30.rows_in_ref = bf16[8,384,384]{2,1,0:T(8,128)(2,1)S(1)} all-to-all(bf16[8,384,384]{2,1,0:T(8,128)(2,1)S(1)} %bitcast.40), channel_id=1, replica_groups=mesh['ctx'=32,'exp'=8] {'exp'}, dimensions={0} | all-to-all | bytes 4718592 | tf_op jit(solution)/shard_map/all_to_all | solution.py:398
  127.5 6.6 %shard_map.156 = bf16[8,384,384]{2,1,0:T(8,128)(2,1)S(1)} custom-call(bf16[8,384,384]{2,1,0:T(8,128)(2,1)S(1)} %all_to_all.30.rows_in_ref, bf16[180,2880]{1,0:T(8,128)(2,1)S(1)} %bitcast.35, bf16[180,2880]{1,0:T(8,128)(2,1)S(1)} %bitcast.26, bf16[180,2880]{1,0:T(8,128)(2,1)S(1)} %bitcast.28, bf16[180,2880]{1,0:T(8,128)(2,1)} %collective-permute-done.7.far_gate_ref, ...), custom_call_target="tpu_custom_call" | custom-call | tf_op jit(solution)/shard_map/pallas_call | solution.py:354
  134.1 30.4 %all_to_all.31.parts_ref = bf16[8,384,384]{2,1,0:T(8,128)(2,1)S(1)} all-to-all(bf16[8,384,384]{2,1,0:T(8,128)(2,1)S(1)} %shard_map.156), channel_id=1, replica_groups=mesh['ctx'=32,'exp'=8] {'exp'}, dimensions={0} | all-to-all | bytes 4718592 | tf_op jit(solution)/shard_map/all_to_all | solution.py:398
  164.9 27.2 %all_to_all.32 = bf16[32,24,384]{2,1,0:T(8,128)(2,1)S(1)} all-to-all(bf16[32,24,384]{2,1,0:T(8,128)(2,1)S(1)} %bitcast.33), channel_id=1, replica_groups=mesh['ctx'=32,'exp'=8] {'ctx'}, dimensions={0} | all-to-all | bytes 1179648 | tf_op jit(solution)/shard_map/all_to_all | solution.py:398
  192.6 9.8 %all_to_all.33.parts_ref = bf16[8,16,768]{2,1,0:T(8,128)(2,1)S(1)} all-to-all(bf16[8,16,768]{2,1,0:T(8,128)(2,1)S(1)} %bitcast.36), channel_id=1, replica_groups=mesh['ctx'=32,'exp'=8] {'exp'}, dimensions={0} | all-to-all | bytes 393216 | tf_op jit(solution)/shard_map/all_to_all | solution.py:398
  (66 shorter events, 12.3 us)
Async XLA Ops:
  0.6 15.0 %copy-start = (bf16[1,2880,180]{1,2,0:T(8,128)(2,1)S(1)}, bf16[1,2880,180]{1,2,0:T(8,128)(2,1)}, u32[]{:S(2)}) copy-start(bf16[1,2880,180]{1,2,0:T(8,128)(2,1)} %param.26) | copy-start | bytes 3110404
  0.6 39.6 %collective-permute-start.7 = (bf16[180,2880]{1,0:T(8,128)(2,1)}, bf16[180,2880]{1,0:T(8,128)(2,1)}, u32[]{:S(2)}, u32[]{:S(2)}) collective-permute-start(bf16[180,2880]{1,0:T(8,128)(2,1)} %bitcast.34), channel_id=1, source_target_pairs={{0,2},{1,3},{2,0},{3,1},{4,6},{5,7},{6,4},{7,5},{8,10},{9,11},{10,... | collective-permute-start | bytes 3110408 | tf_op jit(solution)/shard_map/ppermute | solution.py:434
  6.3 13.1 %collective-permute-start.2 = (bf16[144,128]{1,0:T(8,128)(2,1)S(1)}, bf16[144,128]{1,0:T(8,128)(2,1)S(1)}, u32[]{:S(2)}, u32[]{:S(2)}) collective-permute-start(bf16[144,128]{1,0:T(8,128)(2,1)S(1)} %get-tuple-element.37), channel_id=1, source_target_pairs={{0,48},{8,56},{16,0},{24,8},{32,16},{40,24},{48,32},{56,40},{64,11... | collective-permute-start | bytes 110600 | tf_op jit(solution)/shard_map/ppermute | solution.py:442
  12.4 7.0 %collective-permute-start.1 = (bf16[144,128]{1,0:T(8,128)(2,1)S(1)}, bf16[144,128]{1,0:T(8,128)(2,1)S(1)}, u32[]{:S(2)}, u32[]{:S(2)}) collective-permute-start(bf16[144,128]{1,0:T(8,128)(2,1)S(1)} %get-tuple-element.37), channel_id=1, source_target_pairs={{0,32},{8,40},{16,48},{24,56},{32,0},{40,8},{48,16},{56,24},{64,96... | collective-permute-start | bytes 110600 | tf_op jit(solution)/shard_map/ppermute | solution.py:442
  13.4 6.0 %collective-permute-start = (bf16[144,128]{1,0:T(8,128)(2,1)S(1)}, bf16[144,128]{1,0:T(8,128)(2,1)S(1)}, u32[]{:S(2)}, u32[]{:S(2)}) collective-permute-start(bf16[144,128]{1,0:T(8,128)(2,1)S(1)} %get-tuple-element.37), channel_id=1, source_target_pairs={{0,16},{8,24},{16,32},{24,40},{32,48},{40,56},{48,0},{56,8},{64,80... | collective-permute-start | bytes 110600 | tf_op jit(solution)/shard_map/ppermute | solution.py:442
  16.6 29.4 %collective-permute-start.11 = (bf16[132,2880]{1,0:T(8,128)(2,1)}, bf16[132,2880]{1,0:T(8,128)(2,1)}, u32[]{:S(2)}, u32[]{:S(2)}) collective-permute-start(bf16[132,2880]{1,0:T(8,128)(2,1)} %slice.9), channel_id=1, source_target_pairs={{0,2},{1,3},{2,0},{3,1},{4,6},{5,7},{6,4},{7,5},{8,10},{9,11},{10,... | collective-permute-start | bytes 2280968 | tf_op jit(solution)/shard_map/ppermute | solution.py:465
  18.8 7.3 %copy-start.1 = (bf16[1,180,2880]{2,1,0:T(8,128)(2,1)S(1)}, bf16[1,180,2880]{2,1,0:T(8,128)(2,1)}, u32[]{:S(2)}) copy-start(bf16[1,180,2880]{2,1,0:T(8,128)(2,1)} %param.27) | copy-start | bytes 3110404
  19.5 5.3 %collective-permute-start.6 = (bf16[4,144,128]{2,1,0:T(8,128)(2,1)S(1)}, bf16[4,144,128]{2,1,0:T(8,128)(2,1)S(1)}, u32[]{:S(2)}, u32[]{:S(2)}) collective-permute-start(bf16[4,144,128]{2,1,0:T(8,128)(2,1)S(1)} %pad_maximum_fusion.1.refs_0_), channel_id=1, source_target_pairs={{0,8},{8,0},{16,24},{24,16},{32,40},{40,32},{48,56},{56,48},{64,72... | collective-permute-start | bytes 442376 | tf_op jit(solution)/shard_map/ppermute | solution.py:442
  21.7 12.0 %collective-permute-start.5 = (bf16[4,144,128]{2,1,0:T(8,128)(2,1)S(1)}, bf16[4,144,128]{2,1,0:T(8,128)(2,1)}, u32[]{:S(2)}, u32[]{:S(2)}) collective-permute-start(bf16[4,144,128]{2,1,0:T(8,128)(2,1)S(1)} %pad_maximum_fusion.1.refs_0_), channel_id=1, source_target_pairs={{0,192},{8,200},{16,208},{24,216},{32,224},{40,232},{48,240},{56,2... | collective-permute-start | bytes 442376 | tf_op jit(solution)/shard_map/ppermute | solution.py:442
  24.3 9.5 %collective-permute-start.4 = (bf16[4,144,128]{2,1,0:T(8,128)(2,1)S(1)}, bf16[4,144,128]{2,1,0:T(8,128)(2,1)}, u32[]{:S(2)}, u32[]{:S(2)}) collective-permute-start(bf16[4,144,128]{2,1,0:T(8,128)(2,1)S(1)} %pad_maximum_fusion.1.refs_0_), channel_id=1, source_target_pairs={{0,128},{8,136},{16,144},{24,152},{32,160},{40,168},{48,176},{56,1... | collective-permute-start | bytes 442376 | tf_op jit(solution)/shard_map/ppermute | solution.py:442
  25.5 9.4 %collective-permute-start.3 = (bf16[4,144,128]{2,1,0:T(8,128)(2,1)S(1)}, bf16[4,144,128]{2,1,0:T(8,128)(2,1)}, u32[]{:S(2)}, u32[]{:S(2)}) collective-permute-start(bf16[4,144,128]{2,1,0:T(8,128)(2,1)S(1)} %pad_maximum_fusion.1.refs_0_), channel_id=1, source_target_pairs={{0,64},{8,72},{16,80},{24,88},{32,96},{40,104},{48,112},{56,120},{... | collective-permute-start | bytes 442376 | tf_op jit(solution)/shard_map/ppermute | solution.py:442
  26.1 3.6 %copy-start.16 = (s32[128]{0:T(128)S(1)}, s32[128]{0:T(128)}, u32[]{:S(2)}) copy-start(s32[128]{0:T(128)} %pos_ref.7) | copy-start | bytes 1540
  26.1 3.6 %copy-start.19 = (f32[8]{0:T(128)S(1)}, f32[8]{0:T(128)}, u32[]{:S(2)}) copy-start(f32[8]{0:T(128)} %sink_ref.1) | copy-start | bytes 100
  27.3 12.9 %copy-start.4 = (bf16[512,2880]{0,1:T(8,128)(2,1)S(1)}, bf16[512,2880]{0,1:T(8,128)(2,1)}, u32[]{:S(2)}) copy-start(bf16[512,2880]{0,1:T(8,128)(2,1)} %param.21) | copy-start | bytes 8847364
  34.8 5.4 %collective-permute-start.8 = (bf16[4,144,128]{2,1,0:T(8,128)(2,1)}, bf16[4,144,128]{2,1,0:T(8,128)(2,1)S(1)}, u32[]{:S(2)}, u32[]{:S(2)}) collective-permute-start(bf16[4,144,128]{2,1,0:T(8,128)(2,1)} %collective-permute-done.3.refs_0_), channel_id=1, source_target_pairs={{0,8},{8,0},{16,24},{24,16},{32,40},{40,32},{48,56},{56,48},{64,72... | collective-permute-start | bytes 442376 | tf_op jit(solution)/shard_map/ppermute | solution.py:442
  35.3 4.9 %collective-permute-start.9 = (bf16[4,144,128]{2,1,0:T(8,128)(2,1)}, bf16[4,144,128]{2,1,0:T(8,128)(2,1)S(1)}, u32[]{:S(2)}, u32[]{:S(2)}) collective-permute-start(bf16[4,144,128]{2,1,0:T(8,128)(2,1)} %collective-permute-done.4.refs_1_), channel_id=1, source_target_pairs={{0,8},{8,0},{16,24},{24,16},{32,40},{40,32},{48,56},{56,48},{64,72... | collective-permute-start | bytes 442376 | tf_op jit(solution)/shard_map/ppermute | solution.py:442
  35.3 4.9 %collective-permute-start.10 = (bf16[4,144,128]{2,1,0:T(8,128)(2,1)}, bf16[4,144,128]{2,1,0:T(8,128)(2,1)S(1)}, u32[]{:S(2)}, u32[]{:S(2)}) collective-permute-start(bf16[4,144,128]{2,1,0:T(8,128)(2,1)} %collective-permute-done.5.refs_2_), channel_id=1, source_target_pairs={{0,8},{8,0},{16,24},{24,16},{32,40},{40,32},{48,56},{56,48},{64,72... | collective-permute-start | bytes 442376 | tf_op jit(solution)/shard_map/ppermute | solution.py:442
  46.0 17.1 %copy-start.12 = (bf16[128,384]{1,0:T(8,128)(2,1)S(1)}, bf16[128,384]{1,0:T(8,128)(2,1)}, u32[]{:S(2)}) copy-start(bf16[128,384]{1,0:T(8,128)(2,1)} %copy-done.11) | copy-start | bytes 294916
  46.0 17.1 %all-to-all-start = ((bf16[8,128,384]{2,1,0:T(8,128)(2,1)}), bf16[8,128,384]{2,1,0:T(8,128)(2,1)S(1)}, u32[]{:S(2)}, u32[]{:S(2)}) async-start(bf16[8,128,384]{2,1,0:T(8,128)(2,1)} %copy-done.2), calls=%async_computation | async-start | bytes 1572864 | tf_op jit(solution)/shard_map/all_to_all | solution.py:398
  50.6 39.7 %collective-permute-start.12 = (bf16[228,2880]{1,0:T(8,128)(2,1)}, bf16[228,2880]{1,0:T(8,128)(2,1)}, u32[]{:S(2)}, u32[]{:S(2)}) collective-permute-start(bf16[228,2880]{1,0:T(8,128)(2,1)} %pad_maximum_fusion), channel_id=1, source_target_pairs={{0,2},{1,3},{2,0},{3,1},{4,6},{5,7},{6,4},{7,5},{8,10},{9,11},{10,... | collective-permute-start | bytes 3939848 | tf_op jit(solution)/shard_map/ppermute | solution.py:477
  65.0 31.0 %all-to-all-start.1 = ((bf16[32,24,384]{2,1,0:T(8,128)(2,1)}), bf16[32,24,384]{2,1,0:T(8,128)(2,1)S(1)}, u32[]{:S(2)}, u32[]{:S(2)}) async-start(bf16[32,24,384]{2,1,0:T(8,128)(2,1)} %bitcast.17), calls=%async_computation.1 | async-start | bytes 1179648 | tf_op jit(solution)/shard_map/all_to_all | solution.py:398
  96.3 31.2 %copy-start.6 = (bf16[1,2880,180]{1,2,0:T(8,128)(2,1)S(1)}, bf16[1,2880,180]{1,2,0:T(8,128)(2,1)}, u32[]{:S(2)}) copy-start(bf16[1,2880,180]{1,2,0:T(8,128)(2,1)} %param.25) | copy-start | bytes 3110404
  164.6 27.5 %copy-start.8 = (bf16[384,768]{1,0:T(8,128)(2,1)S(1)}, bf16[384,768]{1,0:T(8,128)(2,1)}, u32[]{:S(2)}) copy-start(bf16[384,768]{1,0:T(8,128)(2,1)} %copy-done.7) | copy-start | bytes 1769476
  164.6 27.5 %copy-start.14 = (bf16[128,384]{1,0:T(8,128)(2,1)S(1)}, bf16[128,384]{1,0:T(8,128)(2,1)}, u32[]{:S(2)}) copy-start(bf16[128,384]{1,0:T(8,128)(2,1)} %copy-done.13) | copy-start | bytes 294916
  (11 other events, 11.5 us)

commit v5 on v4

--- a/solution.py
+++ b/solution.py
@@ -454,9 +454,8 @@
     prepared = prepare(
         experts, slots, member, expert_ids.T, expert_weights.T, tokens.T, norm_moe
     )
-    *planes, top_row, mixed, gather_table, combine_table, own_tokens, own_gain, late = (
-        lax.optimization_barrier((*planes, *carried, *prepared, late))
-    )
+    gather_table, combine_table, own_tokens, own_gain = prepared
+    *planes, top_row, mixed, late = lax.optimization_barrier((*planes, *carried, late))
     planes_far = [moved(plane, 0, 0, 1) for plane in planes]
     carried = call(middle_attention_kernel, state, [SMEM] + [VMEM] * 6)(
         positions, queries, top_row, mixed, *planes

time: 204 us -> 207 us (1.015)
  local copies, waits for them, and re-layouts: 7.66 us -> 12.4 us
    unnamed x40 -> x54, local copies, waits for them, and re-layouts: 6.47 us -> 12.1 us
    ppermute x1, waiting for transfers between devices: 13.5 us -> 8.72 us  [local(): far_late = lax.ppermute(late, 'exp', swap)]
    ppermute x10, waiting for transfers between devices: 1.1 us -> 5.5 us  [moved(): return lax.ppermute(block, 'ctx', route)]
  transfers between devices with their start and end apart: 15 -> 15, of which waited for: 4 -> 7; matrix products, arithmetic and copies ran while one was open for 1% -> 1% of each run, Pallas kernels for 9% -> 8%
where the time goes in v5:
time: 207 us; the launch traced here: 206 us
  blocking collectives  98.4 us (48%)
  starting transfers between devices  38.3 us (19%)
  waiting for transfers between devices  30.3 us (15%)
  Pallas kernels  24.8 us (12%)
  local copies, waits for them, and re-layouts  12.4 us (6%)
    all_to_all x4, blocking collectives, exchange(): lax.all_to_all(block, axis, split_axis=0, concat_axis=0, tiled=True, axis...  98.4 us
    all_to_all x2, starting transfers between devices, exchange(): lax.all_to_all(block, axis, split_axis=0, concat_axis=0, tiled=True, axis...  17.7 us
    ppermute x10, starting transfers between devices, moved(): return lax.ppermute(block, 'ctx', route)  16.6 us
    all_to_all x2, waiting for transfers between devices, exchange(): lax.all_to_all(block, axis, split_axis=0, concat_axis=0, tiled=True, axis...  16.1 us
    unnamed x54, local copies, waits for them, and re-layouts  12.1 us
    ppermute x1, waiting for transfers between devices, local(): far_late = lax.ppermute(late, 'exp', swap)  8.72 us
    pallas_call x1, Pallas kernels, run_experts(): pl.pallas_call(functools.partial(expert_kernel, width), out_shape=shape(e...  6.07 us
    ppermute x10, waiting for transfers between devices, moved(): return lax.ppermute(block, 'ctx', route)  5.5 us
  transfers between devices with their start and end apart: 15, of which 7 were waited for; matrix products, arithmetic and copies ran while one was open for 1% of the time, Pallas kernels for 8%

profile of v5, /device:TPU:1, one launch (start us, length us, event | category | flops | bytes accessed | tf_op | source)
XLA Modules:
  0.0 206.3 jit_solution(11003258312395819964)
XLA Ops:
  0.6 2.2 %collective-permute-start.7 = (bf16[180,2880]{1,0:T(8,128)(2,1)}, bf16[180,2880]{1,0:T(8,128)(2,1)S(1)}, u32[]{:S(2)}, u32[]{:S(2)}) collective-permute-start(bf16[180,2880]{1,0:T(8,128)(2,1)} %bitcast.34), channel_id=1, source_target_pairs={{0,2},{1,3},{2,0},{3,1},{4,6},{5,7},{6,4},{7,5},{8,10},{9,11},{10,... | collective-permute-start | bytes 3110408 | tf_op jit(solution)/shard_map/ppermute | solution.py:434
  2.9 3.5 %shard_map.149 = (bf16[128,2880]{1,0:T(8,128)(2,1)S(1)}, bf16[144,128]{1,0:T(8,128)(2,1)S(1)}) custom-call(s32[128]{0:T(128)} %pos_ref.7, bf16[2880,128]{1,0:T(8,128)(2,1)} %bitcast.30, f32[2880]{0:T(1024)} %gain_hbm.1, bf16[64,2880]{1,0:T(8,128)(2,1)} %bitcast.43, bf16[64,2880]{1,0:T(8,128)(2,1)} %bitcast.44), custom_call_target="tpu_custom_call" | custom-call | tf_op jit(solution)/shard_map/pallas_call | solution.py:96
  6.3 6.1 %collective-permute-start.2 = (bf16[144,128]{1,0:T(8,128)(2,1)S(1)}, bf16[144,128]{1,0:T(8,128)(2,1)S(1)}, u32[]{:S(2)}, u32[]{:S(2)}) collective-permute-start(bf16[144,128]{1,0:T(8,128)(2,1)S(1)} %get-tuple-element.33), channel_id=1, source_target_pairs={{0,48},{8,56},{16,0},{24,8},{32,16},{40,24},{48,32},{56,40},{64,11... | collective-permute-start | bytes 110600 | tf_op jit(solution)/shard_map/ppermute | solution.py:442
  13.4 2.3 %collective-permute-start = (bf16[144,128]{1,0:T(8,128)(2,1)S(1)}, bf16[144,128]{1,0:T(8,128)(2,1)S(1)}, u32[]{:S(2)}, u32[]{:S(2)}) collective-permute-start(bf16[144,128]{1,0:T(8,128)(2,1)S(1)} %get-tuple-element.33), channel_id=1, source_target_pairs={{0,16},{8,24},{16,32},{24,40},{32,48},{40,56},{48,0},{56,8},{64,80... | collective-permute-start | bytes 110600 | tf_op jit(solution)/shard_map/ppermute | solution.py:442
  16.1 1.8 copy-done.3
  19.2 2.5 %collective-permute-start.6 = (bf16[4,144,128]{2,1,0:T(8,128)(2,1)S(1)}, bf16[4,144,128]{2,1,0:T(8,128)(2,1)S(1)}, u32[]{:S(2)}, u32[]{:S(2)}) collective-permute-start(bf16[4,144,128]{2,1,0:T(8,128)(2,1)S(1)} %pad_maximum_fusion.1.refs_0_), channel_id=1, source_target_pairs={{0,8},{8,0},{16,24},{24,16},{32,40},{40,32},{48,56},{56,48},{64,72... | collective-permute-start | bytes 442376 | tf_op jit(solution)/shard_map/ppermute | solution.py:442
  21.7 2.6 %collective-permute-start.5 = (bf16[4,144,128]{2,1,0:T(8,128)(2,1)S(1)}, bf16[4,144,128]{2,1,0:T(8,128)(2,1)S(1)}, u32[]{:S(2)}, u32[]{:S(2)}) collective-permute-start(bf16[4,144,128]{2,1,0:T(8,128)(2,1)S(1)} %pad_maximum_fusion.1.refs_0_), channel_id=1, source_target_pairs={{0,192},{8,200},{16,208},{24,216},{32,224},{40,232},{48,240},{56,2... | collective-permute-start | bytes 442376 | tf_op jit(solution)/shard_map/ppermute | solution.py:442
  25.4 1.2 pad_maximum_fusion
  26.6 3.1 %shard_map.151 = (f32[1024,1]{1,0:T(8,128)S(1)}, f32[1024,128]{1,0:T(8,128)S(1)}) custom-call(s32[128]{0:T(128)S(1)} %copy-done.21, f32[8]{0:T(128)S(1)} %copy-done.26, bf16[1024,128]{1,0:T(8,128)(2,1)S(1)} %shard_map.150.query_ref, bf16[4,144,128]{2,1,0:T(8,128)(2,1)S(1)} %pad_maximum_fusion.1.refs_0_, bf16[4,144,128]{2,1,0:T(8,128)(2,1)S(1)} %collective-permute-done.6.refs_1_), custom_call_target="tpu_custom_call" | custom-call | tf_op jit(solution)/shard_map/pallas_call | solution.py:451
  31.0 3.8 %collective-permute-done.3.refs_0_ = bf16[4,144,128]{2,1,0:T(8,128)(2,1)S(1)} collective-permute-done((bf16[4,144,128]{2,1,0:T(8,128)(2,1)S(1)}, bf16[4,144,128]{2,1,0:T(8,128)(2,1)S(1)}, u32[]{:S(2)}, u32[]{:S(2)}) %collective-permute-start.3) | collective-permute-done | bytes 147488 | tf_op jit(solution)/shard_map/ppermute | solution.py:442
  35.7 3.8 %shard_map.152 = (f32[1024,1]{1,0:T(8,128)S(1)}, f32[1024,128]{1,0:T(8,128)S(1)}) custom-call(s32[128]{0:T(128)S(1)} %copy-done.21, bf16[1024,128]{1,0:T(8,128)(2,1)S(1)} %shard_map.150.query_ref, f32[1024,1]{1,0:T(8,128)S(1)} %get-tuple-element.41.old_top_ref, f32[1024,128]{1,0:T(8,128)S(1)} %get-tuple-element.42.old_mixed_ref, ...), custom_call_target="tpu_custom_call" | custom-call | tf_op jit(solution)/shard_map/pallas_call | solution.py:460
  39.6 4.9 %shard_map.153 = bf16[8,128,384]{2,1,0:T(8,128)(2,1)S(1)} custom-call(s32[128]{0:T(128)S(1)} %copy-done.21, bf16[1024,128]{1,0:T(8,128)(2,1)S(1)} %shard_map.150.query_ref, f32[1024,1]{1,0:T(8,128)S(1)} %get-tuple-element.48.old_top_ref, f32[1024,128]{1,0:T(8,128)S(1)} %get-tuple-element.49.old_mixed_ref, bf16[2880,512]{1,0:T(8,128)(2,1)S(1)} %bitcast.29, ...), custom_call_target="tpu_custom_call" | custom-call | tf_op jit(solution)/shard_map/pallas_call | solution.py:465
  46.4 4.3 %all-to-all-start = ((bf16[8,128,384]{2,1,0:T(8,128)(2,1)}), bf16[8,128,384]{2,1,0:T(8,128)(2,1)S(1)}, u32[]{:S(2)}, u32[]{:S(2)}) async-start(bf16[8,128,384]{2,1,0:T(8,128)(2,1)} %copy-done.2), calls=%async_computation | async-start | bytes 1572864 | tf_op jit(solution)/shard_map/all_to_all | solution.py:398
  50.7 1.5 collective-permute-start.12
  52.1 1.1 copy-done.5
  56.7 5.6 %all-to-all-done.parts_ref = bf16[8,128,384]{2,1,0:T(8,128)(2,1)S(1)} async-done(((bf16[8,128,384]{2,1,0:T(8,128)(2,1)}), bf16[8,128,384]{2,1,0:T(8,128)(2,1)S(1)}, u32[]{:S(2)}, u32[]{:S(2)}) %all-to-all-start) | async-done | bytes 786464 | tf_op jit(solution)/shard_map/all_to_all | solution.py:398
  67.4 13.4 %all-to-all-start.1 = ((bf16[32,24,384]{2,1,0:T(8,128)(2,1)}), bf16[32,24,384]{2,1,0:T(8,128)(2,1)S(1)}, u32[]{:S(2)}, u32[]{:S(2)}) async-start(bf16[32,24,384]{2,1,0:T(8,128)(2,1)} %bitcast.37), calls=%async_computation.1 | async-start | bytes 1179648 | tf_op jit(solution)/shard_map/all_to_all | solution.py:398
  80.8 8.7 %collective-permute-done.12.late_ref = bf16[228,2880]{1,0:T(8,128)(2,1)} collective-permute-done((bf16[228,2880]{1,0:T(8,128)(2,1)}, bf16[228,2880]{1,0:T(8,128)(2,1)}, u32[]{:S(2)}, u32[]{:S(2)}) %collective-permute-start.12) | collective-permute-done | bytes 1313312 | tf_op jit(solution)/shard_map/ppermute | solution.py:476
  89.5 10.5 %all-to-all-done.1 = bf16[32,24,384]{2,1,0:T(8,128)(2,1)S(1)} async-done(((bf16[32,24,384]{2,1,0:T(8,128)(2,1)}), bf16[32,24,384]{2,1,0:T(8,128)(2,1)S(1)}, u32[]{:S(2)}, u32[]{:S(2)}) %all-to-all-start.1) | async-done | bytes 589856 | tf_op jit(solution)/shard_map/all_to_all | solution.py:398
  100.3 31.4 %all_to_all.30.rows_in_ref = bf16[8,384,384]{2,1,0:T(8,128)(2,1)S(1)} all-to-all(bf16[8,384,384]{2,1,0:T(8,128)(2,1)S(1)} %bitcast.41), channel_id=1, replica_groups=mesh['ctx'=32,'exp'=8] {'exp'}, dimensions={0} | all-to-all | bytes 4718592 | tf_op jit(solution)/shard_map/all_to_all | solution.py:398
  131.7 6.1 %shard_map.156 = bf16[8,384,384]{2,1,0:T(8,128)(2,1)S(1)} custom-call(bf16[8,384,384]{2,1,0:T(8,128)(2,1)S(1)} %all_to_all.30.rows_in_ref, bf16[180,2880]{1,0:T(8,128)(2,1)S(1)} %bitcast.35, bf16[180,2880]{1,0:T(8,128)(2,1)S(1)} %bitcast.26, bf16[180,2880]{1,0:T(8,128)(2,1)S(1)} %bitcast.28, bf16[180,2880]{1,0:T(8,128)(2,1)S(1)} %copy-done.8, ...), custom_call_target="tpu_custom_call" | custom-call | tf_op jit(solution)/shard_map/pallas_call | solution.py:354
  137.8 30.5 %all_to_all.31.parts_ref = bf16[8,384,384]{2,1,0:T(8,128)(2,1)S(1)} all-to-all(bf16[8,384,384]{2,1,0:T(8,128)(2,1)S(1)} %shard_map.156), channel_id=1, replica_groups=mesh['ctx'=32,'exp'=8] {'exp'}, dimensions={0} | all-to-all | bytes 4718592 | tf_op jit(solution)/shard_map/all_to_all | solution.py:398
  168.5 27.1 %all_to_all.32 = bf16[32,24,384]{2,1,0:T(8,128)(2,1)S(1)} all-to-all(bf16[32,24,384]{2,1,0:T(8,128)(2,1)S(1)} %bitcast.33), channel_id=1, replica_groups=mesh['ctx'=32,'exp'=8] {'ctx'}, dimensions={0} | all-to-all | bytes 1179648 | tf_op jit(solution)/shard_map/all_to_all | solution.py:398
  196.1 9.4 %all_to_all.33.parts_ref = bf16[8,16,768]{2,1,0:T(8,128)(2,1)S(1)} all-to-all(bf16[8,16,768]{2,1,0:T(8,128)(2,1)S(1)} %bitcast.36), channel_id=1, replica_groups=mesh['ctx'=32,'exp'=8] {'exp'}, dimensions={0} | all-to-all | bytes 393216 | tf_op jit(solution)/shard_map/all_to_all | solution.py:398
  (80 shorter events, 18.2 us)
Async XLA Ops:
  0.6 15.0 %copy-start = (bf16[1,2880,180]{1,2,0:T(8,128)(2,1)S(1)}, bf16[1,2880,180]{1,2,0:T(8,128)(2,1)}, u32[]{:S(2)}) copy-start(bf16[1,2880,180]{1,2,0:T(8,128)(2,1)} %param.26) | copy-start | bytes 3110404
  0.6 38.9 %collective-permute-start.7 = (bf16[180,2880]{1,0:T(8,128)(2,1)}, bf16[180,2880]{1,0:T(8,128)(2,1)S(1)}, u32[]{:S(2)}, u32[]{:S(2)}) collective-permute-start(bf16[180,2880]{1,0:T(8,128)(2,1)} %bitcast.34), channel_id=1, source_target_pairs={{0,2},{1,3},{2,0},{3,1},{4,6},{5,7},{6,4},{7,5},{8,10},{9,11},{10,... | collective-permute-start | bytes 3110408 | tf_op jit(solution)/shard_map/ppermute | solution.py:434
  6.3 12.3 %collective-permute-start.2 = (bf16[144,128]{1,0:T(8,128)(2,1)S(1)}, bf16[144,128]{1,0:T(8,128)(2,1)S(1)}, u32[]{:S(2)}, u32[]{:S(2)}) collective-permute-start(bf16[144,128]{1,0:T(8,128)(2,1)S(1)} %get-tuple-element.33), channel_id=1, source_target_pairs={{0,48},{8,56},{16,0},{24,8},{32,16},{40,24},{48,32},{56,40},{64,11... | collective-permute-start | bytes 110600 | tf_op jit(solution)/shard_map/ppermute | solution.py:442
  12.4 6.7 %collective-permute-start.1 = (bf16[144,128]{1,0:T(8,128)(2,1)S(1)}, bf16[144,128]{1,0:T(8,128)(2,1)S(1)}, u32[]{:S(2)}, u32[]{:S(2)}) collective-permute-start(bf16[144,128]{1,0:T(8,128)(2,1)S(1)} %get-tuple-element.33), channel_id=1, source_target_pairs={{0,32},{8,40},{16,48},{24,56},{32,0},{40,8},{48,16},{56,24},{64,96... | collective-permute-start | bytes 110600 | tf_op jit(solution)/shard_map/ppermute | solution.py:442
  13.4 5.7 %collective-permute-start = (bf16[144,128]{1,0:T(8,128)(2,1)S(1)}, bf16[144,128]{1,0:T(8,128)(2,1)S(1)}, u32[]{:S(2)}, u32[]{:S(2)}) collective-permute-start(bf16[144,128]{1,0:T(8,128)(2,1)S(1)} %get-tuple-element.33), channel_id=1, source_target_pairs={{0,16},{8,24},{16,32},{24,40},{32,48},{40,56},{48,0},{56,8},{64,80... | collective-permute-start | bytes 110600 | tf_op jit(solution)/shard_map/ppermute | solution.py:442
  15.7 29.7 %collective-permute-start.11 = (bf16[132,2880]{1,0:T(8,128)(2,1)S(1)}, bf16[132,2880]{1,0:T(8,128)(2,1)S(1)}, u32[]{:S(2)}, u32[]{:S(2)}) collective-permute-start(bf16[132,2880]{1,0:T(8,128)(2,1)S(1)} %slice.9), channel_id=1, source_target_pairs={{0,2},{1,3},{2,0},{3,1},{4,6},{5,7},{6,4},{7,5},{8,10},{9,11},{10,... | collective-permute-start | bytes 2280968 | tf_op jit(solution)/shard_map/ppermute | solution.py:464
  18.0 7.5 %copy-start.1 = (bf16[1,180,2880]{2,1,0:T(8,128)(2,1)S(1)}, bf16[1,180,2880]{2,1,0:T(8,128)(2,1)}, u32[]{:S(2)}) copy-start(bf16[1,180,2880]{2,1,0:T(8,128)(2,1)} %param.27) | copy-start | bytes 3110404
  19.2 5.6 %collective-permute-start.6 = (bf16[4,144,128]{2,1,0:T(8,128)(2,1)S(1)}, bf16[4,144,128]{2,1,0:T(8,128)(2,1)S(1)}, u32[]{:S(2)}, u32[]{:S(2)}) collective-permute-start(bf16[4,144,128]{2,1,0:T(8,128)(2,1)S(1)} %pad_maximum_fusion.1.refs_0_), channel_id=1, source_target_pairs={{0,8},{8,0},{16,24},{24,16},{32,40},{40,32},{48,56},{56,48},{64,72... | collective-permute-start | bytes 442376 | tf_op jit(solution)/shard_map/ppermute | solution.py:442
  21.7 8.8 %collective-permute-start.5 = (bf16[4,144,128]{2,1,0:T(8,128)(2,1)S(1)}, bf16[4,144,128]{2,1,0:T(8,128)(2,1)S(1)}, u32[]{:S(2)}, u32[]{:S(2)}) collective-permute-start(bf16[4,144,128]{2,1,0:T(8,128)(2,1)S(1)} %pad_maximum_fusion.1.refs_0_), channel_id=1, source_target_pairs={{0,192},{8,200},{16,208},{24,216},{32,224},{40,232},{48,240},{56,2... | collective-permute-start | bytes 442376 | tf_op jit(solution)/shard_map/ppermute | solution.py:442
  24.3 6.7 %collective-permute-start.4 = (bf16[4,144,128]{2,1,0:T(8,128)(2,1)S(1)}, bf16[4,144,128]{2,1,0:T(8,128)(2,1)S(1)}, u32[]{:S(2)}, u32[]{:S(2)}) collective-permute-start(bf16[4,144,128]{2,1,0:T(8,128)(2,1)S(1)} %pad_maximum_fusion.1.refs_0_), channel_id=1, source_target_pairs={{0,128},{8,136},{16,144},{24,152},{32,160},{40,168},{48,176},{56,1... | collective-permute-start | bytes 442376 | tf_op jit(solution)/shard_map/ppermute | solution.py:442
  24.8 9.9 %collective-permute-start.3 = (bf16[4,144,128]{2,1,0:T(8,128)(2,1)S(1)}, bf16[4,144,128]{2,1,0:T(8,128)(2,1)S(1)}, u32[]{:S(2)}, u32[]{:S(2)}) collective-permute-start(bf16[4,144,128]{2,1,0:T(8,128)(2,1)S(1)} %pad_maximum_fusion.1.refs_0_), channel_id=1, source_target_pairs={{0,64},{8,72},{16,80},{24,88},{32,96},{40,104},{48,112},{56,120},{... | collective-permute-start | bytes 442376 | tf_op jit(solution)/shard_map/ppermute | solution.py:442
  25.4 14.2 %copy-start.4 = (bf16[512,2880]{0,1:T(8,128)(2,1)S(1)}, bf16[512,2880]{0,1:T(8,128)(2,1)}, u32[]{:S(2)}) copy-start(bf16[512,2880]{0,1:T(8,128)(2,1)} %param.21) | copy-start | bytes 8847364
  34.7 4.9 %collective-permute-start.8 = (bf16[4,144,128]{2,1,0:T(8,128)(2,1)S(1)}, bf16[4,144,128]{2,1,0:T(8,128)(2,1)S(1)}, u32[]{:S(2)}, u32[]{:S(2)}) collective-permute-start(bf16[4,144,128]{2,1,0:T(8,128)(2,1)S(1)} %collective-permute-done.3.refs_0_), channel_id=1, source_target_pairs={{0,8},{8,0},{16,24},{24,16},{32,40},{40,32},{48,56},{56,48},{64,72... | collective-permute-start | bytes 442376 | tf_op jit(solution)/shard_map/ppermute | solution.py:442
  35.2 4.4 %collective-permute-start.9 = (bf16[4,144,128]{2,1,0:T(8,128)(2,1)S(1)}, bf16[4,144,128]{2,1,0:T(8,128)(2,1)S(1)}, u32[]{:S(2)}, u32[]{:S(2)}) collective-permute-start(bf16[4,144,128]{2,1,0:T(8,128)(2,1)S(1)} %collective-permute-done.4.refs_1_), channel_id=1, source_target_pairs={{0,8},{8,0},{16,24},{24,16},{32,40},{40,32},{48,56},{56,48},{64,72... | collective-permute-start | bytes 442376 | tf_op jit(solution)/shard_map/ppermute | solution.py:442
  35.2 4.4 %collective-permute-start.10 = (bf16[4,144,128]{2,1,0:T(8,128)(2,1)S(1)}, bf16[4,144,128]{2,1,0:T(8,128)(2,1)S(1)}, u32[]{:S(2)}, u32[]{:S(2)}) collective-permute-start(bf16[4,144,128]{2,1,0:T(8,128)(2,1)S(1)} %collective-permute-done.5.refs_2_), channel_id=1, source_target_pairs={{0,8},{8,0},{16,24},{24,16},{32,40},{40,32},{48,56},{56,48},{64,72... | collective-permute-start | bytes 442376 | tf_op jit(solution)/shard_map/ppermute | solution.py:442
  45.5 6.7 %copy-start.23 = (f32[128,4]{0,1:T(4,128)S(1)}, f32[128,4]{0,1:T(4,128)}, u32[]{:S(2)}) copy-start(f32[128,4]{0,1:T(4,128)} %param.24) | copy-start | bytes 6148
  46.4 15.9 %all-to-all-start = ((bf16[8,128,384]{2,1,0:T(8,128)(2,1)}), bf16[8,128,384]{2,1,0:T(8,128)(2,1)S(1)}, u32[]{:S(2)}, u32[]{:S(2)}) async-start(bf16[8,128,384]{2,1,0:T(8,128)(2,1)} %copy-done.2), calls=%async_computation | async-start | bytes 1572864 | tf_op jit(solution)/shard_map/all_to_all | solution.py:398
  50.7 38.9 %collective-permute-start.12 = (bf16[228,2880]{1,0:T(8,128)(2,1)}, bf16[228,2880]{1,0:T(8,128)(2,1)}, u32[]{:S(2)}, u32[]{:S(2)}) collective-permute-start(bf16[228,2880]{1,0:T(8,128)(2,1)} %pad_maximum_fusion), channel_id=1, source_target_pairs={{0,2},{1,3},{2,0},{3,1},{4,6},{5,7},{6,4},{7,5},{8,10},{9,11},{10,... | collective-permute-start | bytes 3939848 | tf_op jit(solution)/shard_map/ppermute | solution.py:476
  67.4 32.6 %all-to-all-start.1 = ((bf16[32,24,384]{2,1,0:T(8,128)(2,1)}), bf16[32,24,384]{2,1,0:T(8,128)(2,1)S(1)}, u32[]{:S(2)}, u32[]{:S(2)}) async-start(bf16[32,24,384]{2,1,0:T(8,128)(2,1)} %bitcast.37), calls=%async_computation.1 | async-start | bytes 1179648 | tf_op jit(solution)/shard_map/all_to_all | solution.py:398
  100.3 31.4 %copy-start.6 = (bf16[1,2880,180]{1,2,0:T(8,128)(2,1)S(1)}, bf16[1,2880,180]{1,2,0:T(8,128)(2,1)}, u32[]{:S(2)}) copy-start(bf16[1,2880,180]{1,2,0:T(8,128)(2,1)} %param.25) | copy-start | bytes 3110404
  100.3 31.4 %copy-start.8 = (bf16[180,2880]{1,0:T(8,128)(2,1)S(1)}, bf16[180,2880]{1,0:T(8,128)(2,1)}, u32[]{:S(2)}) copy-start(bf16[180,2880]{1,0:T(8,128)(2,1)} %copy-done.7) | copy-start | bytes 3110404
  100.3 31.4 %copy-start.10 = (bf16[132,2880]{1,0:T(8,128)(2,1)S(1)}, bf16[132,2880]{1,0:T(8,128)(2,1)}, u32[]{:S(2)}) copy-start(bf16[132,2880]{1,0:T(8,128)(2,1)} %copy-done.9) | copy-start | bytes 2280964
  168.2 27.4 %copy-start.13 = (f32[128,384]{1,0:T(8,128)S(1)}, f32[128,384]{1,0:T(8,128)}, u32[]{:S(2)}) copy-start(f32[128,384]{1,0:T(8,128)} %copy-done.12) | copy-start | bytes 589828
  168.2 27.4 %copy-start.17 = (bf16[128,384]{1,0:T(8,128)(2,1)S(1)}, bf16[128,384]{1,0:T(8,128)(2,1)}, u32[]{:S(2)}) copy-start(bf16[128,384]{1,0:T(8,128)(2,1)} %copy-done.16) | copy-start | bytes 294916
  (18 other events, 33.5 us)

commit v6 on v4

--- a/solution.py
+++ b/solution.py
@@ -207,10 +207,12 @@
     for _ in range(1):
         keys = []
         vals = []
+        limits = []
         for kv_ref, block in [(ref, i) for ref in kv_refs for i in range(ref.shape[0])]:
             marks = kv_ref[block, rows:rows + EXTRA, :].astype(F32)
             base = marks[0:1, 0:1] * 128.0 + marks[0:1, 1:2]
             hidden = jnp.where(base <= mine, 0.0, -1e30)
+            limits.append(mine - base)
             kv = kv_ref[block, :rows, :].astype(F32)
             keys.append(jnp.where(key_side, kv, jnp.where(flag_lane, hidden, 0.0)).astype(BF16))
             vals.append(jnp.where(key_side, 1.0, kv).astype(BF16))
@@ -218,11 +220,14 @@
         vals = jnp.concatenate(vals, axis=0)
         scores = dot(query_ref[...], keys, ((1,), (1,)))
         if diagonal:
-            own = scores[:, :rows]
-            query_row = lax.broadcasted_iota(jnp.int32, own.shape, 0) % rows
-            key_row = lax.broadcasted_iota(jnp.int32, own.shape, 1)
-            own = jnp.where(key_row <= query_row, own, -1e30)
-            scores = jnp.concatenate([own, scores[:, rows:]], axis=1)
+            parts = []
+            for block in range(kv_refs[0].shape[0]):
+                part = scores[:, block * rows:(block + 1) * rows]
+                query_row = lax.broadcasted_iota(jnp.int32, part.shape, 0) % rows
+                key_row = lax.broadcasted_iota(jnp.int32, part.shape, 1)
+                ahead = (key_row - query_row).astype(F32)
+                parts.append(jnp.where(ahead <= limits[block], part, -1e30))
+            scores = jnp.concatenate(parts + [scores[:, len(parts) * rows:]], axis=1)
         top_new = jnp.maximum(top, jnp.max(scores, axis=1, keepdims=True))
         probs = jnp.exp(scores - top_new).astype(BF16)
         mixed = mixed * jnp.exp(top - top_new) + dot(probs, vals)
@@ -442,9 +447,14 @@
         return lax.ppermute(block, "ctx", route)
 
     queries = call(query_kernel, shape((heads * rows, 2 * HEAD_WIDTH)), [VMEM, VMEM])(normed, w_query)
-    stops = [moved(payload, 0, z, 0) for z in range(1, 4)]
-    *stops, queries = lax.optimization_barrier((*stops, queries))
-    column = jnp.stack([payload] + stops)
+    lines = [
+        [i for i in range(ctx_count) if i // 8 == x and i % 2 == core]
+        for x in range(ctx_count // 8)
+        for core in range(2)
+    ]
+    copies = jnp.broadcast_to(payload[None], (len(lines[0]),) + payload.shape)
+    column = exchange(copies, "ctx", lines)
+    column, queries = lax.optimization_barrier((column, queries))
     column_far = moved(column, 0, 0, 1)
     planes = [moved(column, x, 0, 0) for x in range(1, 4)]
     state = [shape((heads * rows, 1), F32), shape((heads * rows, 2 * HEAD_WIDTH), F32)]

time: 204 us -> 203 us (level)
  starting transfers between devices: 36.6 us -> 31.6 us
  waiting for transfers between devices: 31.4 us -> 35.7 us
    ppermute x10 -> x7, starting transfers between devices: 16.3 us -> 7.31 us  [moved(): return lax.ppermute(block, 'ctx', route)]
    all_to_all x2 -> x3, starting transfers between devices: 16.4 us -> 20.3 us  [exchange(): lax.all_to_all(block, axis, split_axis=0, concat_axis=0, tiled=True, axis...]
    ppermute x1, waiting for transfers between devices: 13.5 us -> 17.1 us  [local(): far_late = lax.ppermute(late, 'exp', swap)]
    all_to_all x2 -> x3, waiting for transfers between devices: 16.8 us -> 17.1 us  [exchange(): lax.all_to_all(block, axis, split_axis=0, concat_axis=0, tiled=True, axis...]
  transfers between devices with their start and end apart: 15 -> 13, of which waited for: 4 -> 5; matrix products, arithmetic and copies ran while one was open for 1% -> 1% of each run, Pallas kernels for 9% -> 9%
where the time goes in v6:
time: 203 us
  blocking collectives  98.2 us (48%)
  waiting for transfers between devices  35.7 us (18%)
  starting transfers between devices  31.6 us (16%)
  Pallas kernels  26.8 us (13%)
  local copies, waits for them, and re-layouts  8.36 us (4%)
    all_to_all x4, blocking collectives, exchange(): lax.all_to_all(block, axis, split_axis=0, concat_axis=0, tiled=True, axis...  98.2 us
    all_to_all x3, starting transfers between devices, exchange(): lax.all_to_all(block, axis, split_axis=0, concat_axis=0, tiled=True, axis...  20.3 us
    all_to_all x3, waiting for transfers between devices, exchange(): lax.all_to_all(block, axis, split_axis=0, concat_axis=0, tiled=True, axis...  17.1 us
    ppermute x1, waiting for transfers between devices, local(): far_late = lax.ppermute(late, 'exp', swap)  17.1 us
    ppermute x7, starting transfers between devices, moved(): return lax.ppermute(block, 'ctx', route)  7.31 us
    pallas_call x1, Pallas kernels, run_experts(): pl.pallas_call(functools.partial(expert_kernel, width), out_shape=shape(e...  6.62 us
    unnamed x40, local copies, waits for them, and re-layouts  6.49 us
    pallas_call x1, Pallas kernels, local(): call(last_attention_kernel, shape((exp_count, rows, CHUNK)), [SMEM] + [VM...  4.84 us
  transfers between devices with their start and end apart: 13, of which 5 were waited for; matrix products, arithmetic and copies ran while one was open for 1% of the time, Pallas kernels for 9%

profile of v6, /device:TPU:1, one launch (start us, length us, event | category | flops | bytes accessed | tf_op | source)
XLA Modules:
  0.0 202.7 jit_solution(9943081528959078375)
XLA Ops:
  0.6 2.2 %collective-permute-start.4 = (bf16[180,2880]{1,0:T(8,128)(2,1)}, bf16[180,2880]{1,0:T(8,128)(2,1)}, u32[]{:S(2)}, u32[]{:S(2)}) collective-permute-start(bf16[180,2880]{1,0:T(8,128)(2,1)} %bitcast.30), channel_id=1, source_target_pairs={{0,2},{1,3},{2,0},{3,1},{4,6},{5,7},{6,4},{7,5},{8,10},{9,11},{10,... | collective-permute-start | bytes 3110408 | tf_op jit(solution)/shard_map/ppermute | solution.py:439
  2.9 3.5 %shard_map.149 = (bf16[128,2880]{1,0:T(8,128)(2,1)S(1)}, bf16[144,128]{1,0:T(8,128)(2,1)S(1)}) custom-call(s32[128]{0:T(128)} %pos_ref.7, bf16[2880,128]{1,0:T(8,128)(2,1)} %bitcast.26, f32[2880]{0:T(1024)} %gain_hbm.1, bf16[64,2880]{1,0:T(8,128)(2,1)} %bitcast.37, bf16[64,2880]{1,0:T(8,128)(2,1)} %bitcast.38), custom_call_target="tpu_custom_call" | custom-call | tf_op jit(solution)/shard_map/pallas_call | solution.py:96
  7.0 8.2 %all-to-all-start = ((bf16[4,144,128]{2,1,0:T(8,128)(2,1)}), bf16[4,144,128]{2,1,0:T(8,128)(2,1)S(1)}, u32[]{:S(2)}, u32[]{:S(2)}) async-start(bf16[4,144,128]{2,1,0:T(8,128)(2,1)} %broadcast_in_dim.6), calls=%async_computation | async-start | bytes 294912 | tf_op jit(solution)/shard_map/all_to_all | solution.py:403
  16.4 1.8 copy-done.3
  18.9 3.7 %all-to-all-done.refs_0_ = bf16[4,144,128]{2,1,0:T(8,128)(2,1)S(1)} async-done(((bf16[4,144,128]{2,1,0:T(8,128)(2,1)}), bf16[4,144,128]{2,1,0:T(8,128)(2,1)S(1)}, u32[]{:S(2)}, u32[]{:S(2)}) %all-to-all-start) | async-done | bytes 147488 | tf_op jit(solution)/shard_map/all_to_all | solution.py:403
  22.6 3.1 %collective-permute-start.3 = (bf16[4,144,128]{2,1,0:T(8,128)(2,1)S(1)}, bf16[4,144,128]{2,1,0:T(8,128)(2,1)S(1)}, u32[]{:S(2)}, u32[]{:S(2)}) collective-permute-start(bf16[4,144,128]{2,1,0:T(8,128)(2,1)S(1)} %all-to-all-done.refs_0_), channel_id=1, source_target_pairs={{0,8},{8,0},{16,24},{24,16},{32,40},{40,32},{48,56},{56,48},{64,72... | collective-permute-start | bytes 442376 | tf_op jit(solution)/shard_map/ppermute | solution.py:447
  25.7 2.6 %collective-permute-start.2 = (bf16[4,144,128]{2,1,0:T(8,128)(2,1)S(1)}, bf16[4,144,128]{2,1,0:T(8,128)(2,1)}, u32[]{:S(2)}, u32[]{:S(2)}) collective-permute-start(bf16[4,144,128]{2,1,0:T(8,128)(2,1)S(1)} %all-to-all-done.refs_0_), channel_id=1, source_target_pairs={{0,192},{8,200},{16,208},{24,216},{32,224},{40,232},{48,240},{56,2... | collective-permute-start | bytes 442376 | tf_op jit(solution)/shard_map/ppermute | solution.py:447
  29.6 1.2 pad_maximum_fusion
  34.1 3.2 %shard_map.151 = (f32[1024,1]{1,0:T(8,128)S(1)}, f32[1024,128]{1,0:T(8,128)S(1)}) custom-call(s32[128]{0:T(128)S(1)} %copy-done.16, f32[8]{0:T(128)S(1)} %copy-done.19, bf16[1024,128]{1,0:T(8,128)(2,1)S(1)} %shard_map.150.query_ref, bf16[4,144,128]{2,1,0:T(8,128)(2,1)S(1)} %all-to-all-done.refs_0_, bf16[4,144,128]{2,1,0:T(8,128)(2,1)S(1)} %copy-done.10), custom_call_target="tpu_custom_call" | custom-call | tf_op jit(solution)/shard_map/pallas_call | solution.py:461
  37.3 1.5 collective-permute-done.refs_0_
  39.8 4.4 %shard_map.153 = (f32[1024,1]{1,0:T(8,128)S(1)}, f32[1024,128]{1,0:T(8,128)S(1)}) custom-call(s32[128]{0:T(128)S(1)} %copy-done.16, bf16[1024,128]{1,0:T(8,128)(2,1)S(1)} %shard_map.150.query_ref, f32[1024,1]{1,0:T(8,128)S(1)} %get-tuple-element.45.old_top_ref, f32[1024,128]{1,0:T(8,128)S(1)} %get-tuple-element.46.old_mixed_ref, ...), custom_call_target="tpu_custom_call" | custom-call | tf_op jit(solution)/shard_map/pallas_call | solution.py:471
  44.2 4.8 %shard_map.154 = bf16[8,128,384]{2,1,0:T(8,128)(2,1)S(1)} custom-call(s32[128]{0:T(128)S(1)} %copy-done.16, bf16[1024,128]{1,0:T(8,128)(2,1)S(1)} %shard_map.150.query_ref, f32[1024,1]{1,0:T(8,128)S(1)} %get-tuple-element.52.old_top_ref, f32[1024,128]{1,0:T(8,128)S(1)} %get-tuple-element.53.old_mixed_ref, bf16[2880,512]{1,0:T(8,128)(2,1)S(1)} %bitcast.25, ...), custom_call_target="tpu_custom_call" | custom-call | tf_op jit(solution)/shard_map/pallas_call | solution.py:476
  50.0 3.9 %all-to-all-start.1 = ((bf16[8,128,384]{2,1,0:T(8,128)(2,1)}), bf16[8,128,384]{2,1,0:T(8,128)(2,1)S(1)}, u32[]{:S(2)}, u32[]{:S(2)}) async-start(bf16[8,128,384]{2,1,0:T(8,128)(2,1)} %copy-done.2), calls=%async_computation.1 | async-start | bytes 1572864 | tf_op jit(solution)/shard_map/all_to_all | solution.py:403
  53.9 1.5 collective-permute-start.9
  55.4 11.3 %all-to-all-done.1.parts_ref = bf16[8,128,384]{2,1,0:T(8,128)(2,1)S(1)} async-done(((bf16[8,128,384]{2,1,0:T(8,128)(2,1)}), bf16[8,128,384]{2,1,0:T(8,128)(2,1)S(1)}, u32[]{:S(2)}, u32[]{:S(2)}) %all-to-all-start.1) | async-done | bytes 786464 | tf_op jit(solution)/shard_map/all_to_all | solution.py:403
  66.7 1.3 shard_map.155
  68.7 8.2 %all-to-all-start.2 = ((bf16[32,24,384]{2,1,0:T(8,128)(2,1)}), bf16[32,24,384]{2,1,0:T(8,128)(2,1)S(1)}, u32[]{:S(2)}, u32[]{:S(2)}) async-start(bf16[32,24,384]{2,1,0:T(8,128)(2,1)} %bitcast.13), calls=%async_computation.2 | async-start | bytes 1179648 | tf_op jit(solution)/shard_map/all_to_all | solution.py:403
  76.9 17.1 %collective-permute-done.9.late_ref = bf16[228,2880]{1,0:T(8,128)(2,1)} collective-permute-done((bf16[228,2880]{1,0:T(8,128)(2,1)}, bf16[228,2880]{1,0:T(8,128)(2,1)}, u32[]{:S(2)}, u32[]{:S(2)}) %collective-permute-start.9) | collective-permute-done | bytes 1313312 | tf_op jit(solution)/shard_map/ppermute | solution.py:487
  93.9 2.2 %all-to-all-done.2 = bf16[32,24,384]{2,1,0:T(8,128)(2,1)S(1)} async-done(((bf16[32,24,384]{2,1,0:T(8,128)(2,1)}), bf16[32,24,384]{2,1,0:T(8,128)(2,1)S(1)}, u32[]{:S(2)}, u32[]{:S(2)}) %all-to-all-start.2) | async-done | bytes 589856 | tf_op jit(solution)/shard_map/all_to_all | solution.py:403
  96.3 32.1 %all_to_all.35.rows_in_ref = bf16[8,384,384]{2,1,0:T(8,128)(2,1)S(1)} all-to-all(bf16[8,384,384]{2,1,0:T(8,128)(2,1)S(1)} %bitcast.35), channel_id=1, replica_groups=mesh['ctx'=32,'exp'=8] {'exp'}, dimensions={0} | all-to-all | bytes 4718592 | tf_op jit(solution)/shard_map/all_to_all | solution.py:403
  128.4 6.6 %shard_map.156 = bf16[8,384,384]{2,1,0:T(8,128)(2,1)S(1)} custom-call(bf16[8,384,384]{2,1,0:T(8,128)(2,1)S(1)} %all_to_all.35.rows_in_ref, bf16[180,2880]{1,0:T(8,128)(2,1)S(1)} %bitcast.31, bf16[180,2880]{1,0:T(8,128)(2,1)S(1)} %bitcast.22, bf16[180,2880]{1,0:T(8,128)(2,1)S(1)} %bitcast.24, bf16[180,2880]{1,0:T(8,128)(2,1)} %collective-permute-done.4.far_gate_ref, ...), custom_call_target="tpu_custom_call" | custom-call | tf_op jit(solution)/shard_map/pallas_call | solution.py:359
  135.1 30.3 %all_to_all.36.parts_ref = bf16[8,384,384]{2,1,0:T(8,128)(2,1)S(1)} all-to-all(bf16[8,384,384]{2,1,0:T(8,128)(2,1)S(1)} %shard_map.156), channel_id=1, replica_groups=mesh['ctx'=32,'exp'=8] {'exp'}, dimensions={0} | all-to-all | bytes 4718592 | tf_op jit(solution)/shard_map/all_to_all | solution.py:403
  165.7 26.4 %all_to_all.37 = bf16[32,24,384]{2,1,0:T(8,128)(2,1)S(1)} all-to-all(bf16[32,24,384]{2,1,0:T(8,128)(2,1)S(1)} %bitcast.29), channel_id=1, replica_groups=mesh['ctx'=32,'exp'=8] {'ctx'}, dimensions={0} | all-to-all | bytes 1179648 | tf_op jit(solution)/shard_map/all_to_all | solution.py:403
  192.6 9.4 %all_to_all.38.parts_ref = bf16[8,16,768]{2,1,0:T(8,128)(2,1)S(1)} all-to-all(bf16[8,16,768]{2,1,0:T(8,128)(2,1)S(1)} %bitcast.32), channel_id=1, replica_groups=mesh['ctx'=32,'exp'=8] {'exp'}, dimensions={0} | all-to-all | bytes 393216 | tf_op jit(solution)/shard_map/all_to_all | solution.py:403
  (62 shorter events, 11.6 us)
Async XLA Ops:
  0.6 14.5 %copy-start = (bf16[1,2880,180]{1,2,0:T(8,128)(2,1)S(1)}, bf16[1,2880,180]{1,2,0:T(8,128)(2,1)}, u32[]{:S(2)}) copy-start(bf16[1,2880,180]{1,2,0:T(8,128)(2,1)} %param.26) | copy-start | bytes 3110404
  0.6 43.5 %collective-permute-start.4 = (bf16[180,2880]{1,0:T(8,128)(2,1)}, bf16[180,2880]{1,0:T(8,128)(2,1)}, u32[]{:S(2)}, u32[]{:S(2)}) collective-permute-start(bf16[180,2880]{1,0:T(8,128)(2,1)} %bitcast.30), channel_id=1, source_target_pairs={{0,2},{1,3},{2,0},{3,1},{4,6},{5,7},{6,4},{7,5},{8,10},{9,11},{10,... | collective-permute-start | bytes 3110408 | tf_op jit(solution)/shard_map/ppermute | solution.py:439
  7.0 15.6 %all-to-all-start = ((bf16[4,144,128]{2,1,0:T(8,128)(2,1)}), bf16[4,144,128]{2,1,0:T(8,128)(2,1)S(1)}, u32[]{:S(2)}, u32[]{:S(2)}) async-start(bf16[4,144,128]{2,1,0:T(8,128)(2,1)} %broadcast_in_dim.6), calls=%async_computation | async-start | bytes 294912 | tf_op jit(solution)/shard_map/all_to_all | solution.py:403
  16.1 33.9 %collective-permute-start.8 = (bf16[132,2880]{1,0:T(8,128)(2,1)}, bf16[132,2880]{1,0:T(8,128)(2,1)}, u32[]{:S(2)}, u32[]{:S(2)}) collective-permute-start(bf16[132,2880]{1,0:T(8,128)(2,1)} %slice.9), channel_id=1, source_target_pairs={{0,2},{1,3},{2,0},{3,1},{4,6},{5,7},{6,4},{7,5},{8,10},{9,11},{10,... | collective-permute-start | bytes 2280968 | tf_op jit(solution)/shard_map/ppermute | solution.py:475
  16.4 1.8 copy-start.3
  18.3 11.3 %copy-start.1 = (bf16[1,180,2880]{2,1,0:T(8,128)(2,1)S(1)}, bf16[1,180,2880]{2,1,0:T(8,128)(2,1)}, u32[]{:S(2)}) copy-start(bf16[1,180,2880]{2,1,0:T(8,128)(2,1)} %param.27) | copy-start | bytes 3110404
  22.6 6.2 %collective-permute-start.3 = (bf16[4,144,128]{2,1,0:T(8,128)(2,1)S(1)}, bf16[4,144,128]{2,1,0:T(8,128)(2,1)S(1)}, u32[]{:S(2)}, u32[]{:S(2)}) collective-permute-start(bf16[4,144,128]{2,1,0:T(8,128)(2,1)S(1)} %all-to-all-done.refs_0_), channel_id=1, source_target_pairs={{0,8},{8,0},{16,24},{24,16},{32,40},{40,32},{48,56},{56,48},{64,72... | collective-permute-start | bytes 442376 | tf_op jit(solution)/shard_map/ppermute | solution.py:447
  25.7 11.6 %collective-permute-start.2 = (bf16[4,144,128]{2,1,0:T(8,128)(2,1)S(1)}, bf16[4,144,128]{2,1,0:T(8,128)(2,1)}, u32[]{:S(2)}, u32[]{:S(2)}) collective-permute-start(bf16[4,144,128]{2,1,0:T(8,128)(2,1)S(1)} %all-to-all-done.refs_0_), channel_id=1, source_target_pairs={{0,192},{8,200},{16,208},{24,216},{32,224},{40,232},{48,240},{56,2... | collective-permute-start | bytes 442376 | tf_op jit(solution)/shard_map/ppermute | solution.py:447
  28.3 9.1 %collective-permute-start.1 = (bf16[4,144,128]{2,1,0:T(8,128)(2,1)S(1)}, bf16[4,144,128]{2,1,0:T(8,128)(2,1)}, u32[]{:S(2)}, u32[]{:S(2)}) collective-permute-start(bf16[4,144,128]{2,1,0:T(8,128)(2,1)S(1)} %all-to-all-done.refs_0_), channel_id=1, source_target_pairs={{0,128},{8,136},{16,144},{24,152},{32,160},{40,168},{48,176},{56,1... | collective-permute-start | bytes 442376 | tf_op jit(solution)/shard_map/ppermute | solution.py:447
  29.4 9.4 %collective-permute-start = (bf16[4,144,128]{2,1,0:T(8,128)(2,1)S(1)}, bf16[4,144,128]{2,1,0:T(8,128)(2,1)}, u32[]{:S(2)}, u32[]{:S(2)}) collective-permute-start(bf16[4,144,128]{2,1,0:T(8,128)(2,1)S(1)} %all-to-all-done.refs_0_), channel_id=1, source_target_pairs={{0,64},{8,72},{16,80},{24,88},{32,96},{40,104},{48,112},{56,120},{... | collective-permute-start | bytes 442376 | tf_op jit(solution)/shard_map/ppermute | solution.py:447
  29.6 1.3 copy-start.17
  29.6 3.6 %copy-start.16 = (s32[128]{0:T(128)S(1)}, s32[128]{0:T(128)}, u32[]{:S(2)}) copy-start(s32[128]{0:T(128)} %pos_ref.7) | copy-start | bytes 1540
  29.6 3.6 %copy-start.19 = (f32[8]{0:T(128)S(1)}, f32[8]{0:T(128)}, u32[]{:S(2)}) copy-start(f32[8]{0:T(128)} %sink_ref.1) | copy-start | bytes 100
  30.9 13.4 %copy-start.4 = (bf16[512,2880]{0,1:T(8,128)(2,1)S(1)}, bf16[512,2880]{0,1:T(8,128)(2,1)}, u32[]{:S(2)}) copy-start(bf16[512,2880]{0,1:T(8,128)(2,1)} %param.21) | copy-start | bytes 8847364
  38.8 5.4 %collective-permute-start.5 = (bf16[4,144,128]{2,1,0:T(8,128)(2,1)}, bf16[4,144,128]{2,1,0:T(8,128)(2,1)S(1)}, u32[]{:S(2)}, u32[]{:S(2)}) collective-permute-start(bf16[4,144,128]{2,1,0:T(8,128)(2,1)} %collective-permute-done.refs_0_), channel_id=1, source_target_pairs={{0,8},{8,0},{16,24},{24,16},{32,40},{40,32},{48,56},{56,48},{64,72... | collective-permute-start | bytes 442376 | tf_op jit(solution)/shard_map/ppermute | solution.py:447
  39.3 4.9 %collective-permute-start.6 = (bf16[4,144,128]{2,1,0:T(8,128)(2,1)}, bf16[4,144,128]{2,1,0:T(8,128)(2,1)S(1)}, u32[]{:S(2)}, u32[]{:S(2)}) collective-permute-start(bf16[4,144,128]{2,1,0:T(8,128)(2,1)} %collective-permute-done.1.refs_1_), channel_id=1, source_target_pairs={{0,8},{8,0},{16,24},{24,16},{32,40},{40,32},{48,56},{56,48},{64,72... | collective-permute-start | bytes 442376 | tf_op jit(solution)/shard_map/ppermute | solution.py:447
  39.3 4.9 %collective-permute-start.7 = (bf16[4,144,128]{2,1,0:T(8,128)(2,1)}, bf16[4,144,128]{2,1,0:T(8,128)(2,1)S(1)}, u32[]{:S(2)}, u32[]{:S(2)}) collective-permute-start(bf16[4,144,128]{2,1,0:T(8,128)(2,1)} %collective-permute-done.2.refs_2_), channel_id=1, source_target_pairs={{0,8},{8,0},{16,24},{24,16},{32,40},{40,32},{48,56},{56,48},{64,72... | collective-permute-start | bytes 442376 | tf_op jit(solution)/shard_map/ppermute | solution.py:447
  50.0 16.7 %copy-start.12 = (bf16[128,384]{1,0:T(8,128)(2,1)S(1)}, bf16[128,384]{1,0:T(8,128)(2,1)}, u32[]{:S(2)}) copy-start(bf16[128,384]{1,0:T(8,128)(2,1)} %copy-done.11) | copy-start | bytes 294916
  50.0 16.7 %all-to-all-start.1 = ((bf16[8,128,384]{2,1,0:T(8,128)(2,1)}), bf16[8,128,384]{2,1,0:T(8,128)(2,1)S(1)}, u32[]{:S(2)}, u32[]{:S(2)}) async-start(bf16[8,128,384]{2,1,0:T(8,128)(2,1)} %copy-done.2), calls=%async_computation.1 | async-start | bytes 1572864 | tf_op jit(solution)/shard_map/all_to_all | solution.py:403
  53.9 40.0 %collective-permute-start.9 = (bf16[228,2880]{1,0:T(8,128)(2,1)}, bf16[228,2880]{1,0:T(8,128)(2,1)}, u32[]{:S(2)}, u32[]{:S(2)}) collective-permute-start(bf16[228,2880]{1,0:T(8,128)(2,1)} %pad_maximum_fusion), channel_id=1, source_target_pairs={{0,2},{1,3},{2,0},{3,1},{4,6},{5,7},{6,4},{7,5},{8,10},{9,11},{10,... | collective-permute-start | bytes 3939848 | tf_op jit(solution)/shard_map/ppermute | solution.py:487
  68.7 27.4 %all-to-all-start.2 = ((bf16[32,24,384]{2,1,0:T(8,128)(2,1)}), bf16[32,24,384]{2,1,0:T(8,128)(2,1)S(1)}, u32[]{:S(2)}, u32[]{:S(2)}) async-start(bf16[32,24,384]{2,1,0:T(8,128)(2,1)} %bitcast.13), calls=%async_computation.2 | async-start | bytes 1179648 | tf_op jit(solution)/shard_map/all_to_all | solution.py:403
  96.3 32.1 %copy-start.6 = (bf16[1,2880,180]{1,2,0:T(8,128)(2,1)S(1)}, bf16[1,2880,180]{1,2,0:T(8,128)(2,1)}, u32[]{:S(2)}) copy-start(bf16[1,2880,180]{1,2,0:T(8,128)(2,1)} %param.25) | copy-start | bytes 3110404
  165.4 26.7 %copy-start.8 = (bf16[384,768]{1,0:T(8,128)(2,1)S(1)}, bf16[384,768]{1,0:T(8,128)(2,1)}, u32[]{:S(2)}) copy-start(bf16[384,768]{1,0:T(8,128)(2,1)} %copy-done.7) | copy-start | bytes 1769476
  165.4 26.7 %copy-start.14 = (bf16[128,384]{1,0:T(8,128)(2,1)S(1)}, bf16[128,384]{1,0:T(8,128)(2,1)}, u32[]{:S(2)}) copy-start(bf16[128,384]{1,0:T(8,128)(2,1)} %copy-done.13) | copy-start | bytes 294916
  (9 other events, 8.4 us)

commit v7 on v6

--- a/solution.py
+++ b/solution.py
@@ -254,7 +254,7 @@
 
 
 def last_attention_kernel(pos_ref, query_ref, old_top_ref, old_mixed_ref, w_ref, *refs):
-    *kv_refs, out_ref = refs
+    *kv_refs, out_hbm, out_ref, sems = refs
     width = w_ref.shape[0]
     columns = query_ref.shape[0]
     rows = out_ref.shape[1]
@@ -264,14 +264,33 @@
         [heads[head * rows:(head + 1) * rows] for head in range(columns // rows)], axis=1
     )
     full = width // CHUNK
+    copies = [
+        pltpu.make_async_copy(out_ref.at[place], out_hbm.at[place], sems.at[place])
+        for place in range(full + 1)
+    ]
+    tail = jnp.concatenate(
+        [w_ref[first:first + size, :] for first, size in tail_spans(width)], axis=0
+    )
+    out_ref[full] = jnp.zeros((rows, CHUNK), BF16)
+    out_ref[full, :, :tail.shape[0]] = dot(stacked, tail, ((1,), (1,))).astype(BF16)
+    copies[full].start()
     for place in range(full):
         part = dot(stacked, w_ref[place * CHUNK:(place + 1) * CHUNK, :], ((1,), (1,)))
         out_ref[place] = part.astype(BF16)
-    tail = jnp.concatenate(
-        [w_ref[first:first + size, :] for first, size in tail_spans(width)], axis=0
-    )
-    out_ref[full] = jnp.zeros((rows, CHUNK), BF16)
-    out_ref[full, :, :tail.shape[0]] = dot(stacked, tail, ((1,), (1,))).astype(BF16)
+        copies[place].start()
+    for copy in copies:
+        copy.wait()
+
+
+def finish_attention(dims, operands):
+    return pl.pallas_call(
+        last_attention_kernel,
+        out_shape=pltpu.HBM(dims, BF16),
+        in_specs=[SMEM] + [VMEM] * (len(operands) - 1),
+        out_specs=HBM,
+        scratch_shapes=[pltpu.VMEM(dims, BF16), pltpu.SemaphoreType.DMA((dims[0],))],
+        compiler_params=pltpu.CompilerParams(vmem_limit_bytes=24 * 1024 * 1024),
+    )(*operands)
 
 
 def dispatch_kernel(
@@ -473,14 +492,17 @@
     )
     top_row, mixed, far_gate = lax.optimization_barrier((*carried, far_gate))
     far_up = lax.ppermute(up[LATE:], "exp", swap)
-    partial_sums = call(
-        last_attention_kernel, shape((exp_count, rows, CHUNK)), [SMEM] + [VMEM] * 7
-    )(positions, queries, top_row, mixed, w_out.T, *planes_far)
+    operands = (positions, queries, top_row, mixed, w_out.T, *planes_far)
+    partial_sums = finish_attention((exp_count, rows, CHUNK), operands)
     partial_sums, far_up, late = lax.optimization_barrier((partial_sums, far_up, late))
     parts = exchange(partial_sums, "exp")
     attended, residual, outgoing = call(
         dispatch_kernel,
-        [shape((rows, CHUNK)), shape((rows, CHUNK), F32), shape((experts * slots, CHUNK))],
+        [
+            pltpu.HBM((rows, CHUNK), BF16),
+            shape((rows, CHUNK), F32),
+            shape((experts * slots, CHUNK)),
+        ],
         [VMEM] * 4,
     )(parts, own_tokens, own_gain, gather_table)
     arrived = exchange(outgoing.reshape(ctx_count, slots, CHUNK), "ctx")

time: 203 us -> 203 us (level)
  local copies, waits for them, and re-layouts: 8.36 us -> 6.13 us
    unnamed x40 -> x36, local copies, waits for them, and re-layouts: 6.49 us -> 4.28 us
  transfers between devices with their start and end apart: 13 -> 13, of which waited for: 5 -> 5; matrix products, arithmetic and copies ran while one was open for 1% -> 1% of each run, Pallas kernels for 9% -> 10%
where the time goes in v7:
time: 203 us; the launch traced here: 202 us
  blocking collectives  98.2 us (48%)
  waiting for transfers between devices  36.4 us (18%)
  starting transfers between devices  31.7 us (16%)
  Pallas kernels  27.5 us (14%)
  local copies, waits for them, and re-layouts  6.13 us (3%)
    all_to_all x4, blocking collectives, exchange(): lax.all_to_all(block, axis, split_axis=0, concat_axis=0, tiled=True, axis...  98.2 us
    all_to_all x3, starting transfers between devices, exchange(): lax.all_to_all(block, axis, split_axis=0, concat_axis=0, tiled=True, axis...  20.5 us
    ppermute x1, waiting for transfers between devices, local(): far_late = lax.ppermute(late, 'exp', swap)  17.6 us
    all_to_all x3, waiting for transfers between devices, exchange(): lax.all_to_all(block, axis, split_axis=0, concat_axis=0, tiled=True, axis...  16.7 us
    ppermute x7, starting transfers between devices, moved(): return lax.ppermute(block, 'ctx', route)  7.31 us
    pallas_call x1, Pallas kernels, run_experts(): pl.pallas_call(functools.partial(expert_kernel, width), out_shape=shape(e...  6.62 us
    pallas_call x1, Pallas kernels, finish_attention(): pl.pallas_call(last_attention_kernel, out_shape=pltpu.HBM(dims, BF16), in...  5.57 us
    pallas_call x1, Pallas kernels, local(): call(middle_attention_kernel, state, [SMEM] + [VMEM] * 6)  4.38 us
  transfers between devices with their start and end apart: 13, of which 5 were waited for; matrix products, arithmetic and copies ran while one was open for 1% of the time, Pallas kernels for 10%

profile of v7, /device:TPU:1, one launch (start us, length us, event | category | flops | bytes accessed | tf_op | source)
XLA Modules:
  0.0 202.0 jit_solution(9063397713607337870)
XLA Ops:
  0.6 2.2 %collective-permute-start.4 = (bf16[180,2880]{1,0:T(8,128)(2,1)}, bf16[180,2880]{1,0:T(8,128)(2,1)}, u32[]{:S(2)}, u32[]{:S(2)}) collective-permute-start(bf16[180,2880]{1,0:T(8,128)(2,1)} %bitcast.30), channel_id=1, source_target_pairs={{0,2},{1,3},{2,0},{3,1},{4,6},{5,7},{6,4},{7,5},{8,10},{9,11},{10,... | collective-permute-start | bytes 3110408 | tf_op jit(solution)/shard_map/ppermute | solution.py:458
  2.9 3.5 %shard_map.149 = (bf16[128,2880]{1,0:T(8,128)(2,1)S(1)}, bf16[144,128]{1,0:T(8,128)(2,1)S(1)}) custom-call(s32[128]{0:T(128)} %pos_ref.7, bf16[2880,128]{1,0:T(8,128)(2,1)} %bitcast.26, f32[2880]{0:T(1024)} %gain_hbm.1, bf16[64,2880]{1,0:T(8,128)(2,1)} %bitcast.37, bf16[64,2880]{1,0:T(8,128)(2,1)} %bitcast.38), custom_call_target="tpu_custom_call" | custom-call | tf_op jit(solution)/shard_map/pallas_call | solution.py:96
  7.0 8.2 %all-to-all-start = ((bf16[4,144,128]{2,1,0:T(8,128)(2,1)}), bf16[4,144,128]{2,1,0:T(8,128)(2,1)S(1)}, u32[]{:S(2)}, u32[]{:S(2)}) async-start(bf16[4,144,128]{2,1,0:T(8,128)(2,1)} %broadcast_in_dim.6), calls=%async_computation | async-start | bytes 294912 | tf_op jit(solution)/shard_map/all_to_all | solution.py:422
  16.4 1.8 copy-done.2
  18.9 3.7 %all-to-all-done.refs_0_ = bf16[4,144,128]{2,1,0:T(8,128)(2,1)S(1)} async-done(((bf16[4,144,128]{2,1,0:T(8,128)(2,1)}), bf16[4,144,128]{2,1,0:T(8,128)(2,1)S(1)}, u32[]{:S(2)}, u32[]{:S(2)}) %all-to-all-start) | async-done | bytes 147488 | tf_op jit(solution)/shard_map/all_to_all | solution.py:422
  22.6 3.1 %collective-permute-start.3 = (bf16[4,144,128]{2,1,0:T(8,128)(2,1)S(1)}, bf16[4,144,128]{2,1,0:T(8,128)(2,1)S(1)}, u32[]{:S(2)}, u32[]{:S(2)}) collective-permute-start(bf16[4,144,128]{2,1,0:T(8,128)(2,1)S(1)} %all-to-all-done.refs_0_), channel_id=1, source_target_pairs={{0,8},{8,0},{16,24},{24,16},{32,40},{40,32},{48,56},{56,48},{64,72... | collective-permute-start | bytes 442376 | tf_op jit(solution)/shard_map/ppermute | solution.py:466
  25.7 2.6 %collective-permute-start.2 = (bf16[4,144,128]{2,1,0:T(8,128)(2,1)S(1)}, bf16[4,144,128]{2,1,0:T(8,128)(2,1)}, u32[]{:S(2)}, u32[]{:S(2)}) collective-permute-start(bf16[4,144,128]{2,1,0:T(8,128)(2,1)S(1)} %all-to-all-done.refs_0_), channel_id=1, source_target_pairs={{0,192},{8,200},{16,208},{24,216},{32,224},{40,232},{48,240},{56,2... | collective-permute-start | bytes 442376 | tf_op jit(solution)/shard_map/ppermute | solution.py:466
  29.6 1.2 pad_maximum_fusion
  33.5 3.2 %shard_map.151 = (f32[1024,1]{1,0:T(8,128)S(1)}, f32[1024,128]{1,0:T(8,128)S(1)}) custom-call(s32[128]{0:T(128)S(1)} %copy-done.14, f32[8]{0:T(128)S(1)} %copy-done.17, bf16[1024,128]{1,0:T(8,128)(2,1)S(1)} %shard_map.150.query_ref, bf16[4,144,128]{2,1,0:T(8,128)(2,1)S(1)} %all-to-all-done.refs_0_, bf16[4,144,128]{2,1,0:T(8,128)(2,1)S(1)} %copy-done.9), custom_call_target="tpu_custom_call" | custom-call | tf_op jit(solution)/shard_map/pallas_call | solution.py:480
  36.7 2.1 %collective-permute-done.refs_0_ = bf16[4,144,128]{2,1,0:T(8,128)(2,1)} collective-permute-done((bf16[4,144,128]{2,1,0:T(8,128)(2,1)S(1)}, bf16[4,144,128]{2,1,0:T(8,128)(2,1)}, u32[]{:S(2)}, u32[]{:S(2)}) %collective-permute-start) | collective-permute-done | bytes 147488 | tf_op jit(solution)/shard_map/ppermute | solution.py:466
  39.8 4.4 %shard_map.153 = (f32[1024,1]{1,0:T(8,128)S(1)}, f32[1024,128]{1,0:T(8,128)S(1)}) custom-call(s32[128]{0:T(128)S(1)} %copy-done.14, bf16[1024,128]{1,0:T(8,128)(2,1)S(1)} %shard_map.150.query_ref, f32[1024,1]{1,0:T(8,128)S(1)} %get-tuple-element.45.old_top_ref, f32[1024,128]{1,0:T(8,128)S(1)} %get-tuple-element.46.old_mixed_ref, ...), custom_call_target="tpu_custom_call" | custom-call | tf_op jit(solution)/shard_map/pallas_call | solution.py:490
  44.2 5.6 %shard_map.154 = bf16[8,128,384]{2,1,0:T(8,128)(2,1)} custom-call(s32[128]{0:T(128)S(1)} %copy-done.14, bf16[1024,128]{1,0:T(8,128)(2,1)S(1)} %shard_map.150.query_ref, f32[1024,1]{1,0:T(8,128)S(1)} %get-tuple-element.52.old_top_ref, f32[1024,128]{1,0:T(8,128)S(1)} %get-tuple-element.53.old_mixed_ref, bf16[2880,512]{1,0:T(8,128)(2,1)S(1)} %bitcast.25, ...), custom_call_target="tpu_custom_call" | custom-call | tf_op jit(solution)/shard_map/pallas_call | solution.py:286
  49.8 3.9 %all-to-all-start.1 = ((bf16[8,128,384]{2,1,0:T(8,128)(2,1)}), bf16[8,128,384]{2,1,0:T(8,128)(2,1)S(1)}, u32[]{:S(2)}, u32[]{:S(2)}) async-start(bf16[8,128,384]{2,1,0:T(8,128)(2,1)} %shard_map.154), calls=%async_computation.1 | async-start | bytes 1572864 | tf_op jit(solution)/shard_map/all_to_all | solution.py:422
  53.8 1.5 collective-permute-start.9
  55.2 11.3 %all-to-all-done.1.parts_ref = bf16[8,128,384]{2,1,0:T(8,128)(2,1)S(1)} async-done(((bf16[8,128,384]{2,1,0:T(8,128)(2,1)}), bf16[8,128,384]{2,1,0:T(8,128)(2,1)S(1)}, u32[]{:S(2)}, u32[]{:S(2)}) %all-to-all-start.1) | async-done | bytes 786464 | tf_op jit(solution)/shard_map/all_to_all | solution.py:422
  66.5 1.3 shard_map.155
  67.8 8.3 %all-to-all-start.2 = ((bf16[32,24,384]{2,1,0:T(8,128)(2,1)}), bf16[32,24,384]{2,1,0:T(8,128)(2,1)S(1)}, u32[]{:S(2)}, u32[]{:S(2)}) async-start(bf16[32,24,384]{2,1,0:T(8,128)(2,1)} %bitcast.13), calls=%async_computation.2 | async-start | bytes 1179648 | tf_op jit(solution)/shard_map/all_to_all | solution.py:422
  76.2 17.6 %collective-permute-done.9.late_ref = bf16[228,2880]{1,0:T(8,128)(2,1)} collective-permute-done((bf16[228,2880]{1,0:T(8,128)(2,1)}, bf16[228,2880]{1,0:T(8,128)(2,1)}, u32[]{:S(2)}, u32[]{:S(2)}) %collective-permute-start.9) | collective-permute-done | bytes 1313312 | tf_op jit(solution)/shard_map/ppermute | solution.py:509
  93.8 1.7 all-to-all-done.2
  95.7 32.6 %all_to_all.35.rows_in_ref = bf16[8,384,384]{2,1,0:T(8,128)(2,1)S(1)} all-to-all(bf16[8,384,384]{2,1,0:T(8,128)(2,1)S(1)} %bitcast.35), channel_id=1, replica_groups=mesh['ctx'=32,'exp'=8] {'exp'}, dimensions={0} | all-to-all | bytes 4718592 | tf_op jit(solution)/shard_map/all_to_all | solution.py:422
  128.3 6.6 %shard_map.156 = bf16[8,384,384]{2,1,0:T(8,128)(2,1)S(1)} custom-call(bf16[8,384,384]{2,1,0:T(8,128)(2,1)S(1)} %all_to_all.35.rows_in_ref, bf16[180,2880]{1,0:T(8,128)(2,1)S(1)} %bitcast.31, bf16[180,2880]{1,0:T(8,128)(2,1)S(1)} %bitcast.22, bf16[180,2880]{1,0:T(8,128)(2,1)S(1)} %bitcast.24, bf16[180,2880]{1,0:T(8,128)(2,1)} %collective-permute-done.4.far_gate_ref, ...), custom_call_target="tpu_custom_call" | custom-call | tf_op jit(solution)/shard_map/pallas_call | solution.py:378
  134.9 30.3 %all_to_all.36.parts_ref = bf16[8,384,384]{2,1,0:T(8,128)(2,1)S(1)} all-to-all(bf16[8,384,384]{2,1,0:T(8,128)(2,1)S(1)} %shard_map.156), channel_id=1, replica_groups=mesh['ctx'=32,'exp'=8] {'exp'}, dimensions={0} | all-to-all | bytes 4718592 | tf_op jit(solution)/shard_map/all_to_all | solution.py:422
  165.5 25.9 %all_to_all.37 = bf16[32,24,384]{2,1,0:T(8,128)(2,1)S(1)} all-to-all(bf16[32,24,384]{2,1,0:T(8,128)(2,1)S(1)} %bitcast.29), channel_id=1, replica_groups=mesh['ctx'=32,'exp'=8] {'ctx'}, dimensions={0} | all-to-all | bytes 1179648 | tf_op jit(solution)/shard_map/all_to_all | solution.py:422
  191.9 9.4 %all_to_all.38.parts_ref = bf16[8,16,768]{2,1,0:T(8,128)(2,1)S(1)} all-to-all(bf16[8,16,768]{2,1,0:T(8,128)(2,1)S(1)} %bitcast.32), channel_id=1, replica_groups=mesh['ctx'=32,'exp'=8] {'exp'}, dimensions={0} | all-to-all | bytes 393216 | tf_op jit(solution)/shard_map/all_to_all | solution.py:422
  (58 shorter events, 9.3 us)
Async XLA Ops:
  0.6 14.5 %copy-start = (bf16[1,2880,180]{1,2,0:T(8,128)(2,1)S(1)}, bf16[1,2880,180]{1,2,0:T(8,128)(2,1)}, u32[]{:S(2)}) copy-start(bf16[1,2880,180]{1,2,0:T(8,128)(2,1)} %param.26) | copy-start | bytes 3110404
  0.6 43.5 %collective-permute-start.4 = (bf16[180,2880]{1,0:T(8,128)(2,1)}, bf16[180,2880]{1,0:T(8,128)(2,1)}, u32[]{:S(2)}, u32[]{:S(2)}) collective-permute-start(bf16[180,2880]{1,0:T(8,128)(2,1)} %bitcast.30), channel_id=1, source_target_pairs={{0,2},{1,3},{2,0},{3,1},{4,6},{5,7},{6,4},{7,5},{8,10},{9,11},{10,... | collective-permute-start | bytes 3110408 | tf_op jit(solution)/shard_map/ppermute | solution.py:458
  7.0 15.6 %all-to-all-start = ((bf16[4,144,128]{2,1,0:T(8,128)(2,1)}), bf16[4,144,128]{2,1,0:T(8,128)(2,1)S(1)}, u32[]{:S(2)}, u32[]{:S(2)}) async-start(bf16[4,144,128]{2,1,0:T(8,128)(2,1)} %broadcast_in_dim.6), calls=%async_computation | async-start | bytes 294912 | tf_op jit(solution)/shard_map/all_to_all | solution.py:422
  16.1 33.7 %collective-permute-start.8 = (bf16[132,2880]{1,0:T(8,128)(2,1)}, bf16[132,2880]{1,0:T(8,128)(2,1)}, u32[]{:S(2)}, u32[]{:S(2)}) collective-permute-start(bf16[132,2880]{1,0:T(8,128)(2,1)} %slice.9), channel_id=1, source_target_pairs={{0,2},{1,3},{2,0},{3,1},{4,6},{5,7},{6,4},{7,5},{8,10},{9,11},{10,... | collective-permute-start | bytes 2280968 | tf_op jit(solution)/shard_map/ppermute | solution.py:494
  16.4 1.8 copy-start.2
  18.3 11.3 %copy-start.1 = (bf16[1,180,2880]{2,1,0:T(8,128)(2,1)S(1)}, bf16[1,180,2880]{2,1,0:T(8,128)(2,1)}, u32[]{:S(2)}) copy-start(bf16[1,180,2880]{2,1,0:T(8,128)(2,1)} %param.27) | copy-start | bytes 3110404
  22.6 6.2 %collective-permute-start.3 = (bf16[4,144,128]{2,1,0:T(8,128)(2,1)S(1)}, bf16[4,144,128]{2,1,0:T(8,128)(2,1)S(1)}, u32[]{:S(2)}, u32[]{:S(2)}) collective-permute-start(bf16[4,144,128]{2,1,0:T(8,128)(2,1)S(1)} %all-to-all-done.refs_0_), channel_id=1, source_target_pairs={{0,8},{8,0},{16,24},{24,16},{32,40},{40,32},{48,56},{56,48},{64,72... | collective-permute-start | bytes 442376 | tf_op jit(solution)/shard_map/ppermute | solution.py:466
  25.7 11.0 %collective-permute-start.2 = (bf16[4,144,128]{2,1,0:T(8,128)(2,1)S(1)}, bf16[4,144,128]{2,1,0:T(8,128)(2,1)}, u32[]{:S(2)}, u32[]{:S(2)}) collective-permute-start(bf16[4,144,128]{2,1,0:T(8,128)(2,1)S(1)} %all-to-all-done.refs_0_), channel_id=1, source_target_pairs={{0,192},{8,200},{16,208},{24,216},{32,224},{40,232},{48,240},{56,2... | collective-permute-start | bytes 442376 | tf_op jit(solution)/shard_map/ppermute | solution.py:466
  28.2 8.4 %collective-permute-start.1 = (bf16[4,144,128]{2,1,0:T(8,128)(2,1)S(1)}, bf16[4,144,128]{2,1,0:T(8,128)(2,1)}, u32[]{:S(2)}, u32[]{:S(2)}) collective-permute-start(bf16[4,144,128]{2,1,0:T(8,128)(2,1)S(1)} %all-to-all-done.refs_0_), channel_id=1, source_target_pairs={{0,128},{8,136},{16,144},{24,152},{32,160},{40,168},{48,176},{56,1... | collective-permute-start | bytes 442376 | tf_op jit(solution)/shard_map/ppermute | solution.py:466
  29.4 9.4 %collective-permute-start = (bf16[4,144,128]{2,1,0:T(8,128)(2,1)S(1)}, bf16[4,144,128]{2,1,0:T(8,128)(2,1)}, u32[]{:S(2)}, u32[]{:S(2)}) collective-permute-start(bf16[4,144,128]{2,1,0:T(8,128)(2,1)S(1)} %all-to-all-done.refs_0_), channel_id=1, source_target_pairs={{0,64},{8,72},{16,80},{24,88},{32,96},{40,104},{48,112},{56,120},{... | collective-permute-start | bytes 442376 | tf_op jit(solution)/shard_map/ppermute | solution.py:466
  29.6 3.0 %copy-start.14 = (s32[128]{0:T(128)S(1)}, s32[128]{0:T(128)}, u32[]{:S(2)}) copy-start(s32[128]{0:T(128)} %pos_ref.7) | copy-start | bytes 1540
  29.6 2.9 %copy-start.17 = (f32[8]{0:T(128)S(1)}, f32[8]{0:T(128)}, u32[]{:S(2)}) copy-start(f32[8]{0:T(128)} %sink_ref.1) | copy-start | bytes 100
  30.9 13.4 %copy-start.3 = (bf16[512,2880]{0,1:T(8,128)(2,1)S(1)}, bf16[512,2880]{0,1:T(8,128)(2,1)}, u32[]{:S(2)}) copy-start(bf16[512,2880]{0,1:T(8,128)(2,1)} %param.21) | copy-start | bytes 8847364
  33.5 5.8 %copy-start.10 = (bf16[128,384]{1,0:T(8,128)(2,1)}, bf16[128,384]{1,0:T(8,128)(2,1)S(1)}, u32[]{:S(2)}) copy-start(bf16[128,384]{1,0:T(8,128)(2,1)S(1)} %get-tuple-element.56.tokens_ref) | copy-start | bytes 294916
  38.8 5.4 %collective-permute-start.5 = (bf16[4,144,128]{2,1,0:T(8,128)(2,1)}, bf16[4,144,128]{2,1,0:T(8,128)(2,1)S(1)}, u32[]{:S(2)}, u32[]{:S(2)}) collective-permute-start(bf16[4,144,128]{2,1,0:T(8,128)(2,1)} %collective-permute-done.refs_0_), channel_id=1, source_target_pairs={{0,8},{8,0},{16,24},{24,16},{32,40},{40,32},{48,56},{56,48},{64,72... | collective-permute-start | bytes 442376 | tf_op jit(solution)/shard_map/ppermute | solution.py:466
  39.3 4.9 %collective-permute-start.6 = (bf16[4,144,128]{2,1,0:T(8,128)(2,1)}, bf16[4,144,128]{2,1,0:T(8,128)(2,1)S(1)}, u32[]{:S(2)}, u32[]{:S(2)}) collective-permute-start(bf16[4,144,128]{2,1,0:T(8,128)(2,1)} %collective-permute-done.1.refs_1_), channel_id=1, source_target_pairs={{0,8},{8,0},{16,24},{24,16},{32,40},{40,32},{48,56},{56,48},{64,72... | collective-permute-start | bytes 442376 | tf_op jit(solution)/shard_map/ppermute | solution.py:466
  39.3 4.9 %collective-permute-start.7 = (bf16[4,144,128]{2,1,0:T(8,128)(2,1)}, bf16[4,144,128]{2,1,0:T(8,128)(2,1)S(1)}, u32[]{:S(2)}, u32[]{:S(2)}) collective-permute-start(bf16[4,144,128]{2,1,0:T(8,128)(2,1)} %collective-permute-done.2.refs_2_), channel_id=1, source_target_pairs={{0,8},{8,0},{16,24},{24,16},{32,40},{40,32},{48,56},{56,48},{64,72... | collective-permute-start | bytes 442376 | tf_op jit(solution)/shard_map/ppermute | solution.py:466
  49.8 16.7 %copy-start.11 = (bf16[128,384]{1,0:T(8,128)(2,1)S(1)}, bf16[128,384]{1,0:T(8,128)(2,1)}, u32[]{:S(2)}) copy-start(bf16[128,384]{1,0:T(8,128)(2,1)} %copy-done.10) | copy-start | bytes 294916
  49.8 16.7 %all-to-all-start.1 = ((bf16[8,128,384]{2,1,0:T(8,128)(2,1)}), bf16[8,128,384]{2,1,0:T(8,128)(2,1)S(1)}, u32[]{:S(2)}, u32[]{:S(2)}) async-start(bf16[8,128,384]{2,1,0:T(8,128)(2,1)} %shard_map.154), calls=%async_computation.1 | async-start | bytes 1572864 | tf_op jit(solution)/shard_map/all_to_all | solution.py:422
  53.8 40.0 %collective-permute-start.9 = (bf16[228,2880]{1,0:T(8,128)(2,1)}, bf16[228,2880]{1,0:T(8,128)(2,1)}, u32[]{:S(2)}, u32[]{:S(2)}) collective-permute-start(bf16[228,2880]{1,0:T(8,128)(2,1)} %pad_maximum_fusion), channel_id=1, source_target_pairs={{0,2},{1,3},{2,0},{3,1},{4,6},{5,7},{6,4},{7,5},{8,10},{9,11},{10,... | collective-permute-start | bytes 3939848 | tf_op jit(solution)/shard_map/ppermute | solution.py:509
  67.8 27.6 %all-to-all-start.2 = ((bf16[32,24,384]{2,1,0:T(8,128)(2,1)}), bf16[32,24,384]{2,1,0:T(8,128)(2,1)S(1)}, u32[]{:S(2)}, u32[]{:S(2)}) async-start(bf16[32,24,384]{2,1,0:T(8,128)(2,1)} %bitcast.13), calls=%async_computation.2 | async-start | bytes 1179648 | tf_op jit(solution)/shard_map/all_to_all | solution.py:422
  95.6 32.6 %copy-start.5 = (bf16[1,2880,180]{1,2,0:T(8,128)(2,1)S(1)}, bf16[1,2880,180]{1,2,0:T(8,128)(2,1)}, u32[]{:S(2)}) copy-start(bf16[1,2880,180]{1,2,0:T(8,128)(2,1)} %param.25) | copy-start | bytes 3110404
  165.2 26.2 %copy-start.7 = (bf16[384,768]{1,0:T(8,128)(2,1)S(1)}, bf16[384,768]{1,0:T(8,128)(2,1)}, u32[]{:S(2)}) copy-start(bf16[384,768]{1,0:T(8,128)(2,1)} %copy-done.6) | copy-start | bytes 1769476
  165.2 26.2 %copy-start.12 = (bf16[128,384]{1,0:T(8,128)(2,1)S(1)}, bf16[128,384]{1,0:T(8,128)(2,1)}, u32[]{:S(2)}) copy-start(bf16[128,384]{1,0:T(8,128)(2,1)} %get-tuple-element.67.attended_ref) | copy-start | bytes 294916
  (7 other events, 7.4 us)
